TPU v7x, 32 devices: a whole 2x2x4 slice. The times are simulated.
32 devices in a mesh: dp: 4 (over y, x), seq: 8 (over z, core).
Axes of the slice: x: 2, y: 2, z: 4, core: 2. Of those that a mesh axis runs over, the one named last changes fastest.
Arguments:
- tokens: bfloat16 [4, 1024, 1024], P('dp', 'seq'), may hold values from -7 to 7
- cotangent: bfloat16 [4, 1024, 1024], P('dp', 'seq'), may hold values from -6 to 6
- weight_qkv: float32 [1024, 3072], P(('dp', 'seq')), may hold values from -0.1875 to 0.1875
- weight_out: float32 [1024, 1024], P(('dp', 'seq')), may hold values from -3.5 to 3.5
- weight_up: float32 [1024, 4096], P(('dp', 'seq')), may hold values from -0.1875 to 0.1875
- weight_down: float32 [4096, 1024], P(('dp', 'seq')), may hold values from -0.09375 to 0.09375
- small_params: float32 [1024, 12], P(('dp', 'seq')), may hold values from -1.3 to 3, as said below
- moment_qkv: float32 [1024, 3072], P(('dp', 'seq')), may hold values from -0.0017089844 to 0.0017089844
- moment_out: float32 [1024, 1024], P(('dp', 'seq')), may hold values from -9.1552734e-05 to 9.1552734e-05
- moment_up: float32 [1024, 4096], P(('dp', 'seq')), may hold values from -0.0017089844 to 0.0017089844
- moment_down: float32 [4096, 1024], P(('dp', 'seq')), may hold values from -0.0017089844 to 0.0017089844
- moment_small: float32 [1024, 12], P(('dp', 'seq')), may hold values from -0.0034179688 to 0.0034179688
- second_qkv: float32 [1024, 3072], P(('dp', 'seq')), may hold values from 6.510417e-08 to 2.6200456e-07
- second_out: float32 [1024, 1024], P(('dp', 'seq')), may hold values from 1.9036306e-10 to 7.6609524e-10
- second_up: float32 [1024, 4096], P(('dp', 'seq')), may hold values from 6.510417e-08 to 2.6200456e-07
- second_down: float32 [4096, 1024], P(('dp', 'seq')), may hold values from 6.510417e-08 to 2.6200456e-07
- second_small: float32 [1024, 12], P(('dp', 'seq')), may hold values from 2.6200456e-07 to 1.0321393e-06
Outputs:
- layer_output: bfloat16 [4, 1024, 1024], P('dp', 'seq')
- grad_tokens: float32 [4, 1024, 1024], P('dp', 'seq')
- grad_norm: float32 [], replicated
- new_qkv: float32 [1024, 3072], P(('dp', 'seq'))
- new_out: float32 [1024, 1024], P(('dp', 'seq'))
- new_up: float32 [1024, 4096], P(('dp', 'seq'))
- new_down: float32 [4096, 1024], P(('dp', 'seq'))
- new_small: float32 [1024, 12], P(('dp', 'seq'))
- new_moment_qkv: float32 [1024, 3072], P(('dp', 'seq'))
- new_moment_out: float32 [1024, 1024], P(('dp', 'seq'))
- new_moment_up: float32 [1024, 4096], P(('dp', 'seq'))
- new_moment_down: float32 [4096, 1024], P(('dp', 'seq'))
- new_moment_small: float32 [1024, 12], P(('dp', 'seq'))
- new_second_qkv: float32 [1024, 3072], P(('dp', 'seq'))
- new_second_out: float32 [1024, 1024], P(('dp', 'seq'))
- new_second_up: float32 [1024, 4096], P(('dp', 'seq'))
- new_second_down: float32 [4096, 1024], P(('dp', 'seq'))
- new_second_small: float32 [1024, 12], P(('dp', 'seq'))
Inputs may be any that keep to these rules, and one draw needn't show every extreme that they name: `small_params`: gain columns are positive.
All inputs are finite; a program needn't handle non-finite values.
Results may differ from a plain program's by a relative error of at most 0.015.
Values may be sent and summed in bfloat16 or wider, within the bound.
No kernel may reach another device: no remote copies, remote signals or barrier semaphores. Data moves between devices by JAX's collectives and lax.ppermute only.
A program may use at most 192 MiB of HBM per device.

v0:
```python
import functools
import math

import jax
import jax.numpy as jnp
from jax import lax
from jax.experimental import pallas as pl
from jax.experimental.pallas import tpu as pltpu
from jax.sharding import Mesh
from jax.sharding import PartitionSpec as P

HEAD = 64
STEP = 5


NORM_EPSILON = 1e-05
ADAM_EPSILON = 1e-08
BETA_FIRST = 0.5
BETA_SECOND = 0.55
CLIP_LIMIT = 1.0
RATE_MATRIX = 0.04
RATE_OUTPUT = 0.5
RATE_SMALL = 0.3
WEIGHT_DECAY = 0.01
SCORE_SCALE = 0.125


def layer_norm(value, gain, shift):
    center = jnp.mean(value, axis=-1, keepdims=True)
    centered = value - center
    variance = jnp.mean(centered * centered, axis=-1, keepdims=True)
    return centered * lax.rsqrt(variance + NORM_EPSILON) * gain + shift


def exact_gelu(value):
    return jax.nn.gelu(value, approximate=False)


def unpack(table_low):
    table = table_low.astype(jnp.float32)
    ratio = table.shape[1] - 8
    bias_up = table[:, 3 : 3 + ratio].T.reshape(-1)
    return (
        table[:, 0],
        table[:, 1],
        table[:, 2],
        bias_up,
        table[:, 3 + ratio],
        table[:, 4 + ratio],
        table[:, 5 + ratio],
        table[:, 6 + ratio],
        table[:, 7 + ratio],
    )


def cross(left, right):
    return lax.dot_general(
        left, right, (((0,), (0,)), ((), ())), preferred_element_type=jnp.float32
    )


def against(left, right):
    return lax.dot_general(
        left, right, (((1,), (1,)), ((), ())), preferred_element_type=jnp.float32
    )


def take_block(source, index, block, heads):
    piece = lax.dynamic_slice_in_dim(source, index * block, block, 0)
    return piece.reshape(block, heads, HEAD)


def scores_of(query_heads, key_heads):
    return (
        jnp.einsum("qhd,khd->hqk", query_heads, key_heads, preferred_element_type=jnp.float32)
        * SCORE_SCALE
    )


def block_grads(query_heads, key_heads, value_heads, dout_heads, log_total, delta):
    scores = scores_of(query_heads, key_heads)
    probs = jnp.exp(scores - log_total[..., None])
    grad_probs = jnp.einsum(
        "qhd,khd->hqk", dout_heads, value_heads, preferred_element_type=jnp.float32
    )
    grad_scores = (probs * (grad_probs - delta[..., None])).astype(jnp.bfloat16)
    return (probs, grad_scores)


def attention_forward(query_heads, keys_all, values_all, block):
    count_rows, heads = (query_heads.shape[0], query_heads.shape[1])
    count = keys_all.shape[0] // block

    def stats_step(index, carry):
        run_top, run_total = carry
        scores = scores_of(query_heads, take_block(keys_all, index, block, heads))
        new_top = jnp.maximum(run_top, jnp.max(scores, axis=-1))
        run_total = run_total * jnp.exp(run_top - new_top) + jnp.sum(
            jnp.exp(scores - new_top[..., None]), axis=-1
        )
        return (new_top, run_total)

    start_top = jnp.full((heads, count_rows), -1e30, jnp.float32)
    start_total = jnp.zeros((heads, count_rows), jnp.float32)
    run_top, run_total = lax.fori_loop(0, count, stats_step, (start_top, start_total))
    log_total = run_top + jnp.log(run_total)

    def value_step(index, accum):
        scores = scores_of(query_heads, take_block(keys_all, index, block, heads))
        weights = jnp.exp(scores - log_total[..., None]).astype(jnp.bfloat16)
        return accum + jnp.einsum(
            "hqk,khd->qhd",
            weights,
            take_block(values_all, index, block, heads),
            preferred_element_type=jnp.float32,
        )

    accum = lax.fori_loop(0, count, value_step, jnp.zeros((count_rows, heads, HEAD), jnp.float32))
    return (accum.reshape(count_rows, heads * HEAD), log_total)


def adam_update(weight, grad, moment, second, rate, decay):
    moment_new = BETA_FIRST * moment + (1.0 - BETA_FIRST) * grad
    second_new = BETA_SECOND * second + (1.0 - BETA_SECOND) * grad * grad
    direction = (
        moment_new
        / (1.0 - BETA_FIRST**STEP)
        / (jnp.sqrt(second_new / (1.0 - BETA_SECOND**STEP)) + ADAM_EPSILON)
    )
    return (weight - rate * (direction + decay * weight), moment_new, second_new)


def on_device(
    tokens,
    cotangent,
    weight_qkv,
    weight_out,
    weight_up,
    weight_down,
    small_params,
    moment_qkv,
    moment_out,
    moment_up,
    moment_down,
    moment_small,
    second_qkv,
    second_out,
    second_up,
    second_down,
    second_small,
):
    rows = tokens[0]
    count_rows = rows.shape[0]
    width = rows.shape[1]
    heads = width // HEAD
    block = 4 * count_rows
    full_qkv, full_out, full_up, full_down, full_small = (
        lax.all_gather(weight_qkv.astype(jnp.bfloat16), ("dp", "seq"), axis=0, tiled=True),
        lax.all_gather(weight_out.astype(jnp.bfloat16), ("dp", "seq"), axis=0, tiled=True),
        lax.all_gather(weight_up.astype(jnp.bfloat16), ("dp", "seq"), axis=0, tiled=True),
        lax.all_gather(weight_down.astype(jnp.bfloat16), ("dp", "seq"), axis=0, tiled=True),
        lax.all_gather(small_params.astype(jnp.bfloat16), ("dp", "seq"), axis=0, tiled=True),
    )
    (
        bias_query,
        bias_value,
        bias_out,
        bias_up,
        bias_down,
        gain_one,
        shift_one,
        gain_two,
        shift_two,
    ) = unpack(full_small)
    projected = jnp.dot(rows, full_qkv, preferred_element_type=jnp.float32)
    query = (projected[:, :width] + bias_query).astype(jnp.bfloat16)
    key_rows = projected[:, width : 2 * width].astype(jnp.bfloat16)
    value_rows = (projected[:, 2 * width :] + bias_value).astype(jnp.bfloat16)
    keys_all, values_all = (
        lax.all_gather(key_rows, "seq", axis=0, tiled=True),
        lax.all_gather(value_rows, "seq", axis=0, tiled=True),
    )
    query_heads = query.reshape(count_rows, heads, HEAD)
    attended, log_total = attention_forward(query_heads, keys_all, values_all, block)
    attended_low = attended.astype(jnp.bfloat16)
    branch = jnp.dot(attended_low, full_out, preferred_element_type=jnp.float32) + bias_out
    middle = rows.astype(jnp.float32) + branch
    hidden, norm_one_back = jax.vjp(layer_norm, middle, gain_one, shift_one)
    hidden_low = hidden.astype(jnp.bfloat16)
    upward = jnp.dot(hidden_low, full_up, preferred_element_type=jnp.float32) + bias_up
    activation, gelu_back = jax.vjp(exact_gelu, upward)
    activation_low = activation.astype(jnp.bfloat16)
    downward = jnp.dot(activation_low, full_down, preferred_element_type=jnp.float32) + bias_down
    output, norm_two_back = jax.vjp(layer_norm, hidden + downward, gain_two, shift_two)
    back_qkv, back_out, back_up, back_down = (full_qkv, full_out, full_up, full_down)
    grad_sum_two, grad_gain_two, grad_shift_two = norm_two_back(cotangent[0].astype(jnp.float32))
    grad_down_low = grad_sum_two.astype(jnp.bfloat16)
    grad_bias_down = jnp.sum(grad_down_low.astype(jnp.float32), axis=0)
    grad_weight_down = cross(activation_low, grad_down_low)
    grad_activation = against(grad_down_low, back_down)
    grad_up_low = gelu_back(grad_activation)[0].astype(jnp.bfloat16)
    grad_bias_up = jnp.sum(grad_up_low.astype(jnp.float32), axis=0)
    grad_weight_up = cross(hidden_low, grad_up_low)
    grad_hidden = grad_sum_two + against(grad_up_low, back_up)
    grad_middle, grad_gain_one, grad_shift_one = norm_one_back(grad_hidden)
    grad_branch_low = grad_middle.astype(jnp.bfloat16)
    grad_bias_out = jnp.sum(grad_branch_low.astype(jnp.float32), axis=0)
    grad_weight_out = cross(attended_low, grad_branch_low)
    grad_attended = against(grad_branch_low, back_out).astype(jnp.bfloat16)
    delta = jnp.sum(
        (grad_attended.astype(jnp.float32) * attended).reshape(count_rows, heads, HEAD), axis=-1
    ).T
    dout_heads = grad_attended.reshape(count_rows, heads, HEAD)
    count = keys_all.shape[0] // block

    def both_step(index, carry):
        grad_query, grad_keys, grad_values = carry
        key_heads = take_block(keys_all, index, block, heads)
        value_heads = take_block(values_all, index, block, heads)
        probs, grad_scores = block_grads(
            query_heads, key_heads, value_heads, dout_heads, log_total, delta
        )
        grad_query = (
            grad_query
            + jnp.einsum("hqk,khd->qhd", grad_scores, key_heads, preferred_element_type=jnp.float32)
            * SCORE_SCALE
        )
        part_keys = (
            jnp.einsum("hqk,qhd->khd", grad_scores, query_heads, preferred_element_type=jnp.float32)
            * SCORE_SCALE
        )
        part_values = jnp.einsum(
            "hqk,qhd->khd",
            probs.astype(jnp.bfloat16),
            dout_heads,
            preferred_element_type=jnp.float32,
        )
        grad_keys = lax.dynamic_update_slice_in_dim(
            grad_keys, part_keys.reshape(block, width), index * block, 0
        )
        grad_values = lax.dynamic_update_slice_in_dim(
            grad_values, part_values.reshape(block, width), index * block, 0
        )
        return (grad_query, grad_keys, grad_values)

    start = (
        jnp.zeros((count_rows, heads, HEAD), jnp.float32),
        jnp.zeros((keys_all.shape[0], width), jnp.float32),
        jnp.zeros((keys_all.shape[0], width), jnp.float32),
    )
    grad_query, grad_keys, grad_values = lax.fori_loop(0, count, both_step, start)
    summed_keys, summed_values = (
        lax.psum_scatter(
            grad_keys.astype(jnp.bfloat16), "seq", scatter_dimension=0, tiled=True
        ).astype(jnp.float32),
        lax.psum_scatter(
            grad_values.astype(jnp.bfloat16), "seq", scatter_dimension=0, tiled=True
        ).astype(jnp.float32),
    )
    grad_query_low = grad_query.reshape(count_rows, width).astype(jnp.bfloat16)
    grad_value_low = summed_values.astype(jnp.bfloat16)
    grad_projected = jnp.concatenate(
        [grad_query_low, summed_keys.astype(jnp.bfloat16), grad_value_low], axis=1
    )
    grad_weight_qkv = cross(rows, grad_projected)
    grad_bias_query = jnp.sum(grad_query_low.astype(jnp.float32), axis=0)
    grad_bias_value = jnp.sum(grad_value_low.astype(jnp.float32), axis=0)
    grad_rows = grad_middle + against(grad_projected, back_qkv)
    ratio = full_up.shape[1] // width
    grad_small = jnp.concatenate(
        [
            jnp.stack([grad_bias_query, grad_bias_value, grad_bias_out], axis=1),
            grad_bias_up.reshape(ratio, width).T,
            jnp.stack(
                [grad_bias_down, grad_gain_one, grad_shift_one, grad_gain_two, grad_shift_two],
                axis=1,
            ),
        ],
        axis=1,
    )
    owned_qkv, owned_out, owned_up, owned_down, owned_small = (
        lax.psum_scatter(grad_weight_qkv, ("dp", "seq"), scatter_dimension=0, tiled=True),
        lax.psum_scatter(grad_weight_out, ("dp", "seq"), scatter_dimension=0, tiled=True),
        lax.psum_scatter(grad_weight_up, ("dp", "seq"), scatter_dimension=0, tiled=True),
        lax.psum_scatter(grad_weight_down, ("dp", "seq"), scatter_dimension=0, tiled=True),
        lax.psum_scatter(grad_small, ("dp", "seq"), scatter_dimension=0, tiled=True),
    )
    squares = jnp.sum(owned_qkv * owned_qkv) + jnp.sum(owned_out * owned_out)
    squares = squares + jnp.sum(owned_up * owned_up) + jnp.sum(owned_down * owned_down)
    squares = squares + jnp.sum(owned_small * owned_small)
    total = lax.psum(squares, ("dp", "seq"))
    grad_norm = jnp.sqrt(total)
    factor = jnp.minimum(1.0, CLIP_LIMIT / (grad_norm + 1e-06))
    new_qkv, new_moment_qkv, new_second_qkv = adam_update(
        weight_qkv, owned_qkv * factor, moment_qkv, second_qkv, RATE_MATRIX, WEIGHT_DECAY
    )
    new_out, new_moment_out, new_second_out = adam_update(
        weight_out, owned_out * factor, moment_out, second_out, RATE_OUTPUT, WEIGHT_DECAY
    )
    new_up, new_moment_up, new_second_up = adam_update(
        weight_up, owned_up * factor, moment_up, second_up, RATE_MATRIX, WEIGHT_DECAY
    )
    new_down, new_moment_down, new_second_down = adam_update(
        weight_down, owned_down * factor, moment_down, second_down, RATE_MATRIX, WEIGHT_DECAY
    )
    new_small, new_moment_small, new_second_small = adam_update(
        small_params, owned_small * factor, moment_small, second_small, RATE_SMALL, 0.0
    )
    return (
        output.astype(jnp.bfloat16)[None],
        grad_rows[None],
        grad_norm,
        new_qkv,
        new_out,
        new_up,
        new_down,
        new_small,
        new_moment_qkv,
        new_moment_out,
        new_moment_up,
        new_moment_down,
        new_moment_small,
        new_second_qkv,
        new_second_out,
        new_second_up,
        new_second_down,
        new_second_small,
    )


AXES = ("y", "x", "h", "l", "c")
LOW = jnp.bfloat16
WIDE = jnp.float32


def swap(value, axes):
    axes = tuple(name for name in AXES if name in axes)
    last = 2 ** len(axes) - 1
    return lax.ppermute(value, axes, [(i, i ^ last) for i in range(last + 1)])


def after(value, *events):
    return lax.optimization_barrier((value, *events))[0]


def tie(*values):
    return lax.optimization_barrier(values)


def send(value, axes, start=(), use=()):
    got = swap(after(value, *start) if start else value, axes)
    return after(got, *use) if use else got


def exchange(parts, a, b, start=(), use=()):
    ways = ((b,), (a,), (a, b))
    return [parts[0]] + [send(part, way, start, use) for part, way in zip(parts[1:], ways)]


def gather_square(value, a, b):
    half = value.shape[0] // 2
    from_a, from_b = swap(value, (a,)), swap(value, (b,))
    return [value, from_b, from_a, swap(from_a[:half], (b,)), swap(from_b[half:], (a,))]


def scatter_square(parts, a, b):
    own, to_b, to_a, far_first, far_second = parts
    half = own.shape[0] // 2
    first = swap(far_first, (a,))
    second = swap(far_second, (b,))
    to_b = jnp.concatenate([to_b[:half] + first.astype(WIDE), to_b[half:]], axis=0).astype(LOW)
    to_a = jnp.concatenate([to_a[:half], to_a[half:] + second.astype(WIDE)], axis=0).astype(LOW)
    return own, swap(to_b, (b,)), swap(to_a, (a,))


def gather_ring(value, a, b, start=(), use=()):
    from_b = send(value, (b,), start, use)
    from_a = swap(after(value, *start) if start else value, (a,))
    far = send(from_a, (b,), use=use)
    return [value, from_b, after(from_a, *use) if use else from_a, far]


def dot(left, right):
    return jnp.dot(left, right, preferred_element_type=WIDE)


def call(kernel, outs, *args, scratch=(), flops=10**9, scalars=0):
    outs = [jax.ShapeDtypeStruct(shape, kind) for shape, kind in outs]
    return pl.pallas_call(
        kernel,
        name=getattr(kernel, "func", kernel).__name__,
        in_specs=[pl.BlockSpec(memory_space=pltpu.SMEM)] * (1 + scalars)
        + [pl.BlockSpec(memory_space=pltpu.VMEM)] * (len(args) - 1 - scalars),
        out_specs=[pl.BlockSpec(memory_space=pltpu.VMEM)] * len(outs),
        out_shape=outs,
        scratch_shapes=list(scratch),
        compiler_params=pltpu.CompilerParams(vmem_limit_bytes=48 * 2**20),
        cost_estimate=pl.CostEstimate(flops=1, bytes_accessed=1, transcendentals=0),
    )(*args)


def at(start, size):
    return pl.ds(pl.multiple_of(start, size), size)


def indices(bits):
    iy, ix, ih, il, ic = (bits[i] for i in range(5))
    return 2 * iy + ix, 2 * ih + il, ic


def pack_qkv_kernel(bits, weight, small, *outs):
    _, z, _ = indices(bits)
    own = weight.shape[0]
    size = outs[0].shape[1] // 3
    for r, out in enumerate(outs):
        for kind in range(3):
            start = kind * 4 * size + (z ^ r) * size
            out[:own, kind * size : (kind + 1) * size] = weight[:, at(start, size)].astype(LOW)
        out[own:, :] = small[...]


def pack_rest_kernel(bits, out_weight, up, down, low_out, low_down, near_up, far_up):
    iy, ix, ih, il, ic = (bits[i] for i in range(5))
    own = up.shape[0]
    size = up.shape[1] // 16
    low_out[...] = out_weight[...].astype(LOW)
    low_down[...] = down[...].astype(LOW)
    for r in range(4):
        out, rows = (near_up, far_up)[r // 2], slice(r % 2 * own, (r % 2 + 1) * own)
        x, l = ix ^ (r // 2), il ^ (r % 2)
        for y in range(2):
            for h in range(2):
                start = (((y * 2 + x) * 2 + h) * 2 + l) * size
                to = (y * 2 + h) * size
                out[rows, to : to + size] = up[:, at(start, size)].astype(LOW)


def lay_rows(bits, full, pieces, own, stride, c):
    d, z, _ = indices(bits)
    for p, piece in enumerate(pieces):
        for s in range(4):
            to = (d ^ p) * 8 * own + (z ^ s) * 2 * own + c * own
            full[at(to, own), :] = piece[s * stride : s * stride + own, :]


def lay_qkv_kernel(bits, near, far, full):
    own = full.shape[0] // 32
    stride = near.shape[0] // 16
    c = bits[4]
    for ref, core in ((near, c), (far, 1 - c)):
        pieces = [ref.at[p * 4 * stride : (p + 1) * 4 * stride] for p in range(4)]
        lay_rows(bits, full, pieces, own, stride, core)


def lay_up_kernel(bits, near, far, full):
    iy, ix, ih, il, ic = (bits[i] for i in range(5))
    own = full.shape[0] // 32
    for ref, core in ((near, ic), (far, 1 - ic)):
        for p in range(4):
            y, h = iy ^ (p // 2), ih ^ (p % 2)
            for q in range(4):
                x, l = ix ^ (q // 2), il ^ (q % 2)
                to = ((((y * 2 + x) * 2 + h) * 2 + l) * 2 + core) * own
                full[at(to, own), :] = ref[(4 * p + q) * own : (4 * p + q + 1) * own, :]


def lay_down_kernel(bits, near, far, full):
    iy, _, ih, _, ic = (bits[i] for i in range(5))
    size = full.shape[0] // 8
    for ref, core in ((near, ic), (far, 1 - ic)):
        for p in range(4):
            to = (((iy ^ (p // 2)) * 2 + (ih ^ (p % 2))) * 2 + core) * size
            full[at(to, size), :] = ref[p * size : (p + 1) * size, :]


def project_kernel(
    bits, bias, near_ref, far_ref, t0, t1, t2, t3, q_ref, kv_ref, full_ref, near, far, rows, sems
):
    d, z, c = indices(bits)
    count = t0.shape[0]
    own = full_ref.shape[0] // 32
    tall = near.shape[0] // 16
    size = q_ref.shape[1]
    pairs = [(near_ref, near), (far_ref, far)]
    pairs += [(ref, rows.at[i * count : (i + 1) * count]) for i, ref in enumerate((t0, t1, t2, t3))]
    copies = [pltpu.make_async_copy(*pair, sems.at[i]) for i, pair in enumerate(pairs)]
    for copy in copies:
        copy.start()
    for copy in copies[:2]:
        copy.wait()
    for ref, core in ((near, c), (far, 1 - c)):
        for p in range(4):
            for s in range(4):
                to = (d ^ p) * 8 * own + (z ^ s) * 2 * own + core * own
                full_ref[at(to, own), :] = ref[(4 * p + s) * tall : (4 * p + s) * tall + own, :]
    for copy in copies[2:]:
        copy.wait()
    projected = dot(rows[...], full_ref[...])
    q_ref[...] = (projected[:, :size] + bias[0:1, :]).astype(LOW)
    kv_ref[:, :size] = projected[:, size : 2 * size].astype(LOW)
    kv_ref[:, size:] = (projected[:, 2 * size :] + bias[1:2, :]).astype(LOW)


def head_mask(shape, axis, head):
    lane = lax.broadcasted_iota(jnp.int32, shape, axis)
    return (lane < HEAD) if head == 0 else (lane >= HEAD)


def forward_kernel(bits, q_ref, near, far, *outs):
    lse_ref = outs[-1]
    count = outs[0].shape[0]
    width = q_ref.shape[1]
    pair = 2 * HEAD
    for group in range(width // pair):
        cols = slice(group * pair, (group + 1) * pair)
        value_cols = slice(width + group * pair, width + (group + 1) * pair)
        keys = jnp.concatenate([near[:, cols], far[:, cols]], axis=0)
        values_t = jnp.concatenate([near[:, value_cols], far[:, value_cols]], axis=0).T
        for piece in range(2):
            rows = slice(2 * piece * count, 2 * (piece + 1) * count)
            queries = q_ref[rows, cols]
            zero = jnp.zeros_like(queries)
            halves = []
            for head in range(2):
                query = jnp.where(head_mask(queries.shape, 1, head), queries, zero)
                scores = against(keys, query) * SCORE_SCALE
                top = jnp.max(scores, axis=0, keepdims=True)
                weights = jnp.exp(scores - top)
                total = jnp.sum(weights, axis=0, keepdims=True)
                at_head = 2 * group + head
                lse_ref[at_head : at_head + 1, rows] = top + jnp.log(total)
                probs = (weights * (1.0 / total)).astype(LOW)
                halves.append(dot(values_t, probs))
            mask = head_mask(halves[0].shape, 0, 0)
            result = jnp.where(mask, halves[0], halves[1]).T.astype(LOW)
            outs[2 * piece][:, cols] = result[:count]
            outs[2 * piece + 1][:, cols] = result[count:]


def backward_kernel(
    bits, q_ref, near, far, lse_ref, d0, d1, d2, d3, dq_ref, near_ref, far_ref, sums
):
    count = d0.shape[0]
    length = 2 * near.shape[0]
    width = q_ref.shape[1]
    pair = 2 * HEAD
    for group in range(width // pair):
        cols = slice(group * pair, (group + 1) * pair)
        value_cols = slice(width + group * pair, width + (group + 1) * pair)
        keys = jnp.concatenate([near[:, cols], far[:, cols]], axis=0)
        values = jnp.concatenate([near[:, value_cols], far[:, value_cols]], axis=0)
        keys_t = keys.T
        sum_keys = jnp.zeros((length, pair), WIDE)
        sum_values = jnp.zeros((length, pair), WIDE)
        bias_query = jnp.zeros((1, pair), WIDE)
        for piece in range(2):
            rows = slice(2 * piece * count, 2 * (piece + 1) * count)
            queries = q_ref[rows, cols]
            refs = (d0, d1) if piece == 0 else (d2, d3)
            douts = jnp.concatenate([refs[0][:, cols], refs[1][:, cols]], axis=0)
            zero = jnp.zeros_like(queries)
            all_probs, all_grads, all_query, all_dout, halves = [], [], [], [], []
            for head in range(2):
                mask = head_mask(queries.shape, 1, head)
                query = jnp.where(mask, queries, zero)
                dout = jnp.where(mask, douts, zero)
                at_head = 2 * group + head
                scores = against(keys, query) * SCORE_SCALE
                probs = jnp.exp(scores - lse_ref[at_head : at_head + 1, rows])
                grad_probs = against(values, dout)
                delta = jnp.sum(probs * grad_probs, axis=0, keepdims=True)
                grads = (probs * (grad_probs - delta)).astype(LOW)
                all_probs.append(probs.astype(LOW))
                all_grads.append(grads)
                all_query.append(query)
                all_dout.append(dout)
                halves.append(dot(keys_t, grads))
            mask = head_mask(halves[0].shape, 0, 0)
            dq = jnp.where(mask, halves[0], halves[1]) * SCORE_SCALE
            dq = dq.T.astype(LOW)
            dq_ref[rows, cols] = dq
            bias_query += jnp.sum(dq.astype(WIDE), axis=0, keepdims=True)
            sum_keys += dot(jnp.concatenate(all_grads, axis=1), jnp.concatenate(all_query, axis=0))
            sum_values += dot(jnp.concatenate(all_probs, axis=1), jnp.concatenate(all_dout, axis=0))
        sum_keys = sum_keys * SCORE_SCALE
        half = length // 2
        near_ref[:, cols] = sum_keys[:half]
        far_ref[:, cols] = sum_keys[half:].astype(LOW)
        sums[0:1, cols] = bias_query
        sums[1:2, cols] = jnp.sum(sum_values, axis=0, keepdims=True)
        near_ref[:, value_cols] = sum_values[:half]
        far_ref[:, value_cols] = sum_values[half:].astype(LOW)


def row_mean(value):
    return jnp.mean(value, axis=-1, keepdims=True)


def column_sums(out, *values):
    out[...] = jnp.zeros_like(out)
    for index, value in enumerate(values):
        out[index : index + 1, :] = jnp.sum(value, axis=0, keepdims=True)


def out_kernel(bits, a0, a1, a2, a3, weight, tokens, table, hidden, low, normed, scale):
    _, z, _ = indices(bits)
    size = a0.shape[1]
    branch = jnp.zeros(hidden.shape, WIDE)
    for r, piece in enumerate((a0, a1, a2, a3)):
        branch += dot(piece[...], weight[at((z ^ r) * size, size), :])
    middle = tokens[...].astype(WIDE) + (branch + table[2:3, :])
    centered = middle - row_mean(middle)
    inverse = lax.rsqrt(row_mean(centered * centered) + NORM_EPSILON)
    unit = centered * inverse
    value = unit * table[-4:-3, :] + table[-3:-2, :]
    hidden[...] = value
    low[...] = value.astype(LOW)
    normed[...] = unit
    scale[...] = jnp.broadcast_to(inverse, scale.shape)


def store_parts(product, own, to_b, to_a, far_first, far_second):
    count = own.shape[0]
    half = count // 2
    own[...] = product[:count]
    to_b[...] = product[count : 2 * count]
    to_a[...] = product[2 * count : 3 * count]
    far_first[...] = product[3 * count : 3 * count + half].astype(LOW)
    far_second[...] = product[3 * count + half :].astype(LOW)


def feed_up_kernel(bits, h0, h1, h2, h3, h4, up, bias, act, slope):
    hidden = jnp.concatenate([ref[...] for ref in (h0, h1, h2, h3, h4)], axis=0)
    upward = dot(hidden, up[...]) + bias[...]
    half = (1.0 + lax.erf(upward * (0.5**0.5))) * 0.5
    act[...] = (upward * half).astype(LOW)
    bell = jnp.exp(upward * upward * -0.5) * (0.5 * 2.0**0.5 * math.pi**-0.5)
    slope[...] = (half + upward * bell).astype(LOW)


def feed_down_kernel(bits, act, down, *parts):
    store_parts(dot(act[...], down[...]), *parts)


def norm_two_kernel(bits, own, from_b, from_a, hidden, cot, table, output, grad, low, sums):
    downward = own[...] + from_b[...].astype(WIDE) + from_a[...].astype(WIDE)
    value = hidden[...] + (downward + table[-5:-4, :])
    centered = value - row_mean(value)
    inverse = lax.rsqrt(row_mean(centered * centered) + NORM_EPSILON)
    unit = centered * inverse
    gain = table[-2:-1, :]
    output[...] = (unit * gain + table[-1:, :]).astype(LOW)
    cotangent = cot[...].astype(WIDE)
    inner = cotangent * gain
    result = inverse * (inner - row_mean(inner) - unit * row_mean(inner * unit))
    grad[...] = result
    rounded = result.astype(LOW)
    low[...] = rounded
    column_sums(sums, rounded.astype(WIDE), cotangent * unit, cotangent)


def feed_back_kernel(bits, g0, g1, g2, g3, g4, down, up, slope, grad_up, sums, *parts):
    grads = jnp.concatenate([ref[...] for ref in (g0, g1, g2, g3, g4)], axis=0)
    upward = (against(grads, down[...]) * slope[...].astype(WIDE)).astype(LOW)
    grad_up[...] = upward
    column_sums(sums, upward.astype(WIDE))
    store_parts(against(upward, up[...]), *parts)


def feed_grad_kernel(
    bits, act, g0, g1, g2, g3, g4, h0, h1, h2, h3, h4, grad_up, near, far, down_full, up_full
):
    iy, ix, ih, il, ic = (bits[i] for i in range(5))
    grads = jnp.concatenate([ref[...] for ref in (g0, g1, g2, g3, g4)], axis=0)
    hidden = jnp.concatenate([ref[...] for ref in (h0, h1, h2, h3, h4)], axis=0)
    down_full[...] = cross(act[...], grads).astype(LOW)
    up_full[...] = cross(hidden, grad_up[...]).astype(LOW)
    own = up_full.shape[0] // 32
    size = down_full.shape[0] // 8
    for p in range(4):
        y, h = iy ^ (p // 2), ih ^ (p % 2)
        base = p * (4 * own + size)
        for q in range(4):
            x, l = ix ^ (q // 2), il ^ (q % 2)
            start = ((((y * 2 + x) * 2 + h) * 2 + l) * 2) * own
            to = base + q * own
            near[to : to + own, :] = up_full[at(start + ic * own, own), :]
            far[to : to + own, :] = up_full[at(start + (1 - ic) * own, own), :]
        start = (y * 2 + h) * 2
        to = base + 4 * own
        near[to : to + size, :] = down_full[at((start + ic) * size, size), :]
        far[to : to + size, :] = down_full[at((start + 1 - ic) * size, size), :]


def norm_one_kernel(
    bits, own, from_b, from_a, above, normed, scale, weight, table, grad, low, sums, *pieces
):
    _, z, _ = indices(bits)
    hidden = own[...] + from_b[...].astype(WIDE) + from_a[...].astype(WIDE)
    hidden = above[...] + hidden
    unit = normed[...]
    inner = hidden * table[-4:-3, :]
    result = scale[:, 0:1] * (inner - row_mean(inner) - unit * row_mean(inner * unit))
    grad[...] = result
    rounded = result.astype(LOW)
    low[...] = rounded
    column_sums(sums, rounded.astype(WIDE), hidden * unit, hidden)
    size = pieces[0].shape[1]
    for r, piece in enumerate(pieces):
        piece[...] = against(rounded, weight[at((z ^ r) * size, size), :]).astype(LOW)


def split_rows(bits, full, near, far, order=(0, 1, 2, 3)):
    d, z, c = indices(bits)
    own = full.shape[0] // 32
    for p in range(4):
        for s in range(4):
            start = (d ^ order[p]) * 8 * own + (z ^ order[s]) * 2 * own
            to = (4 * p + s) * own
            near[to : to + own, :] = full[at(start + c * own, own), :]
            far[to : to + own, :] = full[at(start + (1 - c) * own, own), :]


def out_grad_kernel(bits, a0, a1, a2, a3, grad, near, far, full):
    _, z, _ = indices(bits)
    size = a0.shape[1]
    for r, piece in enumerate((a0, a1, a2, a3)):
        full[at((z ^ r) * size, size), :] = cross(piece[...], grad[...]).astype(LOW)
    split_rows(bits, full, near, far, order=(0, 2, 1, 3))


def qkv_grad_kernel(
    bits, t0, t1, t2, t3, dq, dkv, other, heads, one, two, up, near, far, grads, full, extra
):
    d, z, c = indices(bits)
    tokens = jnp.concatenate([t0[...], t1[...], t2[...], t3[...]], axis=0)
    size = dq.shape[1]
    both = (dkv[...] + other[...].astype(WIDE)).astype(LOW)
    grads[:, :size] = dq[...]
    grads[:, size:] = both
    full[...] = cross(tokens, grads[...]).astype(LOW)
    own = full.shape[0] // 32
    tile = full.shape[0] // 8
    lanes = full.shape[1] // tile
    tall = near.shape[0] // 16
    extra[...] = jnp.zeros_like(extra)
    ratio = up.shape[1] // size
    rows = [(one, 0)] + [None] * ratio + [(two, 0), (one, 1), (one, 2), (two, 1), (two, 2)]
    for k in range(8):
        values = []
        for row in range(2):
            value = heads[row : row + 1, k % 2 * tile : (k % 2 + 1) * tile]
            values.append(jnp.where(z == k // 2, value, 0.0))
        for index, source in enumerate(rows):
            if source is None:
                y, x = (index - 1) // 2, (index - 1) % 2
                lane = ((y * 2 + k // 4) * 2 + k % 2) * tile
                mine = jnp.logical_and(bits[1] == x, bits[3] == k // 2 % 2)
                values.append(jnp.where(mine, up[0:1, lane : lane + tile], 0.0))
            else:
                ref, row = source
                values.append(ref[row : row + 1, k * tile : (k + 1) * tile])
        for column, value in enumerate(values):
            row, lane = column // lanes, column % lanes * tile
            extra[k, row : row + 1, lane : lane + tile] = value
    for p in range(4):
        for s in range(4):
            start = (d ^ p) * 8 * own + (z ^ s) * 2 * own
            to = (4 * p + s) * tall
            near[to : to + own, :] = full[at(start + c * own, own), :]
            far[to : to + own, :] = full[at(start + (1 - c) * own, own), :]
            rows = extra[(d ^ p) * 2 + (z ^ s) // 2].astype(LOW)
            near[to + own : to + tall, :] = rows
            far[to + own : to + tall, :] = rows


def rows_grad_kernel(bits, grads, weight, above, own, *parts):
    product = against(grads[...], weight[...])
    count = own.shape[0]
    own[...] = above[...] + product[:count]
    for r, part in enumerate(parts):
        part[...] = product[(r + 1) * count : (r + 2) * count].astype(LOW)


def squares_kernel(bits, down, out, u0, u1, u2, u3, p0, p1, p2, p3, result, small):
    _, _, c = indices(bits)
    own = out.shape[0]
    values = [ref[...].astype(WIDE) for ref in (down, out, u0, u1, u2, u3)]
    values += [ref[:own, :].astype(WIDE) for ref in (p0, p1, p2, p3)]
    rows = sum(ref[own:, :].astype(WIDE) for ref in (p0, p1, p2, p3))
    small[...] = rows
    lane = lax.broadcasted_iota(jnp.int32, rows.shape, 1) % 128
    mine = (lane // own) == bits[3] * 2 + c
    values.append(jnp.where(mine, rows, 0.0))
    total = jnp.zeros((1, 1), WIDE)
    for value in values:
        total += jnp.sum(jnp.sum(value * value, axis=0, keepdims=True), axis=1, keepdims=True)
    result[...] = jnp.broadcast_to(total, result.shape)


def update_kernel(plans, bits, factor, *refs):
    count = len(plans)
    total = sum(plan[2] for plan in plans)
    sources, refs = refs[:total], refs[total:]
    grads, refs = refs[6 * count : 6 * count + total], refs[: 6 * count] + refs[6 * count + total :]
    brought = refs[-3]
    fetches = [
        pltpu.make_async_copy(sources[i], grads[i], brought.at[i]) for i in range(total)
    ]
    for fetch in fetches:
        fetch.start()
    states, results = refs[: 3 * count], refs[3 * count : 6 * count]
    held, made = refs[6 * count : 9 * count], refs[9 * count : 12 * count]
    arrive, leave = refs[-2:]
    loads = [
        pltpu.make_async_copy(states[i], held[i], arrive.at[i]) for i in range(3 * count)
    ]
    stores = [
        pltpu.make_async_copy(made[i], results[i], leave.at[i]) for i in range(3 * count)
    ]
    for load in loads:
        load.start()
    _, z, _ = indices(bits)
    first = 0
    for index, (rate, places, pieces) in enumerate(plans):
        mine = slice(3 * index, 3 * index + 3)
        for load in loads[mine] + fetches[first : first + pieces]:
            load.wait()
        own = held[3 * index].shape[0]
        for r in range(pieces):
            piece = grads[first + r]
            for source, target in places(bits, z, r, piece.shape[1]):
                grad = piece[:own, source].astype(WIDE) * factor[0]
                weight, moment, second = (ref[:, target] for ref in held[mine])
                values = adam_update(weight, grad, moment, second, rate, WEIGHT_DECAY)
                for ref, value in zip(made[mine], values):
                    ref[:, target] = value
        for store in stores[mine]:
            store.start()
        first += pieces
    for store in stores:
        store.wait()


def whole_places(bits, z, r, columns):
    return [(slice(None), slice(None))]


def qkv_places(bits, z, r, columns):
    size = columns // 3
    return [
        (slice(kind * size, (kind + 1) * size), at(kind * 4 * size + (z ^ r) * size, size))
        for kind in range(3)
    ]


def up_places(bits, z, r, columns):
    size = columns // 4
    x, l = bits[1] ^ (r // 2), bits[3] ^ (r % 2)
    return [
        (
            slice((2 * y + h) * size, (2 * y + h + 1) * size),
            at((((y * 2 + x) * 2 + h) * 2 + l) * size, size),
        )
        for y in range(2)
        for h in range(2)
    ]


def on_square(
    tokens,
    cotangent,
    weight_qkv,
    weight_out,
    weight_up,
    weight_down,
    small_params,
    moment_qkv,
    moment_out,
    moment_up,
    moment_down,
    moment_small,
    second_qkv,
    second_out,
    second_up,
    second_down,
    second_small,
):
    rows = tokens[0]
    count, width = rows.shape
    own = weight_qkv.shape[0]
    down_rows = weight_down.shape[0]
    ratio = weight_up.shape[1] // width
    columns = small_params.shape[1]
    part = width // 4
    units = weight_up.shape[1] // 4
    pad = 8
    tall = own + pad
    iy, ix, ih, il, ic = (lax.axis_index(name) for name in AXES)
    bits = jnp.stack([iy, ix, ih, il, ic]).astype(jnp.int32)
    at_dp, at_z = 2 * iy + ix, 2 * ih + il
    place = 8 * at_dp + 2 * at_z + ic

    low_small = small_params.astype(LOW).T.reshape(1, own * columns)
    low_small = jnp.pad(low_small, ((0, pad - 1), (0, 3 * part - own * columns)))
    with jax.named_scope("weight_qkv"):
        pieces = call(pack_qkv_kernel, [((tall, 3 * part), LOW)] * 4, bits, weight_qkv, low_small)
    with jax.named_scope("tokens"):
        token_l, token_h = swap(rows, ("l",)), swap(rows, ("h",))
    low_out, low_down, up_near, up_far = call(
        pack_rest_kernel,
        [((own, width), LOW), ((down_rows, width), LOW)] + [((2 * own, units), LOW)] * 2,
        bits,
        weight_out,
        weight_up,
        weight_down,
    )
    with jax.named_scope("weight_qkv"):
        near_qkv = jnp.concatenate(exchange(pieces, "h", "l"), axis=0)
        near_qkv = after(near_qkv, token_l, low_out)
    with jax.named_scope("weight_up"):
        up_far = send(up_far, ("x",), start=(near_qkv,))
        up_last = swap(jnp.concatenate([up_near[own:], up_far[own:]], axis=0), ("l",))
        near_up = [up_near[:own], up_last[:own], up_far[:own], up_last[own:]]
        near_up = jnp.concatenate(near_up, axis=0)
    with jax.named_scope("weight_out"):
        out_other = send(low_out, ("l",), start=(near_qkv,))
    with jax.named_scope("weight_qkv"):
        near_qkv = jnp.concatenate(exchange([near_qkv] * 4, "y", "x"), axis=0)
    near_qkv, token_h, near_up, out_other = tie(near_qkv, token_h, near_up, out_other)
    with jax.named_scope("weight_qkv"):
        far_qkv = swap(near_qkv, ("c",))
    with jax.named_scope("tokens"):
        token_parts = [rows, token_l, token_h, swap(token_h, ("l",))]
    with jax.named_scope("weight_up"):
        up_other = swap(near_up, ("h",))
    rows_of = lambda v: v.reshape(16, tall, 3 * part)[:, own, : own * columns]
    blocks = jnp.concatenate([rows_of(near_qkv), rows_of(far_qkv)], axis=0).astype(WIDE)
    index = jnp.arange(32)
    owner = (((index // 4) % 4) ^ at_dp) * 8 + ((index % 4) ^ at_z) * 2 + ((index // 16) ^ ic)
    chosen = (owner[None, :] == index[:, None]).astype(WIDE)
    blocks = jnp.dot(chosen, blocks)
    table = blocks.reshape(32, columns, own).transpose(1, 0, 2).reshape(columns, width)
    bias_heads = lax.dynamic_slice_in_dim(table[0:2], at_z * part, part, axis=1)
    bias_units = table[3 : 3 + ratio].reshape(2, 2, 2, 2, units // 4)
    bias_units = lax.dynamic_slice(bias_units, (0, ix, 0, il, 0), (2, 1, 2, 1, units // 4))
    bias_units = bias_units.reshape(1, units)

    far_qkv, token_parts[3], table, bias_heads, bias_units = tie(
        far_qkv, token_parts[3], table, bias_heads, bias_units
    )
    with jax.named_scope("weight_out"):
        near_out = jnp.concatenate([low_out, after(out_other, token_parts[3])], axis=0)
        out_other = swap(near_out, ("h",))
    far_qkv, up_other = tie(far_qkv, after(up_other, far_qkv))

    vmem, hbm = pl.BlockSpec(memory_space=pltpu.VMEM), pl.BlockSpec(memory_space=pltpu.HBM)
    q, kv, full_qkv = pl.pallas_call(
        project_kernel,
        name="project_kernel",
        in_specs=[pl.BlockSpec(memory_space=pltpu.SMEM), vmem] + [hbm] * 6,
        out_specs=[vmem] * 3,
        out_shape=[
            jax.ShapeDtypeStruct((4 * count, part), LOW),
            jax.ShapeDtypeStruct((4 * count, 2 * part), LOW),
            jax.ShapeDtypeStruct((width, 3 * part), LOW),
        ],
        scratch_shapes=[
            pltpu.VMEM(near_qkv.shape, LOW),
            pltpu.VMEM(far_qkv.shape, LOW),
            pltpu.VMEM((4 * count, width), LOW),
            pltpu.SemaphoreType.DMA((6,)),
        ],
        compiler_params=pltpu.CompilerParams(vmem_limit_bytes=48 * 2**20),
        cost_estimate=pl.CostEstimate(flops=1, bytes_accessed=1, transcendentals=0),
    )(bits, bias_heads, near_qkv, far_qkv, *token_parts)
    kv, out_other = tie(kv, out_other)
    with jax.named_scope("keys_values"):
        kv_far = swap(kv, ("c",))
    with jax.named_scope("weight_out"):
        near_out = jnp.concatenate([near_out, out_other], axis=0)
        out_parts = exchange([near_out] * 4, "y", "x")
    late_q, late_down, late_up = tie(q, after(low_down, kv_far), near_up)
    with jax.named_scope("weight_up"):
        near_up = jnp.concatenate([late_up, up_other], axis=0)
        up_other = swap(near_up, ("y",))
    with jax.named_scope("weight_down"):
        down_other = swap(late_down, ("h",))
    *attended, lse = call(
        forward_kernel,
        [((count, part), LOW)] * 4 + [((4, 4 * count), WIDE)],
        bits,
        late_q,
        kv,
        kv_far,
    )
    out_parts = [near_out] + [after(piece, lse) for piece in out_parts[1:]]
    near_out = jnp.concatenate(out_parts, axis=0)
    *attended, down_other, near_out = tie(*attended, after(down_other, lse), near_out)
    with jax.named_scope("attended"):
        attended = exchange(attended, "h", "l")
    with jax.named_scope("weight_out"):
        far_out = swap(near_out, ("c",))
        (full_out,) = call(lay_qkv_kernel, [((width, width), LOW)], bits, near_out, far_out)
    attended[1:], up_other, down_other = lax.optimization_barrier(
        (attended[1:], up_other, down_other)
    )
    with jax.named_scope("weight_up"):
        near_up = jnp.concatenate([near_up, up_other], axis=0)
        far_up = swap(near_up, ("c",))
    with jax.named_scope("weight_down"):
        near_down = jnp.concatenate([low_down, down_other], axis=0)
        down_other = swap(near_down, ("y",))
    hidden, hidden_low, normed, scale = call(
        out_kernel,
        [((count, width), WIDE), ((count, width), LOW), ((count, width), WIDE), ((count, 128), WIDE)],
        bits,
        *attended,
        full_out,
        rows,
        table,
    )

    half = count // 2
    with jax.named_scope("hidden"):
        from_l, from_x = swap(hidden_low, ("l",)), swap(hidden_low, ("x",))
    from_l, from_x, far_up, down_other = tie(
        from_l, from_x, after(far_up, from_l, from_x), after(down_other, from_l, from_x)
    )
    with jax.named_scope("hidden"):
        hidden_parts = [hidden_low, from_l, from_x]
        hidden_parts += [swap(from_x[:half], ("l",)), swap(from_l[half:], ("x",))]
    with jax.named_scope("weight_down"):
        near_down = jnp.concatenate([near_down, down_other], axis=0)
        far_down = swap(near_down, ("c",))
    (full_up,) = call(lay_up_kernel, [((width, units), LOW)], bits, near_up, far_up)
    (full_down,) = call(lay_down_kernel, [((units, width), LOW)], bits, near_down, far_down)
    parts_shape = [((count, width), WIDE)] * 3 + [((count // 2, width), LOW)] * 2
    hidden_parts[3], full_down = tie(hidden_parts[3], full_down)
    act, slope = call(
        feed_up_kernel,
        [((4 * count, units), LOW)] * 2,
        bits,
        *hidden_parts,
        full_up,
        bias_units,
        flops=10**9,
    )
    parts = call(feed_down_kernel, parts_shape, bits, act, full_down)
    terms = scatter_square(parts, "x", "l")
    output, grad_two, grad_down, sums_two = call(
        norm_two_kernel,
        [((count, width), LOW), ((count, width), WIDE), ((count, width), LOW), ((8, width), WIDE)],
        bits,
        *terms,
        hidden,
        cotangent[0],
        table,
    )

    with jax.named_scope("grad_down"):
        grad_parts = gather_square(grad_down, "x", "l")
    grad_up, sums_up, *parts = call(
        feed_back_kernel,
        [((4 * count, units), LOW), ((8, units), WIDE)] + parts_shape,
        bits,
        *grad_parts,
        full_down,
        full_up,
        slope,
        flops=2 * 10**9,
    )
    with jax.named_scope("grad_hidden"):
        terms = scatter_square(parts, "x", "l")

    feed_near, feed_far = call(
        feed_grad_kernel,
        [((16 * own + 4 * down_rows, width), LOW)] * 2,
        bits,
        act,
        *grad_parts,
        *hidden_parts,
        grad_up,
        scratch=[pltpu.VMEM((units, width), LOW), pltpu.VMEM((width, units), LOW)],
    )

    def halve(value, axis, start=(), use=()):
        size = value.shape[0] // 2
        other = send(value[size:].astype(LOW), (axis,), start, use)
        return value[:size].astype(WIDE) + other.astype(WIDE)

    with jax.named_scope("grad_weight_feed"):
        feed_other = swap(feed_far, ("c",))
        feed_sum = (feed_near.astype(WIDE) + feed_other.astype(WIDE)).astype(LOW)
    *terms, feed_sum = lax.optimization_barrier((*terms, feed_sum))
    grad_middle, grad_branch, sums_one, *douts = call(
        norm_one_kernel,
        [((count, width), WIDE), ((count, width), LOW), ((8, width), WIDE)]
        + [((count, part), LOW)] * 4,
        bits,
        *terms,
        grad_two,
        normed,
        scale,
        full_out,
        table,
    )
    with jax.named_scope("grad_attended"):
        douts = exchange(douts, "h", "l")
    back = tuple(douts[1:])
    out_near, out_far = call(
        out_grad_kernel,
        [((16 * own, width), LOW)] * 2,
        bits,
        *attended,
        grad_branch,
        scratch=[pltpu.VMEM((width, width), LOW)],
    )
    with jax.named_scope("grad_weight_feed"):
        feed_other = swap(feed_sum[feed_sum.shape[0] // 2 :], ("y",))
    with jax.named_scope("grad_weight_out"):
        out_other = send(out_far, ("c",), use=back)
        out_sum = (out_near.astype(WIDE) + out_other.astype(WIDE)).astype(LOW)
    late_lse, out_sum = tie(lse, out_sum)
    dq, dkv_near, dkv_far, sums_heads = call(
        backward_kernel,
        [
            ((4 * count, part), LOW),
            ((4 * count, 2 * part), WIDE),
            ((4 * count, 2 * part), LOW),
            ((8, part), WIDE),
        ],
        bits,
        q,
        kv,
        kv_far,
        late_lse,
        *douts,
    )
    with jax.named_scope("grad_weight_out"):
        out_sum = halve(out_sum, "x", use=(dq,)).astype(LOW)
    def add_first(value, other):
        return value[: other.shape[0]].astype(WIDE) + other.astype(WIDE)

    feed_sum = add_first(feed_sum, after(feed_other, dq)).astype(LOW)
    dkv_far, out_sum, feed_sum = tie(dkv_far, out_sum, feed_sum)
    up_size = 4 * own
    rows_of_part = lambda start, size: jnp.concatenate(
        [feed_sum[start : start + size], feed_sum[start + up_size + down_rows :][:size]], axis=0
    )
    up_sum, down_sum = rows_of_part(0, up_size), rows_of_part(up_size, down_rows)
    with jax.named_scope("grad_keys_values"):
        dkv_other = swap(dkv_far, ("c",))
    with jax.named_scope("grad_weight_up"):
        up_other = swap(up_sum[up_size:], ("h",))
    with jax.named_scope("grad_weight_out"):
        out_other = swap(out_sum[out_sum.shape[0] // 2 :], ("y",))
    near, far, grad_projected = call(
        qkv_grad_kernel,
        [((16 * tall, 3 * part), LOW)] * 2 + [((4 * count, 3 * part), LOW)],
        bits,
        *token_parts,
        dq,
        dkv_near,
        dkv_other,
        sums_heads,
        sums_one,
        sums_two,
        sums_up,
        scratch=[pltpu.VMEM((width, 3 * part), LOW), pltpu.VMEM((8, 8, 3 * part), WIDE)],
    )
    out_sum = add_first(out_sum, after(out_other, near)).astype(LOW)
    owned_up = add_first(up_sum, after(up_other, near)).astype(LOW)
    far, out_sum, owned_up, down_sum = tie(far, out_sum, owned_up, down_sum)
    with jax.named_scope("grad_weight_qkv"):
        far_other = swap(far, ("c",))
        qkv_sum = (near.astype(WIDE) + far_other.astype(WIDE)).astype(LOW)
    with jax.named_scope("grad_weight_out"):
        out_other = swap(out_sum[2 * own :], ("l",))
    with jax.named_scope("grad_weight_up"):
        up_other = swap(owned_up[2 * own :], ("x",))
    with jax.named_scope("grad_weight_down"):
        down_other = swap(down_sum[down_rows:], ("h",))
    qkv_sum, up_other = tie(qkv_sum, after(up_other, far_other))
    with jax.named_scope("grad_weight_up"):
        up_last = swap(jnp.concatenate([owned_up[own : 2 * own], up_other[own:]], axis=0), ("l",))
    parts = call(
        rows_grad_kernel,
        [((count, width), WIDE)] + [((count, width), LOW)] * 3,
        bits,
        after(grad_projected, far_other),
        full_qkv,
        grad_middle,
    )
    with jax.named_scope("grad_weight_qkv"):
        blocks = [qkv_sum[i * 4 * tall : (i + 1) * 4 * tall] for i in range(4)]
        blocks = exchange(blocks, "y", "x")
        owned_qkv = sum(block.astype(WIDE) for block in blocks).astype(LOW)
    late = tuple(blocks[1:])
    out_sum = add_first(out_sum, after(out_other, *late)).astype(LOW)
    owned_down = add_first(down_sum, after(down_other, *late))
    owned_qkv, owned_down, up_last, out_sum, *parts = tie(
        owned_qkv, owned_down, after(up_last, *late), out_sum, *parts
    )
    up_pieces = [owned_up[:own], up_last[:own], up_other[:own], up_last[own:]]
    with jax.named_scope("grad_weight_qkv"):
        qkv_pieces = exchange([owned_qkv[i * tall : (i + 1) * tall] for i in range(4)], "h", "l")
    with jax.named_scope("grad_weight_out"):
        owned_out = add_first(out_sum, send(out_sum[own:], ("h",), use=(qkv_pieces[1],)))

    total, small_tile = call(
        squares_kernel,
        [((8, 128), WIDE), ((8, 3 * part), WIDE)],
        bits,
        owned_down,
        owned_out,
        *up_pieces,
        *qkv_pieces,
    )
    tile = width // 8
    lanes = 3 * part // tile
    small_tile = small_tile[:2].reshape(2 * lanes, tile)[:columns]
    owned_small = lax.dynamic_slice_in_dim(small_tile, (2 * il + ic) * own, own, axis=1).T
    def sum_square(value, a, b):
        terms = exchange([value] * 4, a, b)
        return (terms[0] + terms[1]) + (terms[2] + terms[3])

    with jax.named_scope("norm"):
        total = total + swap(total, ("c",))
        total = sum_square(total, "h", "l")
    with jax.named_scope("grad_tokens"):
        far_l = send(parts[3], ("l",), start=(total,))
        from_l = send(parts[1], ("l",), start=(total,))
        to_h = (parts[2].astype(WIDE) + far_l.astype(WIDE)).astype(LOW)
    with jax.named_scope("norm"):
        total = sum_square(total, "y", "x")
    total, to_h = tie(total, to_h)
    with jax.named_scope("grad_tokens"):
        from_h = swap(to_h, ("h",))
    grad_rows = parts[0] + from_l.astype(WIDE) + from_h.astype(WIDE)
    grad_norm = jnp.sqrt(total[0, 0])
    factor = jnp.minimum(1.0, CLIP_LIMIT / (grad_norm + 1e-06))
    held = jnp.full((1,), factor)

    states = [
        (weight_down, moment_down, second_down),
        (weight_out, moment_out, second_out),
        (weight_up, moment_up, second_up),
        (weight_qkv, moment_qkv, second_qkv),
    ]
    plans = [
        (RATE_MATRIX, whole_places, 1),
        (RATE_OUTPUT, whole_places, 1),
        (RATE_MATRIX, up_places, 4),
        (RATE_MATRIX, qkv_places, 4),
    ]
    grads = [owned_down, owned_out, *up_pieces, *qkv_pieces]
    flat = [array for group in states for array in group]
    results = pl.pallas_call(
        functools.partial(update_kernel, plans),
        name="update_kernel",
        in_specs=[pl.BlockSpec(memory_space=pltpu.SMEM)] * 2
        + [pl.BlockSpec(memory_space=pltpu.HBM)] * (len(grads) + 12),
        out_specs=[pl.BlockSpec(memory_space=pltpu.HBM)] * 12,
        out_shape=[jax.ShapeDtypeStruct(array.shape, WIDE) for array in flat],
        scratch_shapes=[pltpu.VMEM(grad.shape, grad.dtype) for grad in grads]
        + [pltpu.VMEM(array.shape, WIDE) for array in flat * 2]
        + [pltpu.SemaphoreType.DMA((len(grads),))]
        + [pltpu.SemaphoreType.DMA((12,))] * 2,
        compiler_params=pltpu.CompilerParams(vmem_limit_bytes=60 * 2**20),
        cost_estimate=pl.CostEstimate(flops=1, bytes_accessed=1, transcendentals=0),
    )(bits, held, *grads, *flat)
    new_down, new_moment_down, new_second_down = results[0:3]
    new_out, new_moment_out, new_second_out = results[3:6]
    new_up, new_moment_up, new_second_up = results[6:9]
    new_qkv, new_moment_qkv, new_second_qkv = results[9:12]
    new_small, new_moment_small, new_second_small = adam_update(
        small_params, owned_small * factor, moment_small, second_small, RATE_SMALL, 0.0
    )
    return (
        output[None],
        grad_rows[None],
        grad_norm,
        new_qkv,
        new_out,
        new_up,
        new_down,
        new_small,
        new_moment_qkv,
        new_moment_out,
        new_moment_up,
        new_moment_down,
        new_moment_small,
        new_second_qkv,
        new_second_out,
        new_second_up,
        new_second_down,
        new_second_small,
    )


def solution(mesh):
    sizes = (mesh.shape["dp"], mesh.shape["seq"])
    if sizes == (4, 8):
        squares = Mesh(mesh.devices.reshape(2, 2, 2, 2, 2), AXES)
        dp, seq = ("y", "x"), ("h", "l", "c")
        body, mesh = on_square, squares
        every = P(AXES, None)
        over = P(dp, seq, None)
    else:
        body = on_device
        every = P(("dp", "seq"), None)
        over = P("dp", "seq", None)
    return jax.shard_map(
        body,
        mesh=mesh,
        in_specs=(over,) * 2 + (every,) * 15,
        out_specs=(over,) * 2 + (P(),) + (every,) * 15,
        check_vma=False,
    )
```

profile of v0, /device:TPU:0, one launch (start us, length us, event | category | flops | bytes accessed | tf_op | source)
XLA Modules:
  0.0 280.1 jit_solution(10840785145894115214)
XLA Ops:
  0.7 3.1 %collective-permute-start.3 = (bf16[128,1024]{1,0:T(8,128)(2,1)}, bf16[128,1024]{1,0:T(8,128)(2,1)S(1)}, u32[]{:S(2)}, u32[]{:S(2)}) collective-permute-start(bf16[128,1024]{1,0:T(8,128)(2,1)} %bitcast.31), channel_id=1, source_target_pairs={{0,2},{2,0},{1,3},{3,1},{4,6},{6,4},{5,7},{7,5},{8,10},{10,8},{9,1... | collective-permute-start | bytes 786440 | tf_op jit(solution)/shard_map/tokens/ppermute | solution.py:339
  6.3 3.0 %collective-permute-start.1 = (bf16[40,768]{1,0:T(8,128)(2,1)S(1)}, bf16[40,768]{1,0:T(8,128)(2,1)S(1)}, u32[]{:S(2)}, u32[]{:S(2)}) collective-permute-start(bf16[40,768]{1,0:T(8,128)(2,1)S(1)} %get-tuple-element.177), channel_id=1, source_target_pairs={{0,4},{4,0},{1,5},{5,1},{2,6},{6,2},{3,7},{7,3},{8,12},{12,8},{9,1... | collective-permute-start | bytes 184328 | tf_op jit(solution)/shard_map/weight_qkv/ppermute | solution.py:339
  24.2 4.4 %collective-permute-start.10 = (bf16[32,1024]{1,0:T(8,128)(2,1)S(1)}, bf16[32,1024]{1,0:T(8,128)(2,1)S(1)}, u32[]{:S(2)}, u32[]{:S(2)}) collective-permute-start(bf16[32,1024]{1,0:T(8,128)(2,1)S(1)} %get-tuple-element.184), channel_id=1, source_target_pairs={{0,2},{2,0},{1,3},{3,1},{4,6},{6,4},{5,7},{7,5},{8,10},{10,8},{9,1... | collective-permute-start | bytes 196616 | tf_op jit(solution)/shard_map/weight_out/ppermute | solution.py:339
  29.7 2.5 collective-permute-start.9
  32.3 2.9 %collective-permute-done.9 = bf16[64,1024]{1,0:T(8,128)(2,1)S(1)} collective-permute-done((bf16[64,1024]{1,0:T(8,128)(2,1)S(1)}, bf16[64,1024]{1,0:T(8,128)(2,1)S(1)}, u32[]{:S(2)}, u32[]{:S(2)}) %collective-permute-start.9) | collective-permute-done | bytes 131104 | tf_op jit(solution)/shard_map/weight_up/ppermute | solution.py:339
  35.4 2.9 %collective-permute-start.13 = (bf16[128,1024]{1,0:T(8,128)(2,1)S(1)}, bf16[128,1024]{1,0:T(8,128)(2,1)}, u32[]{:S(2)}, u32[]{:S(2)}) collective-permute-start(bf16[128,1024]{1,0:T(8,128)(2,1)S(1)} %pad_maximum_fusion.4), channel_id=1, source_target_pairs={{0,4},{4,0},{1,5},{5,1},{2,6},{6,2},{3,7},{7,3},{8,12},{12,8},{9,1... | collective-permute-start | bytes 786440 | tf_op jit(solution)/shard_map/weight_up/ppermute | solution.py:339
  42.9 1.7 copy.44
  45.6 4.5 %collective-permute-done.12.t3 = bf16[128,1024]{1,0:T(8,128)(2,1)S(1)} collective-permute-done((bf16[128,1024]{1,0:T(8,128)(2,1)S(1)}, bf16[128,1024]{1,0:T(8,128)(2,1)S(1)}, u32[]{:S(2)}, u32[]{:S(2)}) %collective-permute-start.12) | collective-permute-done | bytes 262176 | tf_op jit(solution)/shard_map/tokens/ppermute | solution.py:339
  50.1 2.7 collective-permute-start.14
  55.0 2.6 project_kernel.1
  65.2 7.2 %forward_kernel.1 = (bf16[128,256]{1,0:T(8,128)(2,1)S(1)}, bf16[128,256]{1,0:T(8,128)(2,1)S(1)}, bf16[128,256]{1,0:T(8,128)(2,1)S(1)}, bf16[128,256]{1,0:T(8,128)(2,1)S(1)}, f32[4,512]{1,0:T(4,128)S(1)}) custom-call(s32[5]{0:T(128)S(1)} %stack.23.bits, bf16[512,256]{1,0:T(8,128)(2,1)S(1)} %get-tuple-element.200.q_ref, ...), custom_call_target="tpu_custom_call" | custom-call | flops 1 | bytes 1 | tf_op jit(solution)/shard_map/forward_kernel/pallas_call | solution.py:389
  72.5 2.0 collective-permute-done.19
  74.5 2.4 collective-permute-done.18
  77.2 2.8 collective-permute-start.21
  82.7 2.4 collective-permute-done.21.a2
  93.2 8.5 %collective-permute-done.28 = bf16[256,1024]{1,0:T(8,128)(2,1)S(1)} collective-permute-done((bf16[256,1024]{1,0:T(8,128)(2,1)S(1)}, bf16[256,1024]{1,0:T(8,128)(2,1)S(1)}, u32[]{:S(2)}, u32[]{:S(2)}) %collective-permute-start.28) | collective-permute-done | bytes 524320 | tf_op jit(solution)/shard_map/weight_down/ppermute | solution.py:339
  105.2 2.6 collective-permute-done.29.h3
  107.9 2.5 feed_up_kernel.1
  111.4 1.8 feed_down_kernel.1
  113.2 1.8 collective-permute-start.34
  115.7 2.7 collective-permute-done.34
  121.0 4.7 %collective-permute-done.35.from_a = bf16[128,1024]{1,0:T(8,128)(2,1)S(1)} collective-permute-done((bf16[128,1024]{1,0:T(8,128)(2,1)S(1)}, bf16[128,1024]{1,0:T(8,128)(2,1)S(1)}, u32[]{:S(2)}, u32[]{:S(2)}) %collective-permute-start.35) | collective-permute-done | bytes 262176 | tf_op jit(solution)/shard_map/ppermute | solution.py:339
  130.5 5.6 %collective-permute-done.37.g2 = bf16[128,1024]{1,0:T(8,128)(2,1)S(1)} collective-permute-done((bf16[128,1024]{1,0:T(8,128)(2,1)S(1)}, bf16[128,1024]{1,0:T(8,128)(2,1)S(1)}, u32[]{:S(2)}, u32[]{:S(2)}) %collective-permute-start.37) | collective-permute-done | bytes 262176 | tf_op jit(solution)/shard_map/grad_down/ppermute | solution.py:339
  138.3 2.8 %collective-permute-done.38.g3 = bf16[64,1024]{1,0:T(8,128)(2,1)S(1)} collective-permute-done((bf16[64,1024]{1,0:T(8,128)(2,1)S(1)}, bf16[64,1024]{1,0:T(8,128)(2,1)S(1)}, u32[]{:S(2)}, u32[]{:S(2)}) %collective-permute-start.38) | collective-permute-done | bytes 131104 | tf_op jit(solution)/shard_map/grad_down/ppermute | solution.py:339
  141.8 4.7 %feed_back_kernel.1 = (bf16[512,1024]{1,0:T(8,128)(2,1)S(1)}, f32[8,1024]{1,0:T(8,128)S(1)}, f32[128,1024]{1,0:T(8,128)S(1)}, f32[128,1024]{1,0:T(8,128)S(1)}, f...) custom-call(s32[5]{0:T(128)S(1)} %stack.23.bits, ...), custom_call_target="tpu_custom_call" | custom-call | flops 1 | bytes 1 | tf_op jit(solution)/shard_map/feed_back_kernel/pallas_call | solution.py:389
  146.5 5.1 %feed_grad_kernel.1 = (bf16[1024,1024]{1,0:T(8,128)(2,1)}, bf16[1024,1024]{1,0:T(8,128)(2,1)}) custom-call(s32[5]{0:T(128)S(1)} %stack.23.bits, bf16[512,1024]{1,0:T(8,128)(2,1)S(1)} %get-tuple-element.235.act, bf16[128,1024]{1,0:T(8,128)(2,1)S(1)} %get-tuple-element.244.g0, bf16[128,1024]{1,0:T(8,128)(2,1)S(1)} %collective-permute-done.36.g1, ...), custom_call_target="tpu_custom_call" | custom-call | flops 1 | bytes 1 | tf_op jit(solution)/shard_map/feed_grad_kernel/pallas_call | solution.py:389
  153.7 3.8 %collective-permute-done.42 = bf16[64,1024]{1,0:T(8,128)(2,1)S(1)} collective-permute-done((bf16[64,1024]{1,0:T(8,128)(2,1)S(1)}, bf16[64,1024]{1,0:T(8,128)(2,1)S(1)}, u32[]{:S(2)}, u32[]{:S(2)}) %collective-permute-start.42) | collective-permute-done | bytes 131104 | tf_op jit(solution)/shard_map/grad_hidden/ppermute | solution.py:339
  160.8 4.7 %collective-permute-done.43.from_a = bf16[128,1024]{1,0:T(8,128)(2,1)S(1)} collective-permute-done((bf16[128,1024]{1,0:T(8,128)(2,1)S(1)}, bf16[128,1024]{1,0:T(8,128)(2,1)S(1)}, u32[]{:S(2)}, u32[]{:S(2)}) %collective-permute-start.43) | collective-permute-done | bytes 262176 | tf_op jit(solution)/shard_map/grad_hidden/ppermute | solution.py:339
  175.0 5.4 %collective-permute-done.47.d2 = bf16[128,256]{1,0:T(8,128)(2,1)S(1)} collective-permute-done((bf16[128,256]{1,0:T(8,128)(2,1)S(1)}, bf16[128,256]{1,0:T(8,128)(2,1)S(1)}, u32[]{:S(2)}, u32[]{:S(2)}) %collective-permute-start.47) | collective-permute-done | bytes 65568 | tf_op jit(solution)/shard_map/grad_attended/ppermute | solution.py:339
  181.9 8.6 %backward_kernel.1 = (bf16[512,256]{1,0:T(8,128)(2,1)S(1)}, f32[512,512]{1,0:T(8,128)S(1)}, bf16[512,512]{1,0:T(8,128)(2,1)S(1)}, f32[8,256]{1,0:T(8,128)S(1)}) custom-call(s32[5]{0:T(128)S(1)} %stack.23.bits, bf16[512,256]{1,0:T(8,128)(2,1)S(1)} %copy-done.18, bf16[512,512]{1,0:T(8,128)(2,1)S(1)} %get-tuple-element.198.near, ...), custom_call_target="tpu_custom_call" | custom-call | flops 1 | bytes 1 | tf_op jit(solution)/shard_map/backward_kernel/pallas_call | solution.py:389
  190.5 5.3 %collective-permute-done.50 = bf16[512,1024]{1,0:T(8,128)(2,1)S(1)} collective-permute-done((bf16[512,1024]{1,0:T(8,128)(2,1)S(1)}, bf16[512,1024]{1,0:T(8,128)(2,1)S(1)}, u32[]{:S(2)}, u32[]{:S(2)}) %collective-permute-start.50) | collective-permute-done | bytes 1048608 | tf_op jit(solution)/shard_map/grad_weight_feed/ppermute | solution.py:339
  197.0 2.3 collective-permute-start.53
  199.4 1.8 qkv_grad_kernel.1
  201.3 4.1 %collective-permute-done.52 = bf16[128,1024]{1,0:T(8,128)(2,1)S(1)} collective-permute-done((bf16[128,1024]{1,0:T(8,128)(2,1)S(1)}, bf16[128,1024]{1,0:T(8,128)(2,1)S(1)}, u32[]{:S(2)}, u32[]{:S(2)}) %collective-permute-start.52) | collective-permute-done | bytes 262176 | tf_op jit(solution)/shard_map/grad_weight_out/ppermute | solution.py:339
  205.4 6.6 %collective-permute-done.53 = bf16[128,1024]{1,0:T(8,128)(2,1)S(1)} collective-permute-done((bf16[128,1024]{1,0:T(8,128)(2,1)S(1)}, bf16[128,1024]{1,0:T(8,128)(2,1)S(1)}, u32[]{:S(2)}, u32[]{:S(2)}) %collective-permute-start.53) | collective-permute-done | bytes 262176 | tf_op jit(solution)/shard_map/grad_weight_up/ppermute | solution.py:339
  212.3 1.7 collective-permute-start.55
  214.0 4.2 %collective-permute-done.55 = bf16[64,1024]{1,0:T(8,128)(2,1)S(1)} collective-permute-done((bf16[64,1024]{1,0:T(8,128)(2,1)S(1)}, bf16[64,1024]{1,0:T(8,128)(2,1)S(1)}, u32[]{:S(2)}, u32[]{:S(2)}) %collective-permute-start.55) | collective-permute-done | bytes 131104 | tf_op jit(solution)/shard_map/grad_weight_up/ppermute | solution.py:339
  222.2 1.7 collective-permute-start.60
  225.4 2.2 rows_grad_kernel.1
  227.6 5.0 %collective-permute-done.58 = bf16[160,768]{1,0:T(8,128)(2,1)S(1)} collective-permute-done((bf16[160,768]{1,0:T(8,128)(2,1)S(1)}, bf16[160,768]{1,0:T(8,128)(2,1)S(1)}, u32[]{:S(2)}, u32[]{:S(2)}) %collective-permute-start.58) | collective-permute-done | bytes 245792 | tf_op jit(solution)/shard_map/grad_weight_qkv/ppermute | solution.py:339
  234.0 2.9 %collective-permute-done.59 = bf16[128,1024]{1,0:T(8,128)(2,1)S(1)} collective-permute-done((bf16[128,1024]{1,0:T(8,128)(2,1)S(1)}, bf16[128,1024]{1,0:T(8,128)(2,1)S(1)}, u32[]{:S(2)}, u32[]{:S(2)}) %collective-permute-start.59) | collective-permute-done | bytes 262176 | tf_op jit(solution)/shard_map/grad_weight_down/ppermute | solution.py:339
  237.3 3.2 %collective-permute-start.63 = (bf16[40,768]{1,0:T(8,128)(2,1)S(1)}, bf16[40,768]{1,0:T(8,128)(2,1)S(1)}, u32[]{:S(2)}, u32[]{:S(2)}) collective-permute-start(bf16[40,768]{1,0:T(8,128)(2,1)S(1)} %get-tuple-element.345), channel_id=1, source_target_pairs={{0,2},{2,0},{1,3},{3,1},{4,6},{6,4},{5,7},{7,5},{8,10},{10,8},{9,1... | collective-permute-start | bytes 184328 | tf_op jit(solution)/shard_map/grad_weight_qkv/ppermute | solution.py:339
  243.6 3.1 %collective-permute-done.65.p3.refs_9_ = bf16[40,768]{1,0:T(8,128)(2,1)S(1)} collective-permute-done((bf16[40,768]{1,0:T(8,128)(2,1)S(1)}, bf16[40,768]{1,0:T(8,128)(2,1)S(1)}, u32[]{:S(2)}, u32[]{:S(2)}) %collective-permute-start.65) | collective-permute-done | bytes 61472 | tf_op jit(solution)/shard_map/grad_weight_qkv/ppermute | solution.py:339
  250.1 1.7 collective-permute-start.69
  251.8 2.7 collective-permute-start.67
  256.3 1.8 collective-permute-start.74
  265.5 3.1 %collective-permute-start.75 = (bf16[128,1024]{1,0:T(8,128)(2,1)S(1)}, bf16[128,1024]{1,0:T(8,128)(2,1)S(1)}, u32[]{:S(2)}, u32[]{:S(2)}) collective-permute-start(bf16[128,1024]{1,0:T(8,128)(2,1)S(1)} %add_convert_fusion.5), channel_id=1, source_target_pairs={{0,4},{4,0},{1,5},{5,1},{2,6},{6,2},{3,7},{7,3},{8,12},{12,8},{9,1... | collective-permute-start | bytes 786440 | tf_op jit(solution)/shard_map/grad_tokens/ppermute | solution.py:339
  270.0 5.3 %update_kernel.1 = (f32[128,1024]{1,0:T(8,128)}, f32[128,1024]{1,0:T(8,128)}, f32[128,1024]{1,0:T(8,128)}, f32[32,1024]{1,0:T(8,128)}, f32[32,1024]{1,0:T(8,128)...) custom-call(s32[5]{0:T(128)} %copy-done.45, ...), custom_call_target="tpu_custom_call" | custom-call | flops 1 | bytes 1 | tf_op jit(solution)/shard_map/update_kernel/pallas_call | solution.py:1259
  (325 shorter events, 104.7 us)
Async XLA Ops:
  0.7 17.0 %collective-permute-start.3 = (bf16[128,1024]{1,0:T(8,128)(2,1)}, bf16[128,1024]{1,0:T(8,128)(2,1)S(1)}, u32[]{:S(2)}, u32[]{:S(2)}) collective-permute-start(bf16[128,1024]{1,0:T(8,128)(2,1)} %bitcast.31), channel_id=1, source_target_pairs={{0,2},{2,0},{1,3},{3,1},{4,6},{6,4},{5,7},{7,5},{8,10},{10,8},{9,1... | collective-permute-start | bytes 786440 | tf_op jit(solution)/shard_map/tokens/ppermute | solution.py:339
  6.2 9.8 %collective-permute-start = (bf16[40,768]{1,0:T(8,128)(2,1)S(1)}, bf16[40,768]{1,0:T(8,128)(2,1)S(1)}, u32[]{:S(2)}, u32[]{:S(2)}) collective-permute-start(bf16[40,768]{1,0:T(8,128)(2,1)S(1)} %get-tuple-element.176), channel_id=1, source_target_pairs={{0,2},{2,0},{1,3},{3,1},{4,6},{6,4},{5,7},{7,5},{8,10},{10,8},{9,1... | collective-permute-start | bytes 184328 | tf_op jit(solution)/shard_map/weight_qkv/ppermute | solution.py:339
  6.3 9.7 %collective-permute-start.1 = (bf16[40,768]{1,0:T(8,128)(2,1)S(1)}, bf16[40,768]{1,0:T(8,128)(2,1)S(1)}, u32[]{:S(2)}, u32[]{:S(2)}) collective-permute-start(bf16[40,768]{1,0:T(8,128)(2,1)S(1)} %get-tuple-element.177), channel_id=1, source_target_pairs={{0,4},{4,0},{1,5},{5,1},{2,6},{6,2},{3,7},{7,3},{8,12},{12,8},{9,1... | collective-permute-start | bytes 184328 | tf_op jit(solution)/shard_map/weight_qkv/ppermute | solution.py:339
  9.3 8.3 %collective-permute-start.2 = (bf16[40,768]{1,0:T(8,128)(2,1)S(1)}, bf16[40,768]{1,0:T(8,128)(2,1)S(1)}, u32[]{:S(2)}, u32[]{:S(2)}) collective-permute-start(bf16[40,768]{1,0:T(8,128)(2,1)S(1)} %get-tuple-element.178), channel_id=1, source_target_pairs={{0,6},{2,4},{4,2},{6,0},{1,7},{3,5},{5,3},{7,1},{8,14},{10,12},{12... | collective-permute-start | bytes 184328 | tf_op jit(solution)/shard_map/weight_qkv/ppermute | solution.py:339
  10.7 24.6 %collective-permute-start.7 = (bf16[128,1024]{1,0:T(8,128)(2,1)}, bf16[128,1024]{1,0:T(8,128)(2,1)S(1)}, u32[]{:S(2)}, u32[]{:S(2)}) collective-permute-start(bf16[128,1024]{1,0:T(8,128)(2,1)} %bitcast.32), channel_id=1, source_target_pairs={{0,4},{4,0},{1,5},{5,1},{2,6},{6,2},{3,7},{7,3},{8,12},{12,8},{9,1... | collective-permute-start | bytes 786440 | tf_op jit(solution)/shard_map/tokens/ppermute | solution.py:339
  17.7 6.5 %collective-permute-start.8 = (bf16[64,1024]{1,0:T(8,128)(2,1)S(1)}, bf16[64,1024]{1,0:T(8,128)(2,1)S(1)}, u32[]{:S(2)}, u32[]{:S(2)}) collective-permute-start(bf16[64,1024]{1,0:T(8,128)(2,1)S(1)} %get-tuple-element.183), channel_id=1, source_target_pairs={{0,8},{8,0},{1,9},{9,1},{2,10},{10,2},{3,11},{11,3},{4,12},{12,4},... | collective-permute-start | bytes 393224 | tf_op jit(solution)/shard_map/weight_up/ppermute | solution.py:339
  19.3 10.4 %collective-permute-start.6 = (bf16[160,768]{1,0:T(8,128)(2,1)S(1)}, bf16[160,768]{1,0:T(8,128)(2,1)S(1)}, u32[]{:S(2)}, u32[]{:S(2)}) collective-permute-start(bf16[160,768]{1,0:T(8,128)(2,1)S(1)} %pad_maximum_fusion.9), channel_id=1, source_target_pairs={{0,24},{8,16},{16,8},{24,0},{1,25},{9,17},{17,9},{25,1},{2,26},{10... | collective-permute-start | bytes 737288 | tf_op jit(solution)/shard_map/weight_qkv/ppermute | solution.py:339
  20.8 11.4 %collective-permute-start.5 = (bf16[160,768]{1,0:T(8,128)(2,1)S(1)}, bf16[160,768]{1,0:T(8,128)(2,1)S(1)}, u32[]{:S(2)}, u32[]{:S(2)}) collective-permute-start(bf16[160,768]{1,0:T(8,128)(2,1)S(1)} %pad_maximum_fusion.9), channel_id=1, source_target_pairs={{0,16},{16,0},{1,17},{17,1},{2,18},{18,2},{3,19},{19,3},{4,20},{20... | collective-permute-start | bytes 737288 | tf_op jit(solution)/shard_map/weight_qkv/ppermute | solution.py:339
  21.3 10.9 %collective-permute-start.4 = (bf16[160,768]{1,0:T(8,128)(2,1)S(1)}, bf16[160,768]{1,0:T(8,128)(2,1)S(1)}, u32[]{:S(2)}, u32[]{:S(2)}) collective-permute-start(bf16[160,768]{1,0:T(8,128)(2,1)S(1)} %pad_maximum_fusion.9), channel_id=1, source_target_pairs={{0,8},{8,0},{1,9},{9,1},{2,10},{10,2},{3,11},{11,3},{4,12},{12,4},... | collective-permute-start | bytes 737288 | tf_op jit(solution)/shard_map/weight_qkv/ppermute | solution.py:339
  24.2 11.1 %collective-permute-start.10 = (bf16[32,1024]{1,0:T(8,128)(2,1)S(1)}, bf16[32,1024]{1,0:T(8,128)(2,1)S(1)}, u32[]{:S(2)}, u32[]{:S(2)}) collective-permute-start(bf16[32,1024]{1,0:T(8,128)(2,1)S(1)} %get-tuple-element.184), channel_id=1, source_target_pairs={{0,2},{2,0},{1,3},{3,1},{4,6},{6,4},{5,7},{7,5},{8,10},{10,8},{9,1... | collective-permute-start | bytes 196616 | tf_op jit(solution)/shard_map/weight_out/ppermute | solution.py:339
  35.4 17.4 %collective-permute-start.13 = (bf16[128,1024]{1,0:T(8,128)(2,1)S(1)}, bf16[128,1024]{1,0:T(8,128)(2,1)}, u32[]{:S(2)}, u32[]{:S(2)}) collective-permute-start(bf16[128,1024]{1,0:T(8,128)(2,1)S(1)} %pad_maximum_fusion.4), channel_id=1, source_target_pairs={{0,4},{4,0},{1,5},{5,1},{2,6},{6,2},{3,7},{7,3},{8,12},{12,8},{9,1... | collective-permute-start | bytes 786440 | tf_op jit(solution)/shard_map/weight_up/ppermute | solution.py:339
  38.3 11.9 %collective-permute-start.12 = (bf16[128,1024]{1,0:T(8,128)(2,1)S(1)}, bf16[128,1024]{1,0:T(8,128)(2,1)S(1)}, u32[]{:S(2)}, u32[]{:S(2)}) collective-permute-start(bf16[128,1024]{1,0:T(8,128)(2,1)S(1)} %collective-permute-done.7.t2), channel_id=1, source_target_pairs={{0,2},{2,0},{1,3},{3,1},{4,6},{6,4},{5,7},{7,5},{8,10},{10,8},{9,1... | collective-permute-start | bytes 786440 | tf_op jit(solution)/shard_map/tokens/ppermute | solution.py:339
  50.1 8.9 %collective-permute-start.14 = (bf16[64,1024]{1,0:T(8,128)(2,1)S(1)}, bf16[64,1024]{1,0:T(8,128)(2,1)S(1)}, u32[]{:S(2)}, u32[]{:S(2)}) collective-permute-start(bf16[64,1024]{1,0:T(8,128)(2,1)S(1)} %pad_maximum_fusion.11), channel_id=1, source_target_pairs={{0,4},{4,0},{1,5},{5,1},{2,6},{6,2},{3,7},{7,3},{8,12},{12,8},{9,1... | collective-permute-start | bytes 393224 | tf_op jit(solution)/shard_map/weight_out/ppermute | solution.py:339
  59.1 13.4 %collective-permute-start.17 = (bf16[128,1024]{1,0:T(8,128)(2,1)S(1)}, bf16[128,1024]{1,0:T(8,128)(2,1)S(1)}, u32[]{:S(2)}, u32[]{:S(2)}) collective-permute-start(bf16[128,1024]{1,0:T(8,128)(2,1)S(1)} %get-tuple-element.350), channel_id=1, source_target_pairs={{0,8},{8,0},{1,9},{9,1},{2,10},{10,2},{3,11},{11,3},{4,12},{12,4},... | collective-permute-start | bytes 786440 | tf_op jit(solution)/shard_map/weight_out/ppermute | solution.py:339
  60.5 14.0 %collective-permute-start.19 = (bf16[128,1024]{1,0:T(8,128)(2,1)S(1)}, bf16[128,1024]{1,0:T(8,128)(2,1)S(1)}, u32[]{:S(2)}, u32[]{:S(2)}) collective-permute-start(bf16[128,1024]{1,0:T(8,128)(2,1)S(1)} %get-tuple-element.350), channel_id=1, source_target_pairs={{0,24},{8,16},{16,8},{24,0},{1,25},{9,17},{17,9},{25,1},{2,26},{10... | collective-permute-start | bytes 786440 | tf_op jit(solution)/shard_map/weight_out/ppermute | solution.py:339
  62.1 14.8 %collective-permute-start.18 = (bf16[128,1024]{1,0:T(8,128)(2,1)S(1)}, bf16[128,1024]{1,0:T(8,128)(2,1)S(1)}, u32[]{:S(2)}, u32[]{:S(2)}) collective-permute-start(bf16[128,1024]{1,0:T(8,128)(2,1)S(1)} %get-tuple-element.350), channel_id=1, source_target_pairs={{0,16},{16,0},{1,17},{17,1},{2,18},{18,2},{3,19},{19,3},{4,20},{20... | collective-permute-start | bytes 786440 | tf_op jit(solution)/shard_map/weight_out/ppermute | solution.py:339
  62.6 14.3 %collective-permute-start.16 = (bf16[128,1024]{1,0:T(8,128)(2,1)S(1)}, bf16[128,1024]{1,0:T(8,128)(2,1)S(1)}, u32[]{:S(2)}, u32[]{:S(2)}) collective-permute-start(bf16[128,1024]{1,0:T(8,128)(2,1)S(1)} %copy-done.20), channel_id=1, source_target_pairs={{0,4},{4,0},{1,5},{5,1},{2,6},{6,2},{3,7},{7,3},{8,12},{12,8},{9,1... | collective-permute-start | bytes 786440 | tf_op jit(solution)/shard_map/weight_down/ppermute | solution.py:339
  63.7 23.5 %collective-permute-start.23 = (bf16[256,1024]{1,0:T(8,128)(2,1)S(1)}, bf16[256,1024]{1,0:T(8,128)(2,1)S(1)}, u32[]{:S(2)}, u32[]{:S(2)}) collective-permute-start(bf16[256,1024]{1,0:T(8,128)(2,1)S(1)} %pad_maximum_fusion.1), channel_id=1, source_target_pairs={{0,16},{16,0},{1,17},{17,1},{2,18},{18,2},{3,19},{19,3},{4,20},{20... | collective-permute-start | bytes 1572872 | tf_op jit(solution)/shard_map/weight_up/ppermute | solution.py:339
  77.0 10.9 %collective-permute-start.24 = (bf16[512,1024]{1,0:T(8,128)(2,1)S(1)}, bf16[512,1024]{1,0:T(8,128)(2,1)S(1)}, u32[]{:S(2)}, u32[]{:S(2)}) collective-permute-start(bf16[512,1024]{1,0:T(8,128)(2,1)S(1)} %constant_dynamic-update-slice_fusion.3.near), channel_id=1, source_target_pairs={{0,1},{1,0},{2,3},{3,2},{4,5},{5,4},{6,7},{7,6},{8,9},{9,8},{10,11... | collective-permute-start | bytes 3145736 | tf_op jit(solution)/shard_map/weight_out/ppermute | solution.py:339
  77.2 8.0 %collective-permute-start.21 = (bf16[128,256]{1,0:T(8,128)(2,1)S(1)}, bf16[128,256]{1,0:T(8,128)(2,1)S(1)}, u32[]{:S(2)}, u32[]{:S(2)}) collective-permute-start(bf16[128,256]{1,0:T(8,128)(2,1)S(1)} %get-tuple-element.214), channel_id=1, source_target_pairs={{0,4},{4,0},{1,5},{5,1},{2,6},{6,2},{3,7},{7,3},{8,12},{12,8},{9,1... | collective-permute-start | bytes 196616 | tf_op jit(solution)/shard_map/attended/ppermute | solution.py:339
  87.2 14.5 %collective-permute-start.27 = (bf16[512,1024]{1,0:T(8,128)(2,1)S(1)}, bf16[512,1024]{1,0:T(8,128)(2,1)S(1)}, u32[]{:S(2)}, u32[]{:S(2)}) collective-permute-start(bf16[512,1024]{1,0:T(8,128)(2,1)S(1)} %constant_dynamic-update-slice_fusion.9.near), channel_id=1, source_target_pairs={{0,1},{1,0},{2,3},{3,2},{4,5},{5,4},{6,7},{7,6},{8,9},{9,8},{10,11... | collective-permute-start | bytes 3145736 | tf_op jit(solution)/shard_map/weight_up/ppermute | solution.py:339
  87.3 14.4 %collective-permute-start.28 = (bf16[256,1024]{1,0:T(8,128)(2,1)S(1)}, bf16[256,1024]{1,0:T(8,128)(2,1)S(1)}, u32[]{:S(2)}, u32[]{:S(2)}) collective-permute-start(bf16[256,1024]{1,0:T(8,128)(2,1)S(1)} %pad_maximum_fusion.2), channel_id=1, source_target_pairs={{0,16},{16,0},{1,17},{17,1},{2,18},{18,2},{3,19},{19,3},{4,20},{20... | collective-permute-start | bytes 1572872 | tf_op jit(solution)/shard_map/weight_down/ppermute | solution.py:339
  91.4 10.2 %collective-permute-start.26 = (bf16[128,1024]{1,0:T(8,128)(2,1)S(1)}, bf16[128,1024]{1,0:T(8,128)(2,1)S(1)}, u32[]{:S(2)}, u32[]{:S(2)}) collective-permute-start(bf16[128,1024]{1,0:T(8,128)(2,1)S(1)} %get-tuple-element.224.h0), channel_id=1, source_target_pairs={{0,8},{8,0},{1,9},{9,1},{2,10},{10,2},{3,11},{11,3},{4,12},{12,4},... | collective-permute-start | bytes 786440 | tf_op jit(solution)/shard_map/hidden/ppermute | solution.py:339
  92.8 8.9 %collective-permute-start.25 = (bf16[128,1024]{1,0:T(8,128)(2,1)S(1)}, bf16[128,1024]{1,0:T(8,128)(2,1)S(1)}, u32[]{:S(2)}, u32[]{:S(2)}) collective-permute-start(bf16[128,1024]{1,0:T(8,128)(2,1)S(1)} %get-tuple-element.224.h0), channel_id=1, source_target_pairs={{0,2},{2,0},{1,3},{3,1},{4,6},{6,4},{5,7},{7,5},{8,10},{10,8},{9,1... | collective-permute-start | bytes 786440 | tf_op jit(solution)/shard_map/hidden/ppermute | solution.py:339
  118.6 7.1 %collective-permute-start.35 = (bf16[128,1024]{1,0:T(8,128)(2,1)S(1)}, bf16[128,1024]{1,0:T(8,128)(2,1)S(1)}, u32[]{:S(2)}, u32[]{:S(2)}) collective-permute-start(bf16[128,1024]{1,0:T(8,128)(2,1)S(1)} %pad_maximum_fusion.6), channel_id=1, source_target_pairs={{0,8},{8,0},{1,9},{9,1},{2,10},{10,2},{3,11},{11,3},{4,12},{12,4},... | collective-permute-start | bytes 786440 | tf_op jit(solution)/shard_map/ppermute | solution.py:339
  120.6 6.4 %collective-permute-start.33 = (bf16[128,1024]{1,0:T(8,128)(2,1)S(1)}, bf16[128,1024]{1,0:T(8,128)(2,1)S(1)}, u32[]{:S(2)}, u32[]{:S(2)}) collective-permute-start(bf16[128,1024]{1,0:T(8,128)(2,1)S(1)} %pad_maximum_fusion.5), channel_id=1, source_target_pairs={{0,2},{2,0},{1,3},{3,1},{4,6},{6,4},{5,7},{7,5},{8,10},{10,8},{9,1... | collective-permute-start | bytes 786440 | tf_op jit(solution)/shard_map/ppermute | solution.py:339
  128.6 7.5 %collective-permute-start.37 = (bf16[128,1024]{1,0:T(8,128)(2,1)S(1)}, bf16[128,1024]{1,0:T(8,128)(2,1)S(1)}, u32[]{:S(2)}, u32[]{:S(2)}) collective-permute-start(bf16[128,1024]{1,0:T(8,128)(2,1)S(1)} %get-tuple-element.244.g0), channel_id=1, source_target_pairs={{0,8},{8,0},{1,9},{9,1},{2,10},{10,2},{3,11},{11,3},{4,12},{12,4},... | collective-permute-start | bytes 786440 | tf_op jit(solution)/shard_map/grad_down/ppermute | solution.py:339
  129.0 7.8 %collective-permute-start.36 = (bf16[128,1024]{1,0:T(8,128)(2,1)S(1)}, bf16[128,1024]{1,0:T(8,128)(2,1)S(1)}, u32[]{:S(2)}, u32[]{:S(2)}) collective-permute-start(bf16[128,1024]{1,0:T(8,128)(2,1)S(1)} %get-tuple-element.244.g0), channel_id=1, source_target_pairs={{0,2},{2,0},{1,3},{3,1},{4,6},{6,4},{5,7},{7,5},{8,10},{10,8},{9,1... | collective-permute-start | bytes 786440 | tf_op jit(solution)/shard_map/grad_down/ppermute | solution.py:339
  151.6 8.2 %collective-permute-start.44 = (bf16[1024,1024]{1,0:T(8,128)(2,1)}, bf16[1024,1024]{1,0:T(8,128)(2,1)S(1)}, u32[]{:S(2)}, u32[]{:S(2)}) collective-permute-start(bf16[1024,1024]{1,0:T(8,128)(2,1)} %get-tuple-element.253), channel_id=1, source_target_pairs={{0,1},{1,0},{2,3},{3,2},{4,5},{5,4},{6,7},{7,6},{8,9},{9,8},{10,11... | collective-permute-start | bytes 6291464 | tf_op jit(solution)/shard_map/grad_weight_feed/ppermute | solution.py:339
  157.6 8.0 %collective-permute-start.43 = (bf16[128,1024]{1,0:T(8,128)(2,1)S(1)}, bf16[128,1024]{1,0:T(8,128)(2,1)S(1)}, u32[]{:S(2)}, u32[]{:S(2)}) collective-permute-start(bf16[128,1024]{1,0:T(8,128)(2,1)S(1)} %pad_maximum_fusion.8), channel_id=1, source_target_pairs={{0,8},{8,0},{1,9},{9,1},{2,10},{10,2},{3,11},{11,3},{4,12},{12,4},... | collective-permute-start | bytes 786440 | tf_op jit(solution)/shard_map/grad_hidden/ppermute | solution.py:339
  159.2 7.7 %collective-permute-start.41 = (bf16[128,1024]{1,0:T(8,128)(2,1)S(1)}, bf16[128,1024]{1,0:T(8,128)(2,1)S(1)}, u32[]{:S(2)}, u32[]{:S(2)}) collective-permute-start(bf16[128,1024]{1,0:T(8,128)(2,1)S(1)} %pad_maximum_fusion.7), channel_id=1, source_target_pairs={{0,2},{2,0},{1,3},{3,1},{4,6},{6,4},{5,7},{7,5},{8,10},{10,8},{9,1... | collective-permute-start | bytes 786440 | tf_op jit(solution)/shard_map/grad_hidden/ppermute | solution.py:339
  170.0 10.4 %collective-permute-start.45 = (bf16[512,1024]{1,0:T(8,128)(2,1)S(1)}, bf16[512,1024]{1,0:T(8,128)(2,1)S(1)}, u32[]{:S(2)}, u32[]{:S(2)}) collective-permute-start(bf16[512,1024]{1,0:T(8,128)(2,1)S(1)} %get-tuple-element.262), channel_id=1, source_target_pairs={{0,1},{1,0},{2,3},{3,2},{4,5},{5,4},{6,7},{7,6},{8,9},{9,8},{10,11... | collective-permute-start | bytes 3145736 | tf_op jit(solution)/shard_map/grad_weight_out/ppermute | solution.py:339
  170.2 25.6 %collective-permute-start.50 = (bf16[512,1024]{1,0:T(8,128)(2,1)S(1)}, bf16[512,1024]{1,0:T(8,128)(2,1)S(1)}, u32[]{:S(2)}, u32[]{:S(2)}) collective-permute-start(bf16[512,1024]{1,0:T(8,128)(2,1)S(1)} %slice.201), channel_id=1, source_target_pairs={{0,16},{16,0},{1,17},{17,1},{2,18},{18,2},{3,19},{19,3},{4,20},{20... | collective-permute-start | bytes 3145736 | tf_op jit(solution)/shard_map/grad_weight_feed/ppermute | solution.py:339
  172.1 8.3 %collective-permute-start.47 = (bf16[128,256]{1,0:T(8,128)(2,1)S(1)}, bf16[128,256]{1,0:T(8,128)(2,1)S(1)}, u32[]{:S(2)}, u32[]{:S(2)}) collective-permute-start(bf16[128,256]{1,0:T(8,128)(2,1)S(1)} %get-tuple-element.264), channel_id=1, source_target_pairs={{0,4},{4,0},{1,5},{5,1},{2,6},{6,2},{3,7},{7,3},{8,12},{12,8},{9,1... | collective-permute-start | bytes 196616 | tf_op jit(solution)/shard_map/grad_attended/ppermute | solution.py:339
  173.7 6.7 %collective-permute-start.48 = (bf16[128,256]{1,0:T(8,128)(2,1)S(1)}, bf16[128,256]{1,0:T(8,128)(2,1)S(1)}, u32[]{:S(2)}, u32[]{:S(2)}) collective-permute-start(bf16[128,256]{1,0:T(8,128)(2,1)S(1)} %get-tuple-element.265), channel_id=1, source_target_pairs={{0,6},{2,4},{4,2},{6,0},{1,7},{3,5},{5,3},{7,1},{8,14},{10,12},{12... | collective-permute-start | bytes 196616 | tf_op jit(solution)/shard_map/grad_attended/ppermute | solution.py:339
  180.9 15.4 %collective-permute-start.49 = (bf16[256,1024]{1,0:T(8,128)(2,1)S(1)}, bf16[256,1024]{1,0:T(8,128)(2,1)S(1)}, u32[]{:S(2)}, u32[]{:S(2)}) collective-permute-start(bf16[256,1024]{1,0:T(8,128)(2,1)S(1)} %slice.199), channel_id=1, source_target_pairs={{0,8},{8,0},{1,9},{9,1},{2,10},{10,2},{3,11},{11,3},{4,12},{12,4},... | collective-permute-start | bytes 1572872 | tf_op jit(solution)/shard_map/grad_weight_out/ppermute | solution.py:339
  196.6 8.8 %collective-permute-start.52 = (bf16[128,1024]{1,0:T(8,128)(2,1)S(1)}, bf16[128,1024]{1,0:T(8,128)(2,1)S(1)}, u32[]{:S(2)}, u32[]{:S(2)}) collective-permute-start(bf16[128,1024]{1,0:T(8,128)(2,1)S(1)} %slice.203), channel_id=1, source_target_pairs={{0,16},{16,0},{1,17},{17,1},{2,18},{18,2},{3,19},{19,3},{4,20},{20... | collective-permute-start | bytes 786440 | tf_op jit(solution)/shard_map/grad_weight_out/ppermute | solution.py:339
  197.0 15.0 %collective-permute-start.53 = (bf16[128,1024]{1,0:T(8,128)(2,1)S(1)}, bf16[128,1024]{1,0:T(8,128)(2,1)S(1)}, u32[]{:S(2)}, u32[]{:S(2)}) collective-permute-start(bf16[128,1024]{1,0:T(8,128)(2,1)S(1)} %get-tuple-element.336), channel_id=1, source_target_pairs={{0,4},{4,0},{1,5},{5,1},{2,6},{6,2},{3,7},{7,3},{8,12},{12,8},{9,1... | collective-permute-start | bytes 786440 | tf_op jit(solution)/shard_map/grad_weight_up/ppermute | solution.py:339
  212.2 11.7 %collective-permute-start.61 = (bf16[64,1024]{1,0:T(8,128)(2,1)S(1)}, bf16[64,1024]{1,0:T(8,128)(2,1)S(1)}, u32[]{:S(2)}, u32[]{:S(2)}) collective-permute-start(bf16[64,1024]{1,0:T(8,128)(2,1)S(1)} %slice.218), channel_id=1, source_target_pairs={{0,2},{2,0},{1,3},{3,1},{4,6},{6,4},{5,7},{7,5},{8,10},{10,8},{9,1... | collective-permute-start | bytes 393224 | tf_op jit(solution)/shard_map/grad_weight_out/ppermute | solution.py:339
  218.6 9.0 %collective-permute-start.56 = (bf16[160,768]{1,0:T(8,128)(2,1)S(1)}, bf16[160,768]{1,0:T(8,128)(2,1)S(1)}, u32[]{:S(2)}, u32[]{:S(2)}) collective-permute-start(bf16[160,768]{1,0:T(8,128)(2,1)S(1)} %get-tuple-element.337), channel_id=1, source_target_pairs={{0,8},{8,0},{1,9},{9,1},{2,10},{10,2},{3,11},{11,3},{4,12},{12,4},... | collective-permute-start | bytes 737288 | tf_op jit(solution)/shard_map/grad_weight_qkv/ppermute | solution.py:339
  220.3 12.4 %collective-permute-start.58 = (bf16[160,768]{1,0:T(8,128)(2,1)S(1)}, bf16[160,768]{1,0:T(8,128)(2,1)S(1)}, u32[]{:S(2)}, u32[]{:S(2)}) collective-permute-start(bf16[160,768]{1,0:T(8,128)(2,1)S(1)} %get-tuple-element.338), channel_id=1, source_target_pairs={{0,24},{8,16},{16,8},{24,0},{1,25},{9,17},{17,9},{25,1},{2,26},{10... | collective-permute-start | bytes 737288 | tf_op jit(solution)/shard_map/grad_weight_qkv/ppermute | solution.py:339
  221.8 12.2 %collective-permute-start.57 = (bf16[160,768]{1,0:T(8,128)(2,1)S(1)}, bf16[160,768]{1,0:T(8,128)(2,1)S(1)}, u32[]{:S(2)}, u32[]{:S(2)}) collective-permute-start(bf16[160,768]{1,0:T(8,128)(2,1)S(1)} %get-tuple-element.339), channel_id=1, source_target_pairs={{0,16},{16,0},{1,17},{17,1},{2,18},{18,2},{3,19},{19,3},{4,20},{20... | collective-permute-start | bytes 737288 | tf_op jit(solution)/shard_map/grad_weight_qkv/ppermute | solution.py:339
  222.2 11.9 %collective-permute-start.60 = (bf16[64,1024]{1,0:T(8,128)(2,1)S(1)}, bf16[64,1024]{1,0:T(8,128)(2,1)S(1)}, u32[]{:S(2)}, u32[]{:S(2)}) collective-permute-start(bf16[64,1024]{1,0:T(8,128)(2,1)S(1)} %pad_maximum_fusion.12), channel_id=1, source_target_pairs={{0,2},{2,0},{1,3},{3,1},{4,6},{6,4},{5,7},{7,5},{8,10},{10,8},{9,1... | collective-permute-start | bytes 393224 | tf_op jit(solution)/shard_map/grad_weight_up/ppermute | solution.py:339
  223.9 13.1 %collective-permute-start.59 = (bf16[128,1024]{1,0:T(8,128)(2,1)S(1)}, bf16[128,1024]{1,0:T(8,128)(2,1)S(1)}, u32[]{:S(2)}, u32[]{:S(2)}) collective-permute-start(bf16[128,1024]{1,0:T(8,128)(2,1)S(1)} %slice.214), channel_id=1, source_target_pairs={{0,4},{4,0},{1,5},{5,1},{2,6},{6,2},{3,7},{7,3},{8,12},{12,8},{9,1... | collective-permute-start | bytes 786440 | tf_op jit(solution)/shard_map/grad_weight_down/ppermute | solution.py:339
  237.2 6.3 %collective-permute-start.62 = (bf16[32,1024]{1,0:T(8,128)(2,1)S(1)}, bf16[32,1024]{1,0:T(8,128)(2,1)S(1)}, u32[]{:S(2)}, u32[]{:S(2)}) collective-permute-start(bf16[32,1024]{1,0:T(8,128)(2,1)S(1)} %slice.220), channel_id=1, source_target_pairs={{0,4},{4,0},{1,5},{5,1},{2,6},{6,2},{3,7},{7,3},{8,12},{12,8},{9,1... | collective-permute-start | bytes 196616 | tf_op jit(solution)/shard_map/grad_weight_out/ppermute | solution.py:339
  256.3 9.1 %collective-permute-start.74 = (bf16[128,1024]{1,0:T(8,128)(2,1)S(1)}, bf16[128,1024]{1,0:T(8,128)(2,1)S(1)}, u32[]{:S(2)}, u32[]{:S(2)}) collective-permute-start(bf16[128,1024]{1,0:T(8,128)(2,1)S(1)} %get-tuple-element.316), channel_id=1, source_target_pairs={{0,2},{2,0},{1,3},{3,1},{4,6},{6,4},{5,7},{7,5},{8,10},{10,8},{9,1... | collective-permute-start | bytes 786440 | tf_op jit(solution)/shard_map/grad_tokens/ppermute | solution.py:339
  261.6 14.5 %collective-permute-start.70 = (bf16[128,1024]{1,0:T(8,128)(2,1)}, bf16[128,1024]{1,0:T(8,128)(2,1)S(1)}, u32[]{:S(2)}, u32[]{:S(2)}) collective-permute-start(bf16[128,1024]{1,0:T(8,128)(2,1)} %get-tuple-element.313), channel_id=1, source_target_pairs={{0,2},{2,0},{1,3},{3,1},{4,6},{6,4},{5,7},{7,5},{8,10},{10,8},{9,1... | collective-permute-start | bytes 786440 | tf_op jit(solution)/shard_map/grad_tokens/ppermute | solution.py:339
  265.5 12.1 %collective-permute-start.75 = (bf16[128,1024]{1,0:T(8,128)(2,1)S(1)}, bf16[128,1024]{1,0:T(8,128)(2,1)S(1)}, u32[]{:S(2)}, u32[]{:S(2)}) collective-permute-start(bf16[128,1024]{1,0:T(8,128)(2,1)S(1)} %add_convert_fusion.5), channel_id=1, source_target_pairs={{0,4},{4,0},{1,5},{5,1},{2,6},{6,2},{3,7},{7,3},{8,12},{12,8},{9,1... | collective-permute-start | bytes 786440 | tf_op jit(solution)/shard_map/grad_tokens/ppermute | solution.py:339
  (82 other events, 1009.7 us)
where the time goes:
time: 283 us; the launch traced here: 280 us
  waiting for transfers between devices  112 us (40%)
  starting transfers between devices  87.3 us (31%)
  Pallas kernels  51.7 us (18%)
  local copies, waits for them, and re-layouts  18.2 us (6%)
  other arithmetic  6.62 us (2%)
  between operations  4.27 us (2%)
    ppermute x76, waiting for transfers between devices, swap(): return lax.ppermute(value, axes, [(i, i ^ last) for i in range(last + 1)])  112 us
    ppermute x76, starting transfers between devices, swap(): return lax.ppermute(value, axes, [(i, i ^ last) for i in range(last + 1)])  87.3 us
    pallas_call x18, Pallas kernels, call(): pl.pallas_call(kernel, name=getattr(kernel, 'func', kernel).__name__, in_...  43.8 us
    unnamed x116, local copies, waits for them, and re-layouts  9.96 us
  transfers between devices with their start and end apart: 76, of which 47 were waited for; matrix products, arithmetic and copies ran while one was open for 5% of the time, Pallas kernels for 11%

commit v1 on v0

--- a/solution.py
+++ b/solution.py
@@ -496,7 +496,8 @@
     for copy in copies[2:]:
         copy.wait()
     projected = dot(rows[...], full_ref[...])
-    q_ref[...] = (projected[:, :size] + bias[0:1, :]).astype(LOW)
+    query = (projected[:, :size] + bias[0:1, :]).astype(LOW)
+    q_ref[...] = (query.astype(WIDE) * SCORE_SCALE).astype(LOW)
     kv_ref[:, :size] = projected[:, size : 2 * size].astype(LOW)
     kv_ref[:, size:] = (projected[:, 2 * size :] + bias[1:2, :]).astype(LOW)
 
@@ -523,14 +524,13 @@
             halves = []
             for head in range(2):
                 query = jnp.where(head_mask(queries.shape, 1, head), queries, zero)
-                scores = against(keys, query) * SCORE_SCALE
+                scores = against(keys, query)
                 top = jnp.max(scores, axis=0, keepdims=True)
                 weights = jnp.exp(scores - top)
                 total = jnp.sum(weights, axis=0, keepdims=True)
                 at_head = 2 * group + head
                 lse_ref[at_head : at_head + 1, rows] = top + jnp.log(total)
-                probs = (weights * (1.0 / total)).astype(LOW)
-                halves.append(dot(values_t, probs))
+                halves.append(dot(values_t, weights.astype(LOW)) * (1.0 / total))
             mask = head_mask(halves[0].shape, 0, 0)
             result = jnp.where(mask, halves[0], halves[1]).T.astype(LOW)
             outs[2 * piece][:, cols] = result[:count]
@@ -565,7 +565,7 @@
                 query = jnp.where(mask, queries, zero)
                 dout = jnp.where(mask, douts, zero)
                 at_head = 2 * group + head
-                scores = against(keys, query) * SCORE_SCALE
+                scores = against(keys, query)
                 probs = jnp.exp(scores - lse_ref[at_head : at_head + 1, rows])
                 grad_probs = against(values, dout)
                 delta = jnp.sum(probs * grad_probs, axis=0, keepdims=True)
@@ -582,7 +582,6 @@
             bias_query += jnp.sum(dq.astype(WIDE), axis=0, keepdims=True)
             sum_keys += dot(jnp.concatenate(all_grads, axis=1), jnp.concatenate(all_query, axis=0))
             sum_values += dot(jnp.concatenate(all_probs, axis=1), jnp.concatenate(all_dout, axis=0))
-        sum_keys = sum_keys * SCORE_SCALE
         half = length // 2
         near_ref[:, cols] = sum_keys[:half]
         far_ref[:, cols] = sum_keys[half:].astype(LOW)
@@ -798,10 +797,14 @@
     result[...] = jnp.broadcast_to(total, result.shape)
 
 
-def update_kernel(plans, bits, factor, *refs):
+def update_kernel(
+    plans, bits, t0, t1, t2, t3, small_grad, small_weight, small_moment, small_second, *refs
+):
     count = len(plans)
     total = sum(plan[2] for plan in plans)
     sources, refs = refs[:total], refs[total:]
+    norm_ref, *small_results = refs[6 * count : 6 * count + 4]
+    refs = refs[: 6 * count] + refs[6 * count + 4 :]
     grads, refs = refs[6 * count : 6 * count + total], refs[: 6 * count] + refs[6 * count + total :]
     brought = refs[-3]
     fetches = [
@@ -820,6 +823,19 @@
     ]
     for load in loads:
         load.start()
+    norm = jnp.sqrt((t0[...] + t1[...]) + (t2[...] + t3[...]))
+    norm_ref[...] = norm
+    factor = jnp.minimum(1.0, CLIP_LIMIT / (norm[0:1, 0:1] + 1e-06))
+    values = adam_update(
+        small_weight[...],
+        small_grad[...] * factor,
+        small_moment[...],
+        small_second[...],
+        RATE_SMALL,
+        0.0,
+    )
+    for ref, value in zip(small_results, values):
+        ref[...] = value
     _, z, _ = indices(bits)
     first = 0
     for index, (rate, places, pieces) in enumerate(plans):
@@ -830,7 +846,7 @@
         for r in range(pieces):
             piece = grads[first + r]
             for source, target in places(bits, z, r, piece.shape[1]):
-                grad = piece[:own, source].astype(WIDE) * factor[0]
+                grad = piece[:own, source].astype(WIDE) * factor
                 weight, moment, second = (ref[:, target] for ref in held[mine])
                 values = adam_update(weight, grad, moment, second, rate, WEIGHT_DECAY)
                 for ref, value in zip(made[mine], values):
@@ -1220,28 +1236,23 @@
     tile = width // 8
     lanes = 3 * part // tile
     small_tile = small_tile[:2].reshape(2 * lanes, tile)[:columns]
-    owned_small = lax.dynamic_slice_in_dim(small_tile, (2 * il + ic) * own, own, axis=1).T
-    def sum_square(value, a, b):
-        terms = exchange([value] * 4, a, b)
+    owned_small = lax.dynamic_slice_in_dim(small_tile, (2 * il + ic) * own, own, axis=1)
+    def four(terms):
         return (terms[0] + terms[1]) + (terms[2] + terms[3])
 
     with jax.named_scope("norm"):
         total = total + swap(total, ("c",))
-        total = sum_square(total, "h", "l")
+        total = four(exchange([total] * 4, "h", "l"))
     with jax.named_scope("grad_tokens"):
-        far_l = send(parts[3], ("l",), start=(total,))
-        from_l = send(parts[1], ("l",), start=(total,))
+        far_l = send(parts[3], ("l",), start=late, use=(qkv_pieces[1],))
         to_h = (parts[2].astype(WIDE) + far_l.astype(WIDE)).astype(LOW)
-    with jax.named_scope("norm"):
-        total = sum_square(total, "y", "x")
     total, to_h = tie(total, to_h)
     with jax.named_scope("grad_tokens"):
         from_h = swap(to_h, ("h",))
+        from_l = send(parts[1], ("l",), start=(total,))
+    with jax.named_scope("norm"):
+        totals = exchange([total] * 4, "y", "x")
     grad_rows = parts[0] + from_l.astype(WIDE) + from_h.astype(WIDE)
-    grad_norm = jnp.sqrt(total[0, 0])
-    factor = jnp.minimum(1.0, CLIP_LIMIT / (grad_norm + 1e-06))
-    held = jnp.full((1,), factor)
-
     states = [
         (weight_down, moment_down, second_down),
         (weight_out, moment_out, second_out),
@@ -1259,24 +1270,35 @@
     results = pl.pallas_call(
         functools.partial(update_kernel, plans),
         name="update_kernel",
-        in_specs=[pl.BlockSpec(memory_space=pltpu.SMEM)] * 2
-        + [pl.BlockSpec(memory_space=pltpu.HBM)] * (len(grads) + 12),
-        out_specs=[pl.BlockSpec(memory_space=pltpu.HBM)] * 12,
-        out_shape=[jax.ShapeDtypeStruct(array.shape, WIDE) for array in flat],
+        in_specs=[pl.BlockSpec(memory_space=pltpu.SMEM)]
+        + [vmem] * 8
+        + [hbm] * (len(grads) + 12),
+        out_specs=[hbm] * 12 + [vmem] * 4,
+        out_shape=[jax.ShapeDtypeStruct(array.shape, WIDE) for array in flat]
+        + [jax.ShapeDtypeStruct((8, 128), WIDE)]
+        + [jax.ShapeDtypeStruct((columns, own), WIDE)] * 3,
         scratch_shapes=[pltpu.VMEM(grad.shape, grad.dtype) for grad in grads]
         + [pltpu.VMEM(array.shape, WIDE) for array in flat * 2]
         + [pltpu.SemaphoreType.DMA((len(grads),))]
         + [pltpu.SemaphoreType.DMA((12,))] * 2,
         compiler_params=pltpu.CompilerParams(vmem_limit_bytes=60 * 2**20),
         cost_estimate=pl.CostEstimate(flops=1, bytes_accessed=1, transcendentals=0),
-    )(bits, held, *grads, *flat)
+    )(
+        bits,
+        *totals,
+        owned_small,
+        small_params.T,
+        moment_small.T,
+        second_small.T,
+        *grads,
+        *flat,
+    )
     new_down, new_moment_down, new_second_down = results[0:3]
     new_out, new_moment_out, new_second_out = results[3:6]
     new_up, new_moment_up, new_second_up = results[6:9]
     new_qkv, new_moment_qkv, new_second_qkv = results[9:12]
-    new_small, new_moment_small, new_second_small = adam_update(
-        small_params, owned_small * factor, moment_small, second_small, RATE_SMALL, 0.0
-    )
+    grad_norm = results[12][0, 0]
+    new_small, new_moment_small, new_second_small = (value.T for value in results[13:16])
     return (
         output[None],
         grad_rows[None],

time: 283 us -> 278 us (0.982)
    unnamed x116 -> x118, local copies, waits for them, and re-layouts: 9.96 us -> 10.5 us
  transfers between devices with their start and end apart: 76 -> 76, of which waited for: 47 -> 44; matrix products, arithmetic and copies ran while one was open for 5% -> 5% of each run, Pallas kernels for 11% -> 12%
where the time goes in v1:
time: 278 us; the launch traced here: 275 us
  waiting for transfers between devices  110 us (40%)
  starting transfers between devices  85 us (31%)
  Pallas kernels  51.7 us (19%)
  local copies, waits for them, and re-layouts  20 us (7%)
  other arithmetic  5.69 us (2%)
    ppermute x76, waiting for transfers between devices, swap(): return lax.ppermute(value, axes, [(i, i ^ last) for i in range(last + 1)])  110 us
    ppermute x76, starting transfers between devices, swap(): return lax.ppermute(value, axes, [(i, i ^ last) for i in range(last + 1)])  85 us
    pallas_call x18, Pallas kernels, call(): pl.pallas_call(kernel, name=getattr(kernel, 'func', kernel).__name__, in_...  43.1 us
    unnamed x118, local copies, waits for them, and re-layouts  10.5 us
    pallas_call x1, Pallas kernels, on_square(): pl.pallas_call(functools.partial(update_kernel, plans), name='update_kern...  6 us
  transfers between devices with their start and end apart: 76, of which 44 were waited for; matrix products, arithmetic and copies ran while one was open for 5% of the time, Pallas kernels for 12%

profile of v1, /device:TPU:0, one launch (start us, length us, event | category | flops | bytes accessed | tf_op | source)
XLA Modules:
  0.0 274.7 jit_solution(4451720094140163315)
XLA Ops:
  0.7 3.1 %collective-permute-start.3 = (bf16[128,1024]{1,0:T(8,128)(2,1)}, bf16[128,1024]{1,0:T(8,128)(2,1)S(1)}, u32[]{:S(2)}, u32[]{:S(2)}) collective-permute-start(bf16[128,1024]{1,0:T(8,128)(2,1)} %bitcast.28), channel_id=1, source_target_pairs={{0,2},{2,0},{1,3},{3,1},{4,6},{6,4},{5,7},{7,5},{8,10},{10,8},{9,1... | collective-permute-start | bytes 786440 | tf_op jit(solution)/shard_map/tokens/ppermute | solution.py:339
  6.3 3.0 %collective-permute-start.1 = (bf16[40,768]{1,0:T(8,128)(2,1)S(1)}, bf16[40,768]{1,0:T(8,128)(2,1)S(1)}, u32[]{:S(2)}, u32[]{:S(2)}) collective-permute-start(bf16[40,768]{1,0:T(8,128)(2,1)S(1)} %get-tuple-element.182), channel_id=1, source_target_pairs={{0,4},{4,0},{1,5},{5,1},{2,6},{6,2},{3,7},{7,3},{8,12},{12,8},{9,1... | collective-permute-start | bytes 184328 | tf_op jit(solution)/shard_map/weight_qkv/ppermute | solution.py:339
  10.7 1.7 collective-permute-start.7
  24.2 4.4 %collective-permute-start.10 = (bf16[32,1024]{1,0:T(8,128)(2,1)S(1)}, bf16[32,1024]{1,0:T(8,128)(2,1)S(1)}, u32[]{:S(2)}, u32[]{:S(2)}) collective-permute-start(bf16[32,1024]{1,0:T(8,128)(2,1)S(1)} %get-tuple-element.189), channel_id=1, source_target_pairs={{0,2},{2,0},{1,3},{3,1},{4,6},{6,4},{5,7},{7,5},{8,10},{10,8},{9,1... | collective-permute-start | bytes 196616 | tf_op jit(solution)/shard_map/weight_out/ppermute | solution.py:339
  29.7 2.5 collective-permute-start.9
  32.3 2.9 %collective-permute-done.9 = bf16[64,1024]{1,0:T(8,128)(2,1)S(1)} collective-permute-done((bf16[64,1024]{1,0:T(8,128)(2,1)S(1)}, bf16[64,1024]{1,0:T(8,128)(2,1)S(1)}, u32[]{:S(2)}, u32[]{:S(2)}) %collective-permute-start.9) | collective-permute-done | bytes 131104 | tf_op jit(solution)/shard_map/weight_up/ppermute | solution.py:339
  35.4 2.9 %collective-permute-start.13 = (bf16[128,1024]{1,0:T(8,128)(2,1)S(1)}, bf16[128,1024]{1,0:T(8,128)(2,1)}, u32[]{:S(2)}, u32[]{:S(2)}) collective-permute-start(bf16[128,1024]{1,0:T(8,128)(2,1)S(1)} %pad_maximum_fusion.4), channel_id=1, source_target_pairs={{0,4},{4,0},{1,5},{5,1},{2,6},{6,2},{3,7},{7,3},{8,12},{12,8},{9,1... | collective-permute-start | bytes 786440 | tf_op jit(solution)/shard_map/weight_up/ppermute | solution.py:339
  42.9 1.7 copy.44
  45.6 4.5 %collective-permute-done.12.t3 = bf16[128,1024]{1,0:T(8,128)(2,1)S(1)} collective-permute-done((bf16[128,1024]{1,0:T(8,128)(2,1)S(1)}, bf16[128,1024]{1,0:T(8,128)(2,1)S(1)}, u32[]{:S(2)}, u32[]{:S(2)}) %collective-permute-start.12) | collective-permute-done | bytes 262176 | tf_op jit(solution)/shard_map/tokens/ppermute | solution.py:339
  50.1 2.7 collective-permute-start.14
  55.0 2.6 project_kernel.1
  65.2 6.5 %forward_kernel.1 = (bf16[128,256]{1,0:T(8,128)(2,1)S(1)}, bf16[128,256]{1,0:T(8,128)(2,1)S(1)}, bf16[128,256]{1,0:T(8,128)(2,1)S(1)}, bf16[128,256]{1,0:T(8,128)(2,1)S(1)}, f32[4,512]{1,0:T(4,128)S(1)}) custom-call(s32[5]{0:T(128)S(1)} %stack.23.bits, bf16[512,256]{1,0:T(8,128)(2,1)S(1)} %get-tuple-element.205.q_ref, ...), custom_call_target="tpu_custom_call" | custom-call | flops 1 | bytes 1 | tf_op jit(solution)/shard_map/forward_kernel/pallas_call | solution.py:389
  71.7 2.8 %collective-permute-done.19 = bf16[128,1024]{1,0:T(8,128)(2,1)S(1)} collective-permute-done((bf16[128,1024]{1,0:T(8,128)(2,1)S(1)}, bf16[128,1024]{1,0:T(8,128)(2,1)S(1)}, u32[]{:S(2)}, u32[]{:S(2)}) %collective-permute-start.19) | collective-permute-done | bytes 262176 | tf_op jit(solution)/shard_map/weight_out/ppermute | solution.py:339
  74.5 2.4 collective-permute-done.18
  77.2 2.8 %collective-permute-start.21 = (bf16[128,256]{1,0:T(8,128)(2,1)S(1)}, bf16[128,256]{1,0:T(8,128)(2,1)S(1)}, u32[]{:S(2)}, u32[]{:S(2)}) collective-permute-start(bf16[128,256]{1,0:T(8,128)(2,1)S(1)} %get-tuple-element.219), channel_id=1, source_target_pairs={{0,4},{4,0},{1,5},{5,1},{2,6},{6,2},{3,7},{7,3},{8,12},{12,8},{9,1... | collective-permute-start | bytes 196616 | tf_op jit(solution)/shard_map/attended/ppermute | solution.py:339
  82.7 2.4 collective-permute-done.21.a2
  93.2 8.5 %collective-permute-done.28 = bf16[256,1024]{1,0:T(8,128)(2,1)S(1)} collective-permute-done((bf16[256,1024]{1,0:T(8,128)(2,1)S(1)}, bf16[256,1024]{1,0:T(8,128)(2,1)S(1)}, u32[]{:S(2)}, u32[]{:S(2)}) %collective-permute-start.28) | collective-permute-done | bytes 524320 | tf_op jit(solution)/shard_map/weight_down/ppermute | solution.py:339
  105.2 2.6 collective-permute-done.29.h3
  107.9 2.5 feed_up_kernel.1
  111.4 1.8 feed_down_kernel.1
  113.2 1.8 collective-permute-start.34
  115.6 2.7 collective-permute-done.34
  120.9 4.8 %collective-permute-done.35.from_a = bf16[128,1024]{1,0:T(8,128)(2,1)S(1)} collective-permute-done((bf16[128,1024]{1,0:T(8,128)(2,1)S(1)}, bf16[128,1024]{1,0:T(8,128)(2,1)S(1)}, u32[]{:S(2)}, u32[]{:S(2)}) %collective-permute-start.35) | collective-permute-done | bytes 262176 | tf_op jit(solution)/shard_map/ppermute | solution.py:339
  130.3 6.3 %collective-permute-done.37.g2 = bf16[128,1024]{1,0:T(8,128)(2,1)S(1)} collective-permute-done((bf16[128,1024]{1,0:T(8,128)(2,1)S(1)}, bf16[128,1024]{1,0:T(8,128)(2,1)S(1)}, u32[]{:S(2)}, u32[]{:S(2)}) %collective-permute-start.37) | collective-permute-done | bytes 262176 | tf_op jit(solution)/shard_map/grad_down/ppermute | solution.py:339
  138.3 3.3 %collective-permute-done.38.g3 = bf16[64,1024]{1,0:T(8,128)(2,1)S(1)} collective-permute-done((bf16[64,1024]{1,0:T(8,128)(2,1)S(1)}, bf16[64,1024]{1,0:T(8,128)(2,1)S(1)}, u32[]{:S(2)}, u32[]{:S(2)}) %collective-permute-start.38) | collective-permute-done | bytes 131104 | tf_op jit(solution)/shard_map/grad_down/ppermute | solution.py:339
  142.1 4.7 %feed_back_kernel.1 = (bf16[512,1024]{1,0:T(8,128)(2,1)S(1)}, f32[8,1024]{1,0:T(8,128)S(1)}, f32[128,1024]{1,0:T(8,128)S(1)}, f32[128,1024]{1,0:T(8,128)S(1)}, f...) custom-call(s32[5]{0:T(128)S(1)} %stack.23.bits, ...), custom_call_target="tpu_custom_call" | custom-call | flops 1 | bytes 1 | tf_op jit(solution)/shard_map/feed_back_kernel/pallas_call | solution.py:389
  146.8 5.1 %feed_grad_kernel.1 = (bf16[1024,1024]{1,0:T(8,128)(2,1)}, bf16[1024,1024]{1,0:T(8,128)(2,1)}) custom-call(s32[5]{0:T(128)S(1)} %stack.23.bits, bf16[512,1024]{1,0:T(8,128)(2,1)S(1)} %get-tuple-element.240.act, bf16[128,1024]{1,0:T(8,128)(2,1)S(1)} %get-tuple-element.249.g0, bf16[128,1024]{1,0:T(8,128)(2,1)S(1)} %collective-permute-done.36.g1, ...), custom_call_target="tpu_custom_call" | custom-call | flops 1 | bytes 1 | tf_op jit(solution)/shard_map/feed_grad_kernel/pallas_call | solution.py:389
  151.8 1.7 collective-permute-start.42
  153.7 4.0 %collective-permute-done.42 = bf16[64,1024]{1,0:T(8,128)(2,1)S(1)} collective-permute-done((bf16[64,1024]{1,0:T(8,128)(2,1)S(1)}, bf16[64,1024]{1,0:T(8,128)(2,1)S(1)}, u32[]{:S(2)}, u32[]{:S(2)}) %collective-permute-start.42) | collective-permute-done | bytes 131104 | tf_op jit(solution)/shard_map/grad_hidden/ppermute | solution.py:339
  160.8 5.0 %collective-permute-done.43.from_a = bf16[128,1024]{1,0:T(8,128)(2,1)S(1)} collective-permute-done((bf16[128,1024]{1,0:T(8,128)(2,1)S(1)}, bf16[128,1024]{1,0:T(8,128)(2,1)S(1)}, u32[]{:S(2)}, u32[]{:S(2)}) %collective-permute-start.43) | collective-permute-done | bytes 262176 | tf_op jit(solution)/shard_map/grad_hidden/ppermute | solution.py:339
  170.9 1.7 collective-permute-start.46
  175.3 5.5 %collective-permute-done.47.d2 = bf16[128,256]{1,0:T(8,128)(2,1)S(1)} collective-permute-done((bf16[128,256]{1,0:T(8,128)(2,1)S(1)}, bf16[128,256]{1,0:T(8,128)(2,1)S(1)}, u32[]{:S(2)}, u32[]{:S(2)}) %collective-permute-start.47) | collective-permute-done | bytes 65568 | tf_op jit(solution)/shard_map/grad_attended/ppermute | solution.py:339
  181.8 8.6 %backward_kernel.1 = (bf16[512,256]{1,0:T(8,128)(2,1)S(1)}, f32[512,512]{1,0:T(8,128)S(1)}, bf16[512,512]{1,0:T(8,128)(2,1)S(1)}, f32[8,256]{1,0:T(8,128)S(1)}) custom-call(s32[5]{0:T(128)S(1)} %stack.23.bits, bf16[512,256]{1,0:T(8,128)(2,1)S(1)} %copy-done.18, bf16[512,512]{1,0:T(8,128)(2,1)S(1)} %get-tuple-element.203.near, ...), custom_call_target="tpu_custom_call" | custom-call | flops 1 | bytes 1 | tf_op jit(solution)/shard_map/backward_kernel/pallas_call | solution.py:389
  190.5 5.5 %collective-permute-done.50 = bf16[512,1024]{1,0:T(8,128)(2,1)S(1)} collective-permute-done((bf16[512,1024]{1,0:T(8,128)(2,1)S(1)}, bf16[512,1024]{1,0:T(8,128)(2,1)S(1)}, u32[]{:S(2)}, u32[]{:S(2)}) %collective-permute-start.50) | collective-permute-done | bytes 1048608 | tf_op jit(solution)/shard_map/grad_weight_feed/ppermute | solution.py:339
  197.3 2.4 collective-permute-start.53
  199.9 1.8 qkv_grad_kernel.1
  201.7 3.8 %collective-permute-done.52 = bf16[128,1024]{1,0:T(8,128)(2,1)S(1)} collective-permute-done((bf16[128,1024]{1,0:T(8,128)(2,1)S(1)}, bf16[128,1024]{1,0:T(8,128)(2,1)S(1)}, u32[]{:S(2)}, u32[]{:S(2)}) %collective-permute-start.52) | collective-permute-done | bytes 262176 | tf_op jit(solution)/shard_map/grad_weight_out/ppermute | solution.py:339
  205.5 6.8 %collective-permute-done.53 = bf16[128,1024]{1,0:T(8,128)(2,1)S(1)} collective-permute-done((bf16[128,1024]{1,0:T(8,128)(2,1)S(1)}, bf16[128,1024]{1,0:T(8,128)(2,1)S(1)}, u32[]{:S(2)}, u32[]{:S(2)}) %collective-permute-start.53) | collective-permute-done | bytes 262176 | tf_op jit(solution)/shard_map/grad_weight_up/ppermute | solution.py:339
  214.0 4.5 %collective-permute-done.55 = bf16[64,1024]{1,0:T(8,128)(2,1)S(1)} collective-permute-done((bf16[64,1024]{1,0:T(8,128)(2,1)S(1)}, bf16[64,1024]{1,0:T(8,128)(2,1)S(1)}, u32[]{:S(2)}, u32[]{:S(2)}) %collective-permute-start.55) | collective-permute-done | bytes 131104 | tf_op jit(solution)/shard_map/grad_weight_up/ppermute | solution.py:339
  222.5 1.7 collective-permute-start.60
  225.7 2.2 rows_grad_kernel.1
  227.9 5.0 %collective-permute-done.58 = bf16[160,768]{1,0:T(8,128)(2,1)S(1)} collective-permute-done((bf16[160,768]{1,0:T(8,128)(2,1)S(1)}, bf16[160,768]{1,0:T(8,128)(2,1)S(1)}, u32[]{:S(2)}, u32[]{:S(2)}) %collective-permute-start.58) | collective-permute-done | bytes 245792 | tf_op jit(solution)/shard_map/grad_weight_qkv/ppermute | solution.py:339
  234.2 3.1 %collective-permute-done.59 = bf16[128,1024]{1,0:T(8,128)(2,1)S(1)} collective-permute-done((bf16[128,1024]{1,0:T(8,128)(2,1)S(1)}, bf16[128,1024]{1,0:T(8,128)(2,1)S(1)}, u32[]{:S(2)}, u32[]{:S(2)}) %collective-permute-start.59) | collective-permute-done | bytes 262176 | tf_op jit(solution)/shard_map/grad_weight_down/ppermute | solution.py:339
  237.6 3.1 %collective-permute-start.63 = (bf16[40,768]{1,0:T(8,128)(2,1)S(1)}, bf16[40,768]{1,0:T(8,128)(2,1)S(1)}, u32[]{:S(2)}, u32[]{:S(2)}) collective-permute-start(bf16[40,768]{1,0:T(8,128)(2,1)S(1)} %get-tuple-element.353), channel_id=1, source_target_pairs={{0,2},{2,0},{1,3},{3,1},{4,6},{6,4},{5,7},{7,5},{8,10},{10,8},{9,1... | collective-permute-start | bytes 184328 | tf_op jit(solution)/shard_map/grad_weight_qkv/ppermute | solution.py:339
  242.3 2.9 %collective-permute-start.70 = (bf16[128,1024]{1,0:T(8,128)(2,1)S(1)}, bf16[128,1024]{1,0:T(8,128)(2,1)S(1)}, u32[]{:S(2)}, u32[]{:S(2)}) collective-permute-start(bf16[128,1024]{1,0:T(8,128)(2,1)S(1)} %get-tuple-element.320), channel_id=1, source_target_pairs={{0,2},{2,0},{1,3},{3,1},{4,6},{6,4},{5,7},{7,5},{8,10},{10,8},{9,1... | collective-permute-start | bytes 786440 | tf_op jit(solution)/shard_map/grad_tokens/ppermute | solution.py:339
  245.3 2.4 collective-permute-done.65.p3.refs_9_
  250.0 2.3 collective-permute-start.69
  266.1 6.0 %update_kernel.1 = (f32[128,1024]{1,0:T(8,128)}, f32[128,1024]{1,0:T(8,128)}, f32[128,1024]{1,0:T(8,128)}, f32[32,1024]{1,0:T(8,128)}, f32[32,1024]{1,0:T(8,128)...) custom-call(s32[5]{0:T(128)} %copy-done.45, ...), custom_call_target="tpu_custom_call" | custom-call | flops 1 | bytes 1 | tf_op jit(solution)/shard_map/update_kernel/pallas_call | solution.py:1270
  (326 shorter events, 99.3 us)
Async XLA Ops:
  0.7 17.0 %collective-permute-start.3 = (bf16[128,1024]{1,0:T(8,128)(2,1)}, bf16[128,1024]{1,0:T(8,128)(2,1)S(1)}, u32[]{:S(2)}, u32[]{:S(2)}) collective-permute-start(bf16[128,1024]{1,0:T(8,128)(2,1)} %bitcast.28), channel_id=1, source_target_pairs={{0,2},{2,0},{1,3},{3,1},{4,6},{6,4},{5,7},{7,5},{8,10},{10,8},{9,1... | collective-permute-start | bytes 786440 | tf_op jit(solution)/shard_map/tokens/ppermute | solution.py:339
  6.2 9.8 %collective-permute-start = (bf16[40,768]{1,0:T(8,128)(2,1)S(1)}, bf16[40,768]{1,0:T(8,128)(2,1)S(1)}, u32[]{:S(2)}, u32[]{:S(2)}) collective-permute-start(bf16[40,768]{1,0:T(8,128)(2,1)S(1)} %get-tuple-element.181), channel_id=1, source_target_pairs={{0,2},{2,0},{1,3},{3,1},{4,6},{6,4},{5,7},{7,5},{8,10},{10,8},{9,1... | collective-permute-start | bytes 184328 | tf_op jit(solution)/shard_map/weight_qkv/ppermute | solution.py:339
  6.3 9.7 %collective-permute-start.1 = (bf16[40,768]{1,0:T(8,128)(2,1)S(1)}, bf16[40,768]{1,0:T(8,128)(2,1)S(1)}, u32[]{:S(2)}, u32[]{:S(2)}) collective-permute-start(bf16[40,768]{1,0:T(8,128)(2,1)S(1)} %get-tuple-element.182), channel_id=1, source_target_pairs={{0,4},{4,0},{1,5},{5,1},{2,6},{6,2},{3,7},{7,3},{8,12},{12,8},{9,1... | collective-permute-start | bytes 184328 | tf_op jit(solution)/shard_map/weight_qkv/ppermute | solution.py:339
  9.3 8.3 %collective-permute-start.2 = (bf16[40,768]{1,0:T(8,128)(2,1)S(1)}, bf16[40,768]{1,0:T(8,128)(2,1)S(1)}, u32[]{:S(2)}, u32[]{:S(2)}) collective-permute-start(bf16[40,768]{1,0:T(8,128)(2,1)S(1)} %get-tuple-element.183), channel_id=1, source_target_pairs={{0,6},{2,4},{4,2},{6,0},{1,7},{3,5},{5,3},{7,1},{8,14},{10,12},{12... | collective-permute-start | bytes 184328 | tf_op jit(solution)/shard_map/weight_qkv/ppermute | solution.py:339
  10.7 24.6 %collective-permute-start.7 = (bf16[128,1024]{1,0:T(8,128)(2,1)}, bf16[128,1024]{1,0:T(8,128)(2,1)S(1)}, u32[]{:S(2)}, u32[]{:S(2)}) collective-permute-start(bf16[128,1024]{1,0:T(8,128)(2,1)} %bitcast.29), channel_id=1, source_target_pairs={{0,4},{4,0},{1,5},{5,1},{2,6},{6,2},{3,7},{7,3},{8,12},{12,8},{9,1... | collective-permute-start | bytes 786440 | tf_op jit(solution)/shard_map/tokens/ppermute | solution.py:339
  19.3 10.4 %collective-permute-start.6 = (bf16[160,768]{1,0:T(8,128)(2,1)S(1)}, bf16[160,768]{1,0:T(8,128)(2,1)S(1)}, u32[]{:S(2)}, u32[]{:S(2)}) collective-permute-start(bf16[160,768]{1,0:T(8,128)(2,1)S(1)} %pad_maximum_fusion.9), channel_id=1, source_target_pairs={{0,24},{8,16},{16,8},{24,0},{1,25},{9,17},{17,9},{25,1},{2,26},{10... | collective-permute-start | bytes 737288 | tf_op jit(solution)/shard_map/weight_qkv/ppermute | solution.py:339
  20.8 11.4 %collective-permute-start.5 = (bf16[160,768]{1,0:T(8,128)(2,1)S(1)}, bf16[160,768]{1,0:T(8,128)(2,1)S(1)}, u32[]{:S(2)}, u32[]{:S(2)}) collective-permute-start(bf16[160,768]{1,0:T(8,128)(2,1)S(1)} %pad_maximum_fusion.9), channel_id=1, source_target_pairs={{0,16},{16,0},{1,17},{17,1},{2,18},{18,2},{3,19},{19,3},{4,20},{20... | collective-permute-start | bytes 737288 | tf_op jit(solution)/shard_map/weight_qkv/ppermute | solution.py:339
  21.3 10.9 %collective-permute-start.4 = (bf16[160,768]{1,0:T(8,128)(2,1)S(1)}, bf16[160,768]{1,0:T(8,128)(2,1)S(1)}, u32[]{:S(2)}, u32[]{:S(2)}) collective-permute-start(bf16[160,768]{1,0:T(8,128)(2,1)S(1)} %pad_maximum_fusion.9), channel_id=1, source_target_pairs={{0,8},{8,0},{1,9},{9,1},{2,10},{10,2},{3,11},{11,3},{4,12},{12,4},... | collective-permute-start | bytes 737288 | tf_op jit(solution)/shard_map/weight_qkv/ppermute | solution.py:339
  24.2 11.1 %collective-permute-start.10 = (bf16[32,1024]{1,0:T(8,128)(2,1)S(1)}, bf16[32,1024]{1,0:T(8,128)(2,1)S(1)}, u32[]{:S(2)}, u32[]{:S(2)}) collective-permute-start(bf16[32,1024]{1,0:T(8,128)(2,1)S(1)} %get-tuple-element.189), channel_id=1, source_target_pairs={{0,2},{2,0},{1,3},{3,1},{4,6},{6,4},{5,7},{7,5},{8,10},{10,8},{9,1... | collective-permute-start | bytes 196616 | tf_op jit(solution)/shard_map/weight_out/ppermute | solution.py:339
  35.4 17.4 %collective-permute-start.13 = (bf16[128,1024]{1,0:T(8,128)(2,1)S(1)}, bf16[128,1024]{1,0:T(8,128)(2,1)}, u32[]{:S(2)}, u32[]{:S(2)}) collective-permute-start(bf16[128,1024]{1,0:T(8,128)(2,1)S(1)} %pad_maximum_fusion.4), channel_id=1, source_target_pairs={{0,4},{4,0},{1,5},{5,1},{2,6},{6,2},{3,7},{7,3},{8,12},{12,8},{9,1... | collective-permute-start | bytes 786440 | tf_op jit(solution)/shard_map/weight_up/ppermute | solution.py:339
  38.3 11.9 %collective-permute-start.12 = (bf16[128,1024]{1,0:T(8,128)(2,1)S(1)}, bf16[128,1024]{1,0:T(8,128)(2,1)S(1)}, u32[]{:S(2)}, u32[]{:S(2)}) collective-permute-start(bf16[128,1024]{1,0:T(8,128)(2,1)S(1)} %collective-permute-done.7.t2), channel_id=1, source_target_pairs={{0,2},{2,0},{1,3},{3,1},{4,6},{6,4},{5,7},{7,5},{8,10},{10,8},{9,1... | collective-permute-start | bytes 786440 | tf_op jit(solution)/shard_map/tokens/ppermute | solution.py:339
  50.1 8.9 %collective-permute-start.14 = (bf16[64,1024]{1,0:T(8,128)(2,1)S(1)}, bf16[64,1024]{1,0:T(8,128)(2,1)S(1)}, u32[]{:S(2)}, u32[]{:S(2)}) collective-permute-start(bf16[64,1024]{1,0:T(8,128)(2,1)S(1)} %pad_maximum_fusion.11), channel_id=1, source_target_pairs={{0,4},{4,0},{1,5},{5,1},{2,6},{6,2},{3,7},{7,3},{8,12},{12,8},{9,1... | collective-permute-start | bytes 393224 | tf_op jit(solution)/shard_map/weight_out/ppermute | solution.py:339
  59.1 12.6 %collective-permute-start.17 = (bf16[128,1024]{1,0:T(8,128)(2,1)S(1)}, bf16[128,1024]{1,0:T(8,128)(2,1)S(1)}, u32[]{:S(2)}, u32[]{:S(2)}) collective-permute-start(bf16[128,1024]{1,0:T(8,128)(2,1)S(1)} %get-tuple-element.358), channel_id=1, source_target_pairs={{0,8},{8,0},{1,9},{9,1},{2,10},{10,2},{3,11},{11,3},{4,12},{12,4},... | collective-permute-start | bytes 786440 | tf_op jit(solution)/shard_map/weight_out/ppermute | solution.py:339
  60.5 14.0 %collective-permute-start.19 = (bf16[128,1024]{1,0:T(8,128)(2,1)S(1)}, bf16[128,1024]{1,0:T(8,128)(2,1)S(1)}, u32[]{:S(2)}, u32[]{:S(2)}) collective-permute-start(bf16[128,1024]{1,0:T(8,128)(2,1)S(1)} %get-tuple-element.358), channel_id=1, source_target_pairs={{0,24},{8,16},{16,8},{24,0},{1,25},{9,17},{17,9},{25,1},{2,26},{10... | collective-permute-start | bytes 786440 | tf_op jit(solution)/shard_map/weight_out/ppermute | solution.py:339
  62.1 14.8 %collective-permute-start.18 = (bf16[128,1024]{1,0:T(8,128)(2,1)S(1)}, bf16[128,1024]{1,0:T(8,128)(2,1)S(1)}, u32[]{:S(2)}, u32[]{:S(2)}) collective-permute-start(bf16[128,1024]{1,0:T(8,128)(2,1)S(1)} %get-tuple-element.358), channel_id=1, source_target_pairs={{0,16},{16,0},{1,17},{17,1},{2,18},{18,2},{3,19},{19,3},{4,20},{20... | collective-permute-start | bytes 786440 | tf_op jit(solution)/shard_map/weight_out/ppermute | solution.py:339
  62.6 14.3 %collective-permute-start.16 = (bf16[128,1024]{1,0:T(8,128)(2,1)S(1)}, bf16[128,1024]{1,0:T(8,128)(2,1)S(1)}, u32[]{:S(2)}, u32[]{:S(2)}) collective-permute-start(bf16[128,1024]{1,0:T(8,128)(2,1)S(1)} %copy-done.20), channel_id=1, source_target_pairs={{0,4},{4,0},{1,5},{5,1},{2,6},{6,2},{3,7},{7,3},{8,12},{12,8},{9,1... | collective-permute-start | bytes 786440 | tf_op jit(solution)/shard_map/weight_down/ppermute | solution.py:339
  63.7 23.5 %collective-permute-start.23 = (bf16[256,1024]{1,0:T(8,128)(2,1)S(1)}, bf16[256,1024]{1,0:T(8,128)(2,1)S(1)}, u32[]{:S(2)}, u32[]{:S(2)}) collective-permute-start(bf16[256,1024]{1,0:T(8,128)(2,1)S(1)} %pad_maximum_fusion.1), channel_id=1, source_target_pairs={{0,16},{16,0},{1,17},{17,1},{2,18},{18,2},{3,19},{19,3},{4,20},{20... | collective-permute-start | bytes 1572872 | tf_op jit(solution)/shard_map/weight_up/ppermute | solution.py:339
  77.0 10.9 %collective-permute-start.24 = (bf16[512,1024]{1,0:T(8,128)(2,1)S(1)}, bf16[512,1024]{1,0:T(8,128)(2,1)S(1)}, u32[]{:S(2)}, u32[]{:S(2)}) collective-permute-start(bf16[512,1024]{1,0:T(8,128)(2,1)S(1)} %constant_dynamic-update-slice_fusion.3.near), channel_id=1, source_target_pairs={{0,1},{1,0},{2,3},{3,2},{4,5},{5,4},{6,7},{7,6},{8,9},{9,8},{10,11... | collective-permute-start | bytes 3145736 | tf_op jit(solution)/shard_map/weight_out/ppermute | solution.py:339
  77.2 8.0 %collective-permute-start.21 = (bf16[128,256]{1,0:T(8,128)(2,1)S(1)}, bf16[128,256]{1,0:T(8,128)(2,1)S(1)}, u32[]{:S(2)}, u32[]{:S(2)}) collective-permute-start(bf16[128,256]{1,0:T(8,128)(2,1)S(1)} %get-tuple-element.219), channel_id=1, source_target_pairs={{0,4},{4,0},{1,5},{5,1},{2,6},{6,2},{3,7},{7,3},{8,12},{12,8},{9,1... | collective-permute-start | bytes 196616 | tf_op jit(solution)/shard_map/attended/ppermute | solution.py:339
  87.2 14.5 %collective-permute-start.27 = (bf16[512,1024]{1,0:T(8,128)(2,1)S(1)}, bf16[512,1024]{1,0:T(8,128)(2,1)S(1)}, u32[]{:S(2)}, u32[]{:S(2)}) collective-permute-start(bf16[512,1024]{1,0:T(8,128)(2,1)S(1)} %constant_dynamic-update-slice_fusion.9.near), channel_id=1, source_target_pairs={{0,1},{1,0},{2,3},{3,2},{4,5},{5,4},{6,7},{7,6},{8,9},{9,8},{10,11... | collective-permute-start | bytes 3145736 | tf_op jit(solution)/shard_map/weight_up/ppermute | solution.py:339
  87.3 14.4 %collective-permute-start.28 = (bf16[256,1024]{1,0:T(8,128)(2,1)S(1)}, bf16[256,1024]{1,0:T(8,128)(2,1)S(1)}, u32[]{:S(2)}, u32[]{:S(2)}) collective-permute-start(bf16[256,1024]{1,0:T(8,128)(2,1)S(1)} %pad_maximum_fusion.2), channel_id=1, source_target_pairs={{0,16},{16,0},{1,17},{17,1},{2,18},{18,2},{3,19},{19,3},{4,20},{20... | collective-permute-start | bytes 1572872 | tf_op jit(solution)/shard_map/weight_down/ppermute | solution.py:339
  91.4 10.2 %collective-permute-start.26 = (bf16[128,1024]{1,0:T(8,128)(2,1)S(1)}, bf16[128,1024]{1,0:T(8,128)(2,1)S(1)}, u32[]{:S(2)}, u32[]{:S(2)}) collective-permute-start(bf16[128,1024]{1,0:T(8,128)(2,1)S(1)} %get-tuple-element.229.h0), channel_id=1, source_target_pairs={{0,8},{8,0},{1,9},{9,1},{2,10},{10,2},{3,11},{11,3},{4,12},{12,4},... | collective-permute-start | bytes 786440 | tf_op jit(solution)/shard_map/hidden/ppermute | solution.py:339
  92.8 8.9 %collective-permute-start.25 = (bf16[128,1024]{1,0:T(8,128)(2,1)S(1)}, bf16[128,1024]{1,0:T(8,128)(2,1)S(1)}, u32[]{:S(2)}, u32[]{:S(2)}) collective-permute-start(bf16[128,1024]{1,0:T(8,128)(2,1)S(1)} %get-tuple-element.229.h0), channel_id=1, source_target_pairs={{0,2},{2,0},{1,3},{3,1},{4,6},{6,4},{5,7},{7,5},{8,10},{10,8},{9,1... | collective-permute-start | bytes 786440 | tf_op jit(solution)/shard_map/hidden/ppermute | solution.py:339
  118.4 7.3 %collective-permute-start.35 = (bf16[128,1024]{1,0:T(8,128)(2,1)S(1)}, bf16[128,1024]{1,0:T(8,128)(2,1)S(1)}, u32[]{:S(2)}, u32[]{:S(2)}) collective-permute-start(bf16[128,1024]{1,0:T(8,128)(2,1)S(1)} %pad_maximum_fusion.6), channel_id=1, source_target_pairs={{0,8},{8,0},{1,9},{9,1},{2,10},{10,2},{3,11},{11,3},{4,12},{12,4},... | collective-permute-start | bytes 786440 | tf_op jit(solution)/shard_map/ppermute | solution.py:339
  128.9 7.7 %collective-permute-start.37 = (bf16[128,1024]{1,0:T(8,128)(2,1)S(1)}, bf16[128,1024]{1,0:T(8,128)(2,1)S(1)}, u32[]{:S(2)}, u32[]{:S(2)}) collective-permute-start(bf16[128,1024]{1,0:T(8,128)(2,1)S(1)} %get-tuple-element.249.g0), channel_id=1, source_target_pairs={{0,8},{8,0},{1,9},{9,1},{2,10},{10,2},{3,11},{11,3},{4,12},{12,4},... | collective-permute-start | bytes 786440 | tf_op jit(solution)/shard_map/grad_down/ppermute | solution.py:339
  129.2 7.8 %collective-permute-start.36 = (bf16[128,1024]{1,0:T(8,128)(2,1)S(1)}, bf16[128,1024]{1,0:T(8,128)(2,1)S(1)}, u32[]{:S(2)}, u32[]{:S(2)}) collective-permute-start(bf16[128,1024]{1,0:T(8,128)(2,1)S(1)} %get-tuple-element.249.g0), channel_id=1, source_target_pairs={{0,2},{2,0},{1,3},{3,1},{4,6},{6,4},{5,7},{7,5},{8,10},{10,8},{9,1... | collective-permute-start | bytes 786440 | tf_op jit(solution)/shard_map/grad_down/ppermute | solution.py:339
  151.8 7.9 %collective-permute-start.44 = (bf16[1024,1024]{1,0:T(8,128)(2,1)}, bf16[1024,1024]{1,0:T(8,128)(2,1)S(1)}, u32[]{:S(2)}, u32[]{:S(2)}) collective-permute-start(bf16[1024,1024]{1,0:T(8,128)(2,1)} %get-tuple-element.258), channel_id=1, source_target_pairs={{0,1},{1,0},{2,3},{3,2},{4,5},{5,4},{6,7},{7,6},{8,9},{9,8},{10,11... | collective-permute-start | bytes 6291464 | tf_op jit(solution)/shard_map/grad_weight_feed/ppermute | solution.py:339
  157.8 8.0 %collective-permute-start.43 = (bf16[128,1024]{1,0:T(8,128)(2,1)S(1)}, bf16[128,1024]{1,0:T(8,128)(2,1)S(1)}, u32[]{:S(2)}, u32[]{:S(2)}) collective-permute-start(bf16[128,1024]{1,0:T(8,128)(2,1)S(1)} %pad_maximum_fusion.8), channel_id=1, source_target_pairs={{0,8},{8,0},{1,9},{9,1},{2,10},{10,2},{3,11},{11,3},{4,12},{12,4},... | collective-permute-start | bytes 786440 | tf_op jit(solution)/shard_map/grad_hidden/ppermute | solution.py:339
  159.4 7.7 %collective-permute-start.41 = (bf16[128,1024]{1,0:T(8,128)(2,1)S(1)}, bf16[128,1024]{1,0:T(8,128)(2,1)S(1)}, u32[]{:S(2)}, u32[]{:S(2)}) collective-permute-start(bf16[128,1024]{1,0:T(8,128)(2,1)S(1)} %pad_maximum_fusion.7), channel_id=1, source_target_pairs={{0,2},{2,0},{1,3},{3,1},{4,6},{6,4},{5,7},{7,5},{8,10},{10,8},{9,1... | collective-permute-start | bytes 786440 | tf_op jit(solution)/shard_map/grad_hidden/ppermute | solution.py:339
  170.1 10.7 %collective-permute-start.45 = (bf16[512,1024]{1,0:T(8,128)(2,1)S(1)}, bf16[512,1024]{1,0:T(8,128)(2,1)S(1)}, u32[]{:S(2)}, u32[]{:S(2)}) collective-permute-start(bf16[512,1024]{1,0:T(8,128)(2,1)S(1)} %get-tuple-element.267), channel_id=1, source_target_pairs={{0,1},{1,0},{2,3},{3,2},{4,5},{5,4},{6,7},{7,6},{8,9},{9,8},{10,11... | collective-permute-start | bytes 3145736 | tf_op jit(solution)/shard_map/grad_weight_out/ppermute | solution.py:339
  170.3 25.6 %collective-permute-start.50 = (bf16[512,1024]{1,0:T(8,128)(2,1)S(1)}, bf16[512,1024]{1,0:T(8,128)(2,1)S(1)}, u32[]{:S(2)}, u32[]{:S(2)}) collective-permute-start(bf16[512,1024]{1,0:T(8,128)(2,1)S(1)} %slice.201), channel_id=1, source_target_pairs={{0,16},{16,0},{1,17},{17,1},{2,18},{18,2},{3,19},{19,3},{4,20},{20... | collective-permute-start | bytes 3145736 | tf_op jit(solution)/shard_map/grad_weight_feed/ppermute | solution.py:339
  172.6 8.3 %collective-permute-start.47 = (bf16[128,256]{1,0:T(8,128)(2,1)S(1)}, bf16[128,256]{1,0:T(8,128)(2,1)S(1)}, u32[]{:S(2)}, u32[]{:S(2)}) collective-permute-start(bf16[128,256]{1,0:T(8,128)(2,1)S(1)} %get-tuple-element.269), channel_id=1, source_target_pairs={{0,4},{4,0},{1,5},{5,1},{2,6},{6,2},{3,7},{7,3},{8,12},{12,8},{9,1... | collective-permute-start | bytes 196616 | tf_op jit(solution)/shard_map/grad_attended/ppermute | solution.py:339
  173.9 6.9 %collective-permute-start.48 = (bf16[128,256]{1,0:T(8,128)(2,1)S(1)}, bf16[128,256]{1,0:T(8,128)(2,1)S(1)}, u32[]{:S(2)}, u32[]{:S(2)}) collective-permute-start(bf16[128,256]{1,0:T(8,128)(2,1)S(1)} %get-tuple-element.270), channel_id=1, source_target_pairs={{0,6},{2,4},{4,2},{6,0},{1,7},{3,5},{5,3},{7,1},{8,14},{10,12},{12... | collective-permute-start | bytes 196616 | tf_op jit(solution)/shard_map/grad_attended/ppermute | solution.py:339
  181.3 15.1 %collective-permute-start.49 = (bf16[256,1024]{1,0:T(8,128)(2,1)S(1)}, bf16[256,1024]{1,0:T(8,128)(2,1)S(1)}, u32[]{:S(2)}, u32[]{:S(2)}) collective-permute-start(bf16[256,1024]{1,0:T(8,128)(2,1)S(1)} %slice.199), channel_id=1, source_target_pairs={{0,8},{8,0},{1,9},{9,1},{2,10},{10,2},{3,11},{11,3},{4,12},{12,4},... | collective-permute-start | bytes 1572872 | tf_op jit(solution)/shard_map/grad_weight_out/ppermute | solution.py:339
  196.7 8.8 %collective-permute-start.52 = (bf16[128,1024]{1,0:T(8,128)(2,1)S(1)}, bf16[128,1024]{1,0:T(8,128)(2,1)S(1)}, u32[]{:S(2)}, u32[]{:S(2)}) collective-permute-start(bf16[128,1024]{1,0:T(8,128)(2,1)S(1)} %slice.203), channel_id=1, source_target_pairs={{0,16},{16,0},{1,17},{17,1},{2,18},{18,2},{3,19},{19,3},{4,20},{20... | collective-permute-start | bytes 786440 | tf_op jit(solution)/shard_map/grad_weight_out/ppermute | solution.py:339
  197.3 15.0 %collective-permute-start.53 = (bf16[128,1024]{1,0:T(8,128)(2,1)S(1)}, bf16[128,1024]{1,0:T(8,128)(2,1)S(1)}, u32[]{:S(2)}, u32[]{:S(2)}) collective-permute-start(bf16[128,1024]{1,0:T(8,128)(2,1)S(1)} %get-tuple-element.344), channel_id=1, source_target_pairs={{0,4},{4,0},{1,5},{5,1},{2,6},{6,2},{3,7},{7,3},{8,12},{12,8},{9,1... | collective-permute-start | bytes 786440 | tf_op jit(solution)/shard_map/grad_weight_up/ppermute | solution.py:339
  212.5 11.7 %collective-permute-start.61 = (bf16[64,1024]{1,0:T(8,128)(2,1)S(1)}, bf16[64,1024]{1,0:T(8,128)(2,1)S(1)}, u32[]{:S(2)}, u32[]{:S(2)}) collective-permute-start(bf16[64,1024]{1,0:T(8,128)(2,1)S(1)} %slice.218), channel_id=1, source_target_pairs={{0,2},{2,0},{1,3},{3,1},{4,6},{6,4},{5,7},{7,5},{8,10},{10,8},{9,1... | collective-permute-start | bytes 393224 | tf_op jit(solution)/shard_map/grad_weight_out/ppermute | solution.py:339
  218.9 9.0 %collective-permute-start.56 = (bf16[160,768]{1,0:T(8,128)(2,1)S(1)}, bf16[160,768]{1,0:T(8,128)(2,1)S(1)}, u32[]{:S(2)}, u32[]{:S(2)}) collective-permute-start(bf16[160,768]{1,0:T(8,128)(2,1)S(1)} %get-tuple-element.345), channel_id=1, source_target_pairs={{0,8},{8,0},{1,9},{9,1},{2,10},{10,2},{3,11},{11,3},{4,12},{12,4},... | collective-permute-start | bytes 737288 | tf_op jit(solution)/shard_map/grad_weight_qkv/ppermute | solution.py:339
  220.3 12.5 %collective-permute-start.58 = (bf16[160,768]{1,0:T(8,128)(2,1)S(1)}, bf16[160,768]{1,0:T(8,128)(2,1)S(1)}, u32[]{:S(2)}, u32[]{:S(2)}) collective-permute-start(bf16[160,768]{1,0:T(8,128)(2,1)S(1)} %get-tuple-element.346), channel_id=1, source_target_pairs={{0,24},{8,16},{16,8},{24,0},{1,25},{9,17},{17,9},{25,1},{2,26},{10... | collective-permute-start | bytes 737288 | tf_op jit(solution)/shard_map/grad_weight_qkv/ppermute | solution.py:339
  221.9 12.3 %collective-permute-start.57 = (bf16[160,768]{1,0:T(8,128)(2,1)S(1)}, bf16[160,768]{1,0:T(8,128)(2,1)S(1)}, u32[]{:S(2)}, u32[]{:S(2)}) collective-permute-start(bf16[160,768]{1,0:T(8,128)(2,1)S(1)} %get-tuple-element.347), channel_id=1, source_target_pairs={{0,16},{16,0},{1,17},{17,1},{2,18},{18,2},{3,19},{19,3},{4,20},{20... | collective-permute-start | bytes 737288 | tf_op jit(solution)/shard_map/grad_weight_qkv/ppermute | solution.py:339
  222.5 11.7 %collective-permute-start.60 = (bf16[64,1024]{1,0:T(8,128)(2,1)S(1)}, bf16[64,1024]{1,0:T(8,128)(2,1)S(1)}, u32[]{:S(2)}, u32[]{:S(2)}) collective-permute-start(bf16[64,1024]{1,0:T(8,128)(2,1)S(1)} %pad_maximum_fusion.12), channel_id=1, source_target_pairs={{0,2},{2,0},{1,3},{3,1},{4,6},{6,4},{5,7},{7,5},{8,10},{10,8},{9,1... | collective-permute-start | bytes 393224 | tf_op jit(solution)/shard_map/grad_weight_up/ppermute | solution.py:339
  224.2 13.1 %collective-permute-start.59 = (bf16[128,1024]{1,0:T(8,128)(2,1)S(1)}, bf16[128,1024]{1,0:T(8,128)(2,1)S(1)}, u32[]{:S(2)}, u32[]{:S(2)}) collective-permute-start(bf16[128,1024]{1,0:T(8,128)(2,1)S(1)} %slice.214), channel_id=1, source_target_pairs={{0,4},{4,0},{1,5},{5,1},{2,6},{6,2},{3,7},{7,3},{8,12},{12,8},{9,1... | collective-permute-start | bytes 786440 | tf_op jit(solution)/shard_map/grad_weight_down/ppermute | solution.py:339
  237.5 7.7 %collective-permute-start.62 = (bf16[32,1024]{1,0:T(8,128)(2,1)S(1)}, bf16[32,1024]{1,0:T(8,128)(2,1)S(1)}, u32[]{:S(2)}, u32[]{:S(2)}) collective-permute-start(bf16[32,1024]{1,0:T(8,128)(2,1)S(1)} %slice.220), channel_id=1, source_target_pairs={{0,4},{4,0},{1,5},{5,1},{2,6},{6,2},{3,7},{7,3},{8,12},{12,8},{9,1... | collective-permute-start | bytes 196616 | tf_op jit(solution)/shard_map/grad_weight_out/ppermute | solution.py:339
  237.6 7.6 %collective-permute-start.63 = (bf16[40,768]{1,0:T(8,128)(2,1)S(1)}, bf16[40,768]{1,0:T(8,128)(2,1)S(1)}, u32[]{:S(2)}, u32[]{:S(2)}) collective-permute-start(bf16[40,768]{1,0:T(8,128)(2,1)S(1)} %get-tuple-element.353), channel_id=1, source_target_pairs={{0,2},{2,0},{1,3},{3,1},{4,6},{6,4},{5,7},{7,5},{8,10},{10,8},{9,1... | collective-permute-start | bytes 184328 | tf_op jit(solution)/shard_map/grad_weight_qkv/ppermute | solution.py:339
  240.8 6.9 %collective-permute-start.65 = (bf16[40,768]{1,0:T(8,128)(2,1)S(1)}, bf16[40,768]{1,0:T(8,128)(2,1)S(1)}, u32[]{:S(2)}, u32[]{:S(2)}) collective-permute-start(bf16[40,768]{1,0:T(8,128)(2,1)S(1)} %get-tuple-element.350), channel_id=1, source_target_pairs={{0,6},{2,4},{4,2},{6,0},{1,7},{3,5},{5,3},{7,1},{8,14},{10,12},{12... | collective-permute-start | bytes 184328 | tf_op jit(solution)/shard_map/grad_weight_qkv/ppermute | solution.py:339
  242.3 14.5 %collective-permute-start.70 = (bf16[128,1024]{1,0:T(8,128)(2,1)S(1)}, bf16[128,1024]{1,0:T(8,128)(2,1)S(1)}, u32[]{:S(2)}, u32[]{:S(2)}) collective-permute-start(bf16[128,1024]{1,0:T(8,128)(2,1)S(1)} %get-tuple-element.320), channel_id=1, source_target_pairs={{0,2},{2,0},{1,3},{3,1},{4,6},{6,4},{5,7},{7,5},{8,10},{10,8},{9,1... | collective-permute-start | bytes 786440 | tf_op jit(solution)/shard_map/grad_tokens/ppermute | solution.py:339
  256.9 16.4 %collective-permute-start.71 = (bf16[128,1024]{1,0:T(8,128)(2,1)}, bf16[128,1024]{1,0:T(8,128)(2,1)S(1)}, u32[]{:S(2)}, u32[]{:S(2)}) collective-permute-start(bf16[128,1024]{1,0:T(8,128)(2,1)} %get-tuple-element.323), channel_id=1, source_target_pairs={{0,2},{2,0},{1,3},{3,1},{4,6},{6,4},{5,7},{7,5},{8,10},{10,8},{9,1... | collective-permute-start | bytes 786440 | tf_op jit(solution)/shard_map/grad_tokens/ppermute | solution.py:339
  258.2 15.2 %collective-permute-start.72 = (bf16[128,1024]{1,0:T(8,128)(2,1)S(1)}, bf16[128,1024]{1,0:T(8,128)(2,1)S(1)}, u32[]{:S(2)}, u32[]{:S(2)}) collective-permute-start(bf16[128,1024]{1,0:T(8,128)(2,1)S(1)} %add_convert_fusion.5), channel_id=1, source_target_pairs={{0,4},{4,0},{1,5},{5,1},{2,6},{6,2},{3,7},{7,3},{8,12},{12,8},{9,1... | collective-permute-start | bytes 786440 | tf_op jit(solution)/shard_map/grad_tokens/ppermute | solution.py:339
  (83 other events, 962.2 us)

commit v2 on v1

--- a/solution.py
+++ b/solution.py
@@ -910,7 +910,7 @@
     columns = small_params.shape[1]
     part = width // 4
     units = weight_up.shape[1] // 4
-    pad = 8
+    pad = 16
     tall = own + pad
     iy, ix, ih, il, ic = (lax.axis_index(name) for name in AXES)
     bits = jnp.stack([iy, ix, ih, il, ic]).astype(jnp.int32)
@@ -1183,7 +1183,7 @@
         sums_one,
         sums_two,
         sums_up,
-        scratch=[pltpu.VMEM((width, 3 * part), LOW), pltpu.VMEM((8, 8, 3 * part), WIDE)],
+        scratch=[pltpu.VMEM((width, 3 * part), LOW), pltpu.VMEM((8, pad, 3 * part), WIDE)],
     )
     out_sum = add_first(out_sum, after(out_other, near)).astype(LOW)
     owned_up = add_first(up_sum, after(up_other, near)).astype(LOW)
@@ -1226,7 +1226,7 @@
 
     total, small_tile = call(
         squares_kernel,
-        [((8, 128), WIDE), ((8, 3 * part), WIDE)],
+        [((8, 128), WIDE), ((pad, 3 * part), WIDE)],
         bits,
         owned_down,
         owned_out,

time: 278 us -> 285 us (1.025)
  starting transfers between devices: 85 us -> 88.2 us
    ppermute x76, starting transfers between devices: 85 us -> 88.2 us  [swap(): return lax.ppermute(value, axes, [(i, i ^ last) for i in range(last + 1)])]
    unnamed x118 -> x122, local copies, waits for them, and re-layouts: 10.5 us -> 13.4 us
  transfers between devices with their start and end apart: 76 -> 76, of which waited for: 44 -> 44; matrix products, arithmetic and copies ran while one was open for 5% -> 6% of each run, Pallas kernels for 12% -> 11%
where the time goes in v2:
time: 285 us; the launch traced here: 281 us
  waiting for transfers between devices  112 us (39%)
  starting transfers between devices  88.2 us (31%)
  Pallas kernels  50.9 us (18%)
  local copies, waits for them, and re-layouts  21.7 us (8%)
  other arithmetic  6.56 us (2%)
    ppermute x76, waiting for transfers between devices, swap(): return lax.ppermute(value, axes, [(i, i ^ last) for i in range(last + 1)])  112 us
    ppermute x76, starting transfers between devices, swap(): return lax.ppermute(value, axes, [(i, i ^ last) for i in range(last + 1)])  88.2 us
    pallas_call x18, Pallas kernels, call(): pl.pallas_call(kernel, name=getattr(kernel, 'func', kernel).__name__, in_...  42.5 us
    unnamed x122, local copies, waits for them, and re-layouts  13.4 us
    pallas_call x1, Pallas kernels, on_square(): pl.pallas_call(functools.partial(update_kernel, plans), name='update_kern...  5.99 us
  transfers between devices with their start and end apart: 76, of which 44 were waited for; matrix products, arithmetic and copies ran while one was open for 6% of the time, Pallas kernels for 11%

profile of v2, /device:TPU:0, one launch (start us, length us, event | category | flops | bytes accessed | tf_op | source)
XLA Modules:
  0.0 281.5 jit_solution(15361226498305855893)
XLA Ops:
  0.7 3.1 %collective-permute-start.3 = (bf16[128,1024]{1,0:T(8,128)(2,1)}, bf16[128,1024]{1,0:T(8,128)(2,1)S(1)}, u32[]{:S(2)}, u32[]{:S(2)}) collective-permute-start(bf16[128,1024]{1,0:T(8,128)(2,1)} %bitcast.28), channel_id=1, source_target_pairs={{0,2},{2,0},{1,3},{3,1},{4,6},{6,4},{5,7},{7,5},{8,10},{10,8},{9,1... | collective-permute-start | bytes 786440 | tf_op jit(solution)/shard_map/tokens/ppermute | solution.py:339
  6.3 3.0 %collective-permute-start.1 = (bf16[48,768]{1,0:T(8,128)(2,1)S(1)}, bf16[48,768]{1,0:T(8,128)(2,1)S(1)}, u32[]{:S(2)}, u32[]{:S(2)}) collective-permute-start(bf16[48,768]{1,0:T(8,128)(2,1)S(1)} %get-tuple-element.182), channel_id=1, source_target_pairs={{0,4},{4,0},{1,5},{5,1},{2,6},{6,2},{3,7},{7,3},{8,12},{12,8},{9,1... | collective-permute-start | bytes 221192 | tf_op jit(solution)/shard_map/weight_qkv/ppermute | solution.py:339
  14.3 3.0 %collective-permute-done.2 = bf16[48,768]{1,0:T(8,128)(2,1)S(1)} collective-permute-done((bf16[48,768]{1,0:T(8,128)(2,1)S(1)}, bf16[48,768]{1,0:T(8,128)(2,1)S(1)}, u32[]{:S(2)}, u32[]{:S(2)}) %collective-permute-start.2) | collective-permute-done | bytes 73760 | tf_op jit(solution)/shard_map/weight_qkv/ppermute | solution.py:339
  18.9 3.5 %collective-permute-done.8 = bf16[64,1024]{1,0:T(8,128)(2,1)S(1)} collective-permute-done((bf16[64,1024]{1,0:T(8,128)(2,1)S(1)}, bf16[64,1024]{1,0:T(8,128)(2,1)S(1)}, u32[]{:S(2)}, u32[]{:S(2)}) %collective-permute-start.8) | collective-permute-done | bytes 131104 | tf_op jit(solution)/shard_map/weight_up/ppermute | solution.py:339
  24.5 2.4 collective-permute-start.6
  30.0 4.5 %collective-permute-done.6 = bf16[192,768]{1,0:T(8,128)(2,1)S(1)} collective-permute-done((bf16[192,768]{1,0:T(8,128)(2,1)S(1)}, bf16[192,768]{1,0:T(8,128)(2,1)S(1)}, u32[]{:S(2)}, u32[]{:S(2)}) %collective-permute-start.6) | collective-permute-done | bytes 294944 | tf_op jit(solution)/shard_map/weight_qkv/ppermute | solution.py:339
  34.5 3.0 %collective-permute-done.5 = bf16[192,768]{1,0:T(8,128)(2,1)S(1)} collective-permute-done((bf16[192,768]{1,0:T(8,128)(2,1)S(1)}, bf16[192,768]{1,0:T(8,128)(2,1)S(1)}, u32[]{:S(2)}, u32[]{:S(2)}) %collective-permute-start.5) | collective-permute-done | bytes 294944 | tf_op jit(solution)/shard_map/weight_qkv/ppermute | solution.py:339
  46.9 6.5 %collective-permute-done.12.t3 = bf16[128,1024]{1,0:T(8,128)(2,1)S(1)} collective-permute-done((bf16[128,1024]{1,0:T(8,128)(2,1)S(1)}, bf16[128,1024]{1,0:T(8,128)(2,1)S(1)}, u32[]{:S(2)}, u32[]{:S(2)}) %collective-permute-start.12) | collective-permute-done | bytes 262176 | tf_op jit(solution)/shard_map/tokens/ppermute | solution.py:339
  58.2 2.4 project_kernel.1
  64.4 2.2 collective-permute-start.16
  69.2 6.4 %forward_kernel.1 = (bf16[128,256]{1,0:T(8,128)(2,1)S(1)}, bf16[128,256]{1,0:T(8,128)(2,1)S(1)}, bf16[128,256]{1,0:T(8,128)(2,1)S(1)}, bf16[128,256]{1,0:T(8,128)(2,1)S(1)}, f32[4,512]{1,0:T(4,128)S(1)}) custom-call(s32[5]{0:T(128)S(1)} %stack.23.bits, bf16[512,256]{1,0:T(8,128)(2,1)S(1)} %get-tuple-element.205.q_ref, ...), custom_call_target="tpu_custom_call" | custom-call | flops 1 | bytes 1 | tf_op jit(solution)/shard_map/forward_kernel/pallas_call | solution.py:389
  76.2 2.4 collective-permute-done.18
  80.2 2.4 collective-permute-start.21
  85.7 3.2 %collective-permute-done.22.a3 = bf16[128,256]{1,0:T(8,128)(2,1)S(1)} collective-permute-done((bf16[128,256]{1,0:T(8,128)(2,1)S(1)}, bf16[128,256]{1,0:T(8,128)(2,1)S(1)}, u32[]{:S(2)}, u32[]{:S(2)}) %collective-permute-start.22) | collective-permute-done | bytes 65568 | tf_op jit(solution)/shard_map/attended/ppermute | solution.py:339
  94.6 1.7 collective-permute-start.25
  96.4 7.0 %collective-permute-done.28 = bf16[256,1024]{1,0:T(8,128)(2,1)S(1)} collective-permute-done((bf16[256,1024]{1,0:T(8,128)(2,1)S(1)}, bf16[256,1024]{1,0:T(8,128)(2,1)S(1)}, u32[]{:S(2)}, u32[]{:S(2)}) %collective-permute-start.28) | collective-permute-done | bytes 524320 | tf_op jit(solution)/shard_map/weight_down/ppermute | solution.py:339
  103.5 1.8 collective-permute-start.29
  111.0 2.5 feed_up_kernel.1
  114.5 1.8 feed_down_kernel.1
  118.2 3.1 %collective-permute-done.34 = bf16[64,1024]{1,0:T(8,128)(2,1)S(1)} collective-permute-done((bf16[64,1024]{1,0:T(8,128)(2,1)S(1)}, bf16[64,1024]{1,0:T(8,128)(2,1)S(1)}, u32[]{:S(2)}, u32[]{:S(2)}) %collective-permute-start.34) | collective-permute-done | bytes 131104 | tf_op jit(solution)/shard_map/ppermute | solution.py:339
  122.6 1.7 collective-permute-start.33
  124.3 3.7 %collective-permute-done.35.from_a = bf16[128,1024]{1,0:T(8,128)(2,1)S(1)} collective-permute-done((bf16[128,1024]{1,0:T(8,128)(2,1)S(1)}, bf16[128,1024]{1,0:T(8,128)(2,1)S(1)}, u32[]{:S(2)}, u32[]{:S(2)}) %collective-permute-start.35) | collective-permute-done | bytes 262176 | tf_op jit(solution)/shard_map/ppermute | solution.py:339
  133.1 4.1 %collective-permute-done.37.g2 = bf16[128,1024]{1,0:T(8,128)(2,1)S(1)} collective-permute-done((bf16[128,1024]{1,0:T(8,128)(2,1)S(1)}, bf16[128,1024]{1,0:T(8,128)(2,1)S(1)}, u32[]{:S(2)}, u32[]{:S(2)}) %collective-permute-start.37) | collective-permute-done | bytes 262176 | tf_op jit(solution)/shard_map/grad_down/ppermute | solution.py:339
  137.2 2.4 collective-permute-start.38
  140.5 2.1 collective-permute-done.38.g3
  142.6 2.1 collective-permute-done.39.g4
  144.7 4.7 %feed_back_kernel.1 = (bf16[512,1024]{1,0:T(8,128)(2,1)S(1)}, f32[8,1024]{1,0:T(8,128)S(1)}, f32[128,1024]{1,0:T(8,128)S(1)}, f32[128,1024]{1,0:T(8,128)S(1)}, f...) custom-call(s32[5]{0:T(128)S(1)} %stack.23.bits, ...), custom_call_target="tpu_custom_call" | custom-call | flops 1 | bytes 1 | tf_op jit(solution)/shard_map/feed_back_kernel/pallas_call | solution.py:389
  149.5 5.1 %feed_grad_kernel.1 = (bf16[1024,1024]{1,0:T(8,128)(2,1)}, bf16[1024,1024]{1,0:T(8,128)(2,1)}) custom-call(s32[5]{0:T(128)S(1)} %stack.23.bits, bf16[512,1024]{1,0:T(8,128)(2,1)S(1)} %get-tuple-element.240.act, bf16[128,1024]{1,0:T(8,128)(2,1)S(1)} %get-tuple-element.249.g0, bf16[128,1024]{1,0:T(8,128)(2,1)S(1)} %collective-permute-done.36.g1, ...), custom_call_target="tpu_custom_call" | custom-call | flops 1 | bytes 1 | tf_op jit(solution)/shard_map/feed_grad_kernel/pallas_call | solution.py:389
  157.1 3.4 %collective-permute-done.42 = bf16[64,1024]{1,0:T(8,128)(2,1)S(1)} collective-permute-done((bf16[64,1024]{1,0:T(8,128)(2,1)S(1)}, bf16[64,1024]{1,0:T(8,128)(2,1)S(1)}, u32[]{:S(2)}, u32[]{:S(2)}) %collective-permute-start.42) | collective-permute-done | bytes 131104 | tf_op jit(solution)/shard_map/grad_hidden/ppermute | solution.py:339
  164.1 4.4 %collective-permute-done.43.from_a = bf16[128,1024]{1,0:T(8,128)(2,1)S(1)} collective-permute-done((bf16[128,1024]{1,0:T(8,128)(2,1)S(1)}, bf16[128,1024]{1,0:T(8,128)(2,1)S(1)}, u32[]{:S(2)}, u32[]{:S(2)}) %collective-permute-start.43) | collective-permute-done | bytes 262176 | tf_op jit(solution)/shard_map/grad_hidden/ppermute | solution.py:339
  174.8 2.2 collective-permute-start.47
  179.1 4.1 %collective-permute-done.47.d2 = bf16[128,256]{1,0:T(8,128)(2,1)S(1)} collective-permute-done((bf16[128,256]{1,0:T(8,128)(2,1)S(1)}, bf16[128,256]{1,0:T(8,128)(2,1)S(1)}, u32[]{:S(2)}, u32[]{:S(2)}) %collective-permute-start.47) | collective-permute-done | bytes 65568 | tf_op jit(solution)/shard_map/grad_attended/ppermute | solution.py:339
  184.9 8.6 %backward_kernel.1 = (bf16[512,256]{1,0:T(8,128)(2,1)S(1)}, f32[512,512]{1,0:T(8,128)S(1)}, bf16[512,512]{1,0:T(8,128)(2,1)S(1)}, f32[8,256]{1,0:T(8,128)S(1)}) custom-call(s32[5]{0:T(128)S(1)} %stack.23.bits, bf16[512,256]{1,0:T(8,128)(2,1)S(1)} %copy-done.22, bf16[512,512]{1,0:T(8,128)(2,1)S(1)} %get-tuple-element.203.near, ...), custom_call_target="tpu_custom_call" | custom-call | flops 1 | bytes 1 | tf_op jit(solution)/shard_map/backward_kernel/pallas_call | solution.py:389
  193.5 4.7 %collective-permute-done.50 = bf16[512,1024]{1,0:T(8,128)(2,1)S(1)} collective-permute-done((bf16[512,1024]{1,0:T(8,128)(2,1)S(1)}, bf16[512,1024]{1,0:T(8,128)(2,1)S(1)}, u32[]{:S(2)}, u32[]{:S(2)}) %collective-permute-start.50) | collective-permute-done | bytes 1048608 | tf_op jit(solution)/shard_map/grad_weight_feed/ppermute | solution.py:339
  200.5 1.8 collective-permute-start.53
  202.4 1.8 qkv_grad_kernel.1
  204.3 3.4 %collective-permute-done.52 = bf16[128,1024]{1,0:T(8,128)(2,1)S(1)} collective-permute-done((bf16[128,1024]{1,0:T(8,128)(2,1)S(1)}, bf16[128,1024]{1,0:T(8,128)(2,1)S(1)}, u32[]{:S(2)}, u32[]{:S(2)}) %collective-permute-start.52) | collective-permute-done | bytes 262176 | tf_op jit(solution)/shard_map/grad_weight_out/ppermute | solution.py:339
  207.7 7.8 %collective-permute-done.53 = bf16[128,1024]{1,0:T(8,128)(2,1)S(1)} collective-permute-done((bf16[128,1024]{1,0:T(8,128)(2,1)S(1)}, bf16[128,1024]{1,0:T(8,128)(2,1)S(1)}, u32[]{:S(2)}, u32[]{:S(2)}) %collective-permute-start.53) | collective-permute-done | bytes 262176 | tf_op jit(solution)/shard_map/grad_weight_up/ppermute | solution.py:339
  216.4 5.3 %collective-permute-done.55 = bf16[64,1024]{1,0:T(8,128)(2,1)S(1)} collective-permute-done((bf16[64,1024]{1,0:T(8,128)(2,1)S(1)}, bf16[64,1024]{1,0:T(8,128)(2,1)S(1)}, u32[]{:S(2)}, u32[]{:S(2)}) %collective-permute-start.55) | collective-permute-done | bytes 131104 | tf_op jit(solution)/shard_map/grad_weight_up/ppermute | solution.py:339
  225.8 1.7 collective-permute-start.60
  230.4 1.8 collective-permute-done.56
  232.2 5.2 %collective-permute-done.58 = bf16[192,768]{1,0:T(8,128)(2,1)S(1)} collective-permute-done((bf16[192,768]{1,0:T(8,128)(2,1)S(1)}, bf16[192,768]{1,0:T(8,128)(2,1)S(1)}, u32[]{:S(2)}, u32[]{:S(2)}) %collective-permute-start.58) | collective-permute-done | bytes 294944 | tf_op jit(solution)/shard_map/grad_weight_qkv/ppermute | solution.py:339
  238.8 1.8 collective-permute-done.59
  241.4 2.5 collective-permute-start.63
  245.6 1.9 collective-permute-start.64
  248.5 6.2 %collective-permute-done.65.p3.refs_9_ = bf16[48,768]{1,0:T(8,128)(2,1)S(1)} collective-permute-done((bf16[48,768]{1,0:T(8,128)(2,1)S(1)}, bf16[48,768]{1,0:T(8,128)(2,1)S(1)}, u32[]{:S(2)}, u32[]{:S(2)}) %collective-permute-start.65) | collective-permute-done | bytes 73760 | tf_op jit(solution)/shard_map/grad_weight_qkv/ppermute | solution.py:339
  256.8 2.3 collective-permute-start.69
  272.9 6.0 %update_kernel.1 = (f32[128,1024]{1,0:T(8,128)}, f32[128,1024]{1,0:T(8,128)}, f32[128,1024]{1,0:T(8,128)}, f32[32,1024]{1,0:T(8,128)}, f32[32,1024]{1,0:T(8,128)...) custom-call(s32[5]{0:T(128)} %copy-done.49, ...), custom_call_target="tpu_custom_call" | custom-call | flops 1 | bytes 1 | tf_op jit(solution)/shard_map/update_kernel/pallas_call | solution.py:1270
  (330 shorter events, 110.2 us)
Async XLA Ops:
  0.7 16.7 %collective-permute-start.3 = (bf16[128,1024]{1,0:T(8,128)(2,1)}, bf16[128,1024]{1,0:T(8,128)(2,1)S(1)}, u32[]{:S(2)}, u32[]{:S(2)}) collective-permute-start(bf16[128,1024]{1,0:T(8,128)(2,1)} %bitcast.28), channel_id=1, source_target_pairs={{0,2},{2,0},{1,3},{3,1},{4,6},{6,4},{5,7},{7,5},{8,10},{10,8},{9,1... | collective-permute-start | bytes 786440 | tf_op jit(solution)/shard_map/tokens/ppermute | solution.py:339
  6.2 8.1 %collective-permute-start = (bf16[48,768]{1,0:T(8,128)(2,1)S(1)}, bf16[48,768]{1,0:T(8,128)(2,1)S(1)}, u32[]{:S(2)}, u32[]{:S(2)}) collective-permute-start(bf16[48,768]{1,0:T(8,128)(2,1)S(1)} %get-tuple-element.181), channel_id=1, source_target_pairs={{0,2},{2,0},{1,3},{3,1},{4,6},{6,4},{5,7},{7,5},{8,10},{10,8},{9,1... | collective-permute-start | bytes 221192 | tf_op jit(solution)/shard_map/weight_qkv/ppermute | solution.py:339
  6.3 8.0 %collective-permute-start.1 = (bf16[48,768]{1,0:T(8,128)(2,1)S(1)}, bf16[48,768]{1,0:T(8,128)(2,1)S(1)}, u32[]{:S(2)}, u32[]{:S(2)}) collective-permute-start(bf16[48,768]{1,0:T(8,128)(2,1)S(1)} %get-tuple-element.182), channel_id=1, source_target_pairs={{0,4},{4,0},{1,5},{5,1},{2,6},{6,2},{3,7},{7,3},{8,12},{12,8},{9,1... | collective-permute-start | bytes 221192 | tf_op jit(solution)/shard_map/weight_qkv/ppermute | solution.py:339
  9.3 8.0 %collective-permute-start.2 = (bf16[48,768]{1,0:T(8,128)(2,1)S(1)}, bf16[48,768]{1,0:T(8,128)(2,1)S(1)}, u32[]{:S(2)}, u32[]{:S(2)}) collective-permute-start(bf16[48,768]{1,0:T(8,128)(2,1)S(1)} %get-tuple-element.183), channel_id=1, source_target_pairs={{0,6},{2,4},{4,2},{6,0},{1,7},{3,5},{5,3},{7,1},{8,14},{10,12},{12... | collective-permute-start | bytes 221192 | tf_op jit(solution)/shard_map/weight_qkv/ppermute | solution.py:339
  23.1 14.6 %collective-permute-start.7 = (bf16[128,1024]{1,0:T(8,128)(2,1)S(1)}, bf16[128,1024]{1,0:T(8,128)(2,1)S(1)}, u32[]{:S(2)}, u32[]{:S(2)}) collective-permute-start(bf16[128,1024]{1,0:T(8,128)(2,1)S(1)} %bitcast.29), channel_id=1, source_target_pairs={{0,4},{4,0},{1,5},{5,1},{2,6},{6,2},{3,7},{7,3},{8,12},{12,8},{9,1... | collective-permute-start | bytes 786440 | tf_op jit(solution)/shard_map/tokens/ppermute | solution.py:339
  24.5 10.0 %collective-permute-start.6 = (bf16[192,768]{1,0:T(8,128)(2,1)S(1)}, bf16[192,768]{1,0:T(8,128)(2,1)S(1)}, u32[]{:S(2)}, u32[]{:S(2)}) collective-permute-start(bf16[192,768]{1,0:T(8,128)(2,1)S(1)} %pad_maximum_fusion.4), channel_id=1, source_target_pairs={{0,24},{8,16},{16,8},{24,0},{1,25},{9,17},{17,9},{25,1},{2,26},{10... | collective-permute-start | bytes 884744 | tf_op jit(solution)/shard_map/weight_qkv/ppermute | solution.py:339
  27.0 10.5 %collective-permute-start.5 = (bf16[192,768]{1,0:T(8,128)(2,1)S(1)}, bf16[192,768]{1,0:T(8,128)(2,1)S(1)}, u32[]{:S(2)}, u32[]{:S(2)}) collective-permute-start(bf16[192,768]{1,0:T(8,128)(2,1)S(1)} %pad_maximum_fusion.4), channel_id=1, source_target_pairs={{0,16},{16,0},{1,17},{17,1},{2,18},{18,2},{3,19},{19,3},{4,20},{20... | collective-permute-start | bytes 884744 | tf_op jit(solution)/shard_map/weight_qkv/ppermute | solution.py:339
  27.5 10.2 %collective-permute-start.4 = (bf16[192,768]{1,0:T(8,128)(2,1)S(1)}, bf16[192,768]{1,0:T(8,128)(2,1)S(1)}, u32[]{:S(2)}, u32[]{:S(2)}) collective-permute-start(bf16[192,768]{1,0:T(8,128)(2,1)S(1)} %pad_maximum_fusion.4), channel_id=1, source_target_pairs={{0,8},{8,0},{1,9},{9,1},{2,10},{10,2},{3,11},{11,3},{4,12},{12,4},... | collective-permute-start | bytes 884744 | tf_op jit(solution)/shard_map/weight_qkv/ppermute | solution.py:339
  28.3 9.4 %collective-permute-start.10 = (bf16[32,1024]{1,0:T(8,128)(2,1)S(1)}, bf16[32,1024]{1,0:T(8,128)(2,1)S(1)}, u32[]{:S(2)}, u32[]{:S(2)}) collective-permute-start(bf16[32,1024]{1,0:T(8,128)(2,1)S(1)} %get-tuple-element.189), channel_id=1, source_target_pairs={{0,2},{2,0},{1,3},{3,1},{4,6},{6,4},{5,7},{7,5},{8,10},{10,8},{9,1... | collective-permute-start | bytes 196616 | tf_op jit(solution)/shard_map/weight_out/ppermute | solution.py:339
  37.9 16.2 %collective-permute-start.13 = (bf16[128,1024]{1,0:T(8,128)(2,1)}, bf16[128,1024]{1,0:T(8,128)(2,1)}, u32[]{:S(2)}, u32[]{:S(2)}) collective-permute-start(bf16[128,1024]{1,0:T(8,128)(2,1)} %pad_maximum_fusion.5), channel_id=1, source_target_pairs={{0,4},{4,0},{1,5},{5,1},{2,6},{6,2},{3,7},{7,3},{8,12},{12,8},{9,1... | collective-permute-start | bytes 786440 | tf_op jit(solution)/shard_map/weight_up/ppermute | solution.py:339
  39.3 14.0 %collective-permute-start.12 = (bf16[128,1024]{1,0:T(8,128)(2,1)S(1)}, bf16[128,1024]{1,0:T(8,128)(2,1)S(1)}, u32[]{:S(2)}, u32[]{:S(2)}) collective-permute-start(bf16[128,1024]{1,0:T(8,128)(2,1)S(1)} %collective-permute-done.7.t2), channel_id=1, source_target_pairs={{0,2},{2,0},{1,3},{3,1},{4,6},{6,4},{5,7},{7,5},{8,10},{10,8},{9,1... | collective-permute-start | bytes 786440 | tf_op jit(solution)/shard_map/tokens/ppermute | solution.py:339
  53.4 7.4 %collective-permute-start.14 = (bf16[64,1024]{1,0:T(8,128)(2,1)S(1)}, bf16[64,1024]{1,0:T(8,128)(2,1)S(1)}, u32[]{:S(2)}, u32[]{:S(2)}) collective-permute-start(bf16[64,1024]{1,0:T(8,128)(2,1)S(1)} %pad_maximum_fusion.11), channel_id=1, source_target_pairs={{0,4},{4,0},{1,5},{5,1},{2,6},{6,2},{3,7},{7,3},{8,12},{12,8},{9,1... | collective-permute-start | bytes 393224 | tf_op jit(solution)/shard_map/weight_out/ppermute | solution.py:339
  60.9 14.8 %collective-permute-start.17 = (bf16[128,1024]{1,0:T(8,128)(2,1)S(1)}, bf16[128,1024]{1,0:T(8,128)(2,1)S(1)}, u32[]{:S(2)}, u32[]{:S(2)}) collective-permute-start(bf16[128,1024]{1,0:T(8,128)(2,1)S(1)} %get-tuple-element.358), channel_id=1, source_target_pairs={{0,8},{8,0},{1,9},{9,1},{2,10},{10,2},{3,11},{11,3},{4,12},{12,4},... | collective-permute-start | bytes 786440 | tf_op jit(solution)/shard_map/weight_out/ppermute | solution.py:339
  62.4 13.8 %collective-permute-start.19 = (bf16[128,1024]{1,0:T(8,128)(2,1)S(1)}, bf16[128,1024]{1,0:T(8,128)(2,1)S(1)}, u32[]{:S(2)}, u32[]{:S(2)}) collective-permute-start(bf16[128,1024]{1,0:T(8,128)(2,1)S(1)} %get-tuple-element.358), channel_id=1, source_target_pairs={{0,24},{8,16},{16,8},{24,0},{1,25},{9,17},{17,9},{25,1},{2,26},{10... | collective-permute-start | bytes 786440 | tf_op jit(solution)/shard_map/weight_out/ppermute | solution.py:339
  63.8 14.8 %collective-permute-start.18 = (bf16[128,1024]{1,0:T(8,128)(2,1)S(1)}, bf16[128,1024]{1,0:T(8,128)(2,1)S(1)}, u32[]{:S(2)}, u32[]{:S(2)}) collective-permute-start(bf16[128,1024]{1,0:T(8,128)(2,1)S(1)} %get-tuple-element.358), channel_id=1, source_target_pairs={{0,16},{16,0},{1,17},{17,1},{2,18},{18,2},{3,19},{19,3},{4,20},{20... | collective-permute-start | bytes 786440 | tf_op jit(solution)/shard_map/weight_out/ppermute | solution.py:339
  64.4 14.3 %collective-permute-start.16 = (bf16[128,1024]{1,0:T(8,128)(2,1)S(1)}, bf16[128,1024]{1,0:T(8,128)(2,1)S(1)}, u32[]{:S(2)}, u32[]{:S(2)}) collective-permute-start(bf16[128,1024]{1,0:T(8,128)(2,1)S(1)} %copy-done.24), channel_id=1, source_target_pairs={{0,4},{4,0},{1,5},{5,1},{2,6},{6,2},{3,7},{7,3},{8,12},{12,8},{9,1... | collective-permute-start | bytes 786440 | tf_op jit(solution)/shard_map/weight_down/ppermute | solution.py:339
  67.7 21.1 %collective-permute-start.23 = (bf16[256,1024]{1,0:T(8,128)(2,1)S(1)}, bf16[256,1024]{1,0:T(8,128)(2,1)S(1)}, u32[]{:S(2)}, u32[]{:S(2)}) collective-permute-start(bf16[256,1024]{1,0:T(8,128)(2,1)S(1)} %pad_maximum_fusion.1), channel_id=1, source_target_pairs={{0,16},{16,0},{1,17},{17,1},{2,18},{18,2},{3,19},{19,3},{4,20},{20... | collective-permute-start | bytes 1572872 | tf_op jit(solution)/shard_map/weight_up/ppermute | solution.py:339
  78.7 11.7 %collective-permute-start.24 = (bf16[512,1024]{1,0:T(8,128)(2,1)S(1)}, bf16[512,1024]{1,0:T(8,128)(2,1)S(1)}, u32[]{:S(2)}, u32[]{:S(2)}) collective-permute-start(bf16[512,1024]{1,0:T(8,128)(2,1)S(1)} %constant_dynamic-update-slice_fusion.3.near), channel_id=1, source_target_pairs={{0,1},{1,0},{2,3},{3,2},{4,5},{5,4},{6,7},{7,6},{8,9},{9,8},{10,11... | collective-permute-start | bytes 3145736 | tf_op jit(solution)/shard_map/weight_out/ppermute | solution.py:339
  88.9 14.5 %collective-permute-start.27 = (bf16[512,1024]{1,0:T(8,128)(2,1)S(1)}, bf16[512,1024]{1,0:T(8,128)(2,1)S(1)}, u32[]{:S(2)}, u32[]{:S(2)}) collective-permute-start(bf16[512,1024]{1,0:T(8,128)(2,1)S(1)} %constant_dynamic-update-slice_fusion.9.near), channel_id=1, source_target_pairs={{0,1},{1,0},{2,3},{3,2},{4,5},{5,4},{6,7},{7,6},{8,9},{9,8},{10,11... | collective-permute-start | bytes 3145736 | tf_op jit(solution)/shard_map/weight_up/ppermute | solution.py:339
  89.0 14.4 %collective-permute-start.28 = (bf16[256,1024]{1,0:T(8,128)(2,1)S(1)}, bf16[256,1024]{1,0:T(8,128)(2,1)S(1)}, u32[]{:S(2)}, u32[]{:S(2)}) collective-permute-start(bf16[256,1024]{1,0:T(8,128)(2,1)S(1)} %pad_maximum_fusion.2), channel_id=1, source_target_pairs={{0,16},{16,0},{1,17},{17,1},{2,18},{18,2},{3,19},{19,3},{4,20},{20... | collective-permute-start | bytes 1572872 | tf_op jit(solution)/shard_map/weight_down/ppermute | solution.py:339
  93.8 9.6 %collective-permute-start.26 = (bf16[128,1024]{1,0:T(8,128)(2,1)S(1)}, bf16[128,1024]{1,0:T(8,128)(2,1)S(1)}, u32[]{:S(2)}, u32[]{:S(2)}) collective-permute-start(bf16[128,1024]{1,0:T(8,128)(2,1)S(1)} %get-tuple-element.229.h0), channel_id=1, source_target_pairs={{0,8},{8,0},{1,9},{9,1},{2,10},{10,2},{3,11},{11,3},{4,12},{12,4},... | collective-permute-start | bytes 786440 | tf_op jit(solution)/shard_map/hidden/ppermute | solution.py:339
  94.6 8.8 %collective-permute-start.25 = (bf16[128,1024]{1,0:T(8,128)(2,1)S(1)}, bf16[128,1024]{1,0:T(8,128)(2,1)S(1)}, u32[]{:S(2)}, u32[]{:S(2)}) collective-permute-start(bf16[128,1024]{1,0:T(8,128)(2,1)S(1)} %get-tuple-element.229.h0), channel_id=1, source_target_pairs={{0,2},{2,0},{1,3},{3,1},{4,6},{6,4},{5,7},{7,5},{8,10},{10,8},{9,1... | collective-permute-start | bytes 786440 | tf_op jit(solution)/shard_map/hidden/ppermute | solution.py:339
  121.4 6.5 %collective-permute-start.35 = (bf16[128,1024]{1,0:T(8,128)(2,1)S(1)}, bf16[128,1024]{1,0:T(8,128)(2,1)S(1)}, u32[]{:S(2)}, u32[]{:S(2)}) collective-permute-start(bf16[128,1024]{1,0:T(8,128)(2,1)S(1)} %pad_maximum_fusion.7), channel_id=1, source_target_pairs={{0,8},{8,0},{1,9},{9,1},{2,10},{10,2},{3,11},{11,3},{4,12},{12,4},... | collective-permute-start | bytes 786440 | tf_op jit(solution)/shard_map/ppermute | solution.py:339
  122.6 6.4 %collective-permute-start.33 = (bf16[128,1024]{1,0:T(8,128)(2,1)S(1)}, bf16[128,1024]{1,0:T(8,128)(2,1)S(1)}, u32[]{:S(2)}, u32[]{:S(2)}) collective-permute-start(bf16[128,1024]{1,0:T(8,128)(2,1)S(1)} %pad_maximum_fusion.6), channel_id=1, source_target_pairs={{0,2},{2,0},{1,3},{3,1},{4,6},{6,4},{5,7},{7,5},{8,10},{10,8},{9,1... | collective-permute-start | bytes 786440 | tf_op jit(solution)/shard_map/ppermute | solution.py:339
  130.6 6.6 %collective-permute-start.37 = (bf16[128,1024]{1,0:T(8,128)(2,1)S(1)}, bf16[128,1024]{1,0:T(8,128)(2,1)S(1)}, u32[]{:S(2)}, u32[]{:S(2)}) collective-permute-start(bf16[128,1024]{1,0:T(8,128)(2,1)S(1)} %get-tuple-element.249.g0), channel_id=1, source_target_pairs={{0,8},{8,0},{1,9},{9,1},{2,10},{10,2},{3,11},{11,3},{4,12},{12,4},... | collective-permute-start | bytes 786440 | tf_op jit(solution)/shard_map/grad_down/ppermute | solution.py:339
  131.7 8.0 %collective-permute-start.36 = (bf16[128,1024]{1,0:T(8,128)(2,1)S(1)}, bf16[128,1024]{1,0:T(8,128)(2,1)S(1)}, u32[]{:S(2)}, u32[]{:S(2)}) collective-permute-start(bf16[128,1024]{1,0:T(8,128)(2,1)S(1)} %get-tuple-element.249.g0), channel_id=1, source_target_pairs={{0,2},{2,0},{1,3},{3,1},{4,6},{6,4},{5,7},{7,5},{8,10},{10,8},{9,1... | collective-permute-start | bytes 786440 | tf_op jit(solution)/shard_map/grad_down/ppermute | solution.py:339
  154.5 8.6 %collective-permute-start.44 = (bf16[1024,1024]{1,0:T(8,128)(2,1)}, bf16[1024,1024]{1,0:T(8,128)(2,1)S(1)}, u32[]{:S(2)}, u32[]{:S(2)}) collective-permute-start(bf16[1024,1024]{1,0:T(8,128)(2,1)} %get-tuple-element.258), channel_id=1, source_target_pairs={{0,1},{1,0},{2,3},{3,2},{4,5},{5,4},{6,7},{7,6},{8,9},{9,8},{10,11... | collective-permute-start | bytes 6291464 | tf_op jit(solution)/shard_map/grad_weight_feed/ppermute | solution.py:339
  160.5 8.0 %collective-permute-start.43 = (bf16[128,1024]{1,0:T(8,128)(2,1)S(1)}, bf16[128,1024]{1,0:T(8,128)(2,1)S(1)}, u32[]{:S(2)}, u32[]{:S(2)}) collective-permute-start(bf16[128,1024]{1,0:T(8,128)(2,1)S(1)} %pad_maximum_fusion.9), channel_id=1, source_target_pairs={{0,8},{8,0},{1,9},{9,1},{2,10},{10,2},{3,11},{11,3},{4,12},{12,4},... | collective-permute-start | bytes 786440 | tf_op jit(solution)/shard_map/grad_hidden/ppermute | solution.py:339
  161.6 7.7 %collective-permute-start.41 = (bf16[128,1024]{1,0:T(8,128)(2,1)S(1)}, bf16[128,1024]{1,0:T(8,128)(2,1)S(1)}, u32[]{:S(2)}, u32[]{:S(2)}) collective-permute-start(bf16[128,1024]{1,0:T(8,128)(2,1)S(1)} %pad_maximum_fusion.8), channel_id=1, source_target_pairs={{0,2},{2,0},{1,3},{3,1},{4,6},{6,4},{5,7},{7,5},{8,10},{10,8},{9,1... | collective-permute-start | bytes 786440 | tf_op jit(solution)/shard_map/grad_hidden/ppermute | solution.py:339
  172.4 10.8 %collective-permute-start.45 = (bf16[512,1024]{1,0:T(8,128)(2,1)S(1)}, bf16[512,1024]{1,0:T(8,128)(2,1)S(1)}, u32[]{:S(2)}, u32[]{:S(2)}) collective-permute-start(bf16[512,1024]{1,0:T(8,128)(2,1)S(1)} %get-tuple-element.267), channel_id=1, source_target_pairs={{0,1},{1,0},{2,3},{3,2},{4,5},{5,4},{6,7},{7,6},{8,9},{9,8},{10,11... | collective-permute-start | bytes 3145736 | tf_op jit(solution)/shard_map/grad_weight_out/ppermute | solution.py:339
  172.5 25.6 %collective-permute-start.50 = (bf16[512,1024]{1,0:T(8,128)(2,1)S(1)}, bf16[512,1024]{1,0:T(8,128)(2,1)S(1)}, u32[]{:S(2)}, u32[]{:S(2)}) collective-permute-start(bf16[512,1024]{1,0:T(8,128)(2,1)S(1)} %slice.201), channel_id=1, source_target_pairs={{0,16},{16,0},{1,17},{17,1},{2,18},{18,2},{3,19},{19,3},{4,20},{20... | collective-permute-start | bytes 3145736 | tf_op jit(solution)/shard_map/grad_weight_feed/ppermute | solution.py:339
  174.8 8.4 %collective-permute-start.47 = (bf16[128,256]{1,0:T(8,128)(2,1)S(1)}, bf16[128,256]{1,0:T(8,128)(2,1)S(1)}, u32[]{:S(2)}, u32[]{:S(2)}) collective-permute-start(bf16[128,256]{1,0:T(8,128)(2,1)S(1)} %get-tuple-element.269), channel_id=1, source_target_pairs={{0,4},{4,0},{1,5},{5,1},{2,6},{6,2},{3,7},{7,3},{8,12},{12,8},{9,1... | collective-permute-start | bytes 196616 | tf_op jit(solution)/shard_map/grad_attended/ppermute | solution.py:339
  183.6 14.9 %collective-permute-start.49 = (bf16[256,1024]{1,0:T(8,128)(2,1)S(1)}, bf16[256,1024]{1,0:T(8,128)(2,1)S(1)}, u32[]{:S(2)}, u32[]{:S(2)}) collective-permute-start(bf16[256,1024]{1,0:T(8,128)(2,1)S(1)} %slice.199), channel_id=1, source_target_pairs={{0,8},{8,0},{1,9},{9,1},{2,10},{10,2},{3,11},{11,3},{4,12},{12,4},... | collective-permute-start | bytes 1572872 | tf_op jit(solution)/shard_map/grad_weight_out/ppermute | solution.py:339
  198.9 8.8 %collective-permute-start.52 = (bf16[128,1024]{1,0:T(8,128)(2,1)S(1)}, bf16[128,1024]{1,0:T(8,128)(2,1)S(1)}, u32[]{:S(2)}, u32[]{:S(2)}) collective-permute-start(bf16[128,1024]{1,0:T(8,128)(2,1)S(1)} %slice.203), channel_id=1, source_target_pairs={{0,16},{16,0},{1,17},{17,1},{2,18},{18,2},{3,19},{19,3},{4,20},{20... | collective-permute-start | bytes 786440 | tf_op jit(solution)/shard_map/grad_weight_out/ppermute | solution.py:339
  200.5 15.0 %collective-permute-start.53 = (bf16[128,1024]{1,0:T(8,128)(2,1)S(1)}, bf16[128,1024]{1,0:T(8,128)(2,1)S(1)}, u32[]{:S(2)}, u32[]{:S(2)}) collective-permute-start(bf16[128,1024]{1,0:T(8,128)(2,1)S(1)} %get-tuple-element.347), channel_id=1, source_target_pairs={{0,4},{4,0},{1,5},{5,1},{2,6},{6,2},{3,7},{7,3},{8,12},{12,8},{9,1... | collective-permute-start | bytes 786440 | tf_op jit(solution)/shard_map/grad_weight_up/ppermute | solution.py:339
  215.7 11.8 %collective-permute-start.61 = (bf16[64,1024]{1,0:T(8,128)(2,1)S(1)}, bf16[64,1024]{1,0:T(8,128)(2,1)S(1)}, u32[]{:S(2)}, u32[]{:S(2)}) collective-permute-start(bf16[64,1024]{1,0:T(8,128)(2,1)S(1)} %slice.218), channel_id=1, source_target_pairs={{0,2},{2,0},{1,3},{3,1},{4,6},{6,4},{5,7},{7,5},{8,10},{10,8},{9,1... | collective-permute-start | bytes 393224 | tf_op jit(solution)/shard_map/grad_weight_out/ppermute | solution.py:339
  222.2 10.0 %collective-permute-start.56 = (bf16[192,768]{1,0:T(8,128)(2,1)S(1)}, bf16[192,768]{1,0:T(8,128)(2,1)S(1)}, u32[]{:S(2)}, u32[]{:S(2)}) collective-permute-start(bf16[192,768]{1,0:T(8,128)(2,1)S(1)} %get-tuple-element.342), channel_id=1, source_target_pairs={{0,8},{8,0},{1,9},{9,1},{2,10},{10,2},{3,11},{11,3},{4,12},{12,4},... | collective-permute-start | bytes 884744 | tf_op jit(solution)/shard_map/grad_weight_qkv/ppermute | solution.py:339
  222.8 14.6 %collective-permute-start.58 = (bf16[192,768]{1,0:T(8,128)(2,1)S(1)}, bf16[192,768]{1,0:T(8,128)(2,1)S(1)}, u32[]{:S(2)}, u32[]{:S(2)}) collective-permute-start(bf16[192,768]{1,0:T(8,128)(2,1)S(1)} %get-tuple-element.343), channel_id=1, source_target_pairs={{0,24},{8,16},{16,8},{24,0},{1,25},{9,17},{17,9},{25,1},{2,26},{10... | collective-permute-start | bytes 884744 | tf_op jit(solution)/shard_map/grad_weight_qkv/ppermute | solution.py:339
  224.3 14.4 %collective-permute-start.57 = (bf16[192,768]{1,0:T(8,128)(2,1)S(1)}, bf16[192,768]{1,0:T(8,128)(2,1)S(1)}, u32[]{:S(2)}, u32[]{:S(2)}) collective-permute-start(bf16[192,768]{1,0:T(8,128)(2,1)S(1)} %get-tuple-element.344), channel_id=1, source_target_pairs={{0,16},{16,0},{1,17},{17,1},{2,18},{18,2},{3,19},{19,3},{4,20},{20... | collective-permute-start | bytes 884744 | tf_op jit(solution)/shard_map/grad_weight_qkv/ppermute | solution.py:339
  225.8 12.9 %collective-permute-start.60 = (bf16[64,1024]{1,0:T(8,128)(2,1)S(1)}, bf16[64,1024]{1,0:T(8,128)(2,1)S(1)}, u32[]{:S(2)}, u32[]{:S(2)}) collective-permute-start(bf16[64,1024]{1,0:T(8,128)(2,1)S(1)} %pad_maximum_fusion.12), channel_id=1, source_target_pairs={{0,2},{2,0},{1,3},{3,1},{4,6},{6,4},{5,7},{7,5},{8,10},{10,8},{9,1... | collective-permute-start | bytes 393224 | tf_op jit(solution)/shard_map/grad_weight_up/ppermute | solution.py:339
  227.5 13.1 %collective-permute-start.59 = (bf16[128,1024]{1,0:T(8,128)(2,1)S(1)}, bf16[128,1024]{1,0:T(8,128)(2,1)S(1)}, u32[]{:S(2)}, u32[]{:S(2)}) collective-permute-start(bf16[128,1024]{1,0:T(8,128)(2,1)S(1)} %slice.214), channel_id=1, source_target_pairs={{0,4},{4,0},{1,5},{5,1},{2,6},{6,2},{3,7},{7,3},{8,12},{12,8},{9,1... | collective-permute-start | bytes 786440 | tf_op jit(solution)/shard_map/grad_weight_down/ppermute | solution.py:339
  240.9 6.7 %collective-permute-start.62 = (bf16[32,1024]{1,0:T(8,128)(2,1)S(1)}, bf16[32,1024]{1,0:T(8,128)(2,1)S(1)}, u32[]{:S(2)}, u32[]{:S(2)}) collective-permute-start(bf16[32,1024]{1,0:T(8,128)(2,1)S(1)} %slice.220), channel_id=1, source_target_pairs={{0,4},{4,0},{1,5},{5,1},{2,6},{6,2},{3,7},{7,3},{8,12},{12,8},{9,1... | collective-permute-start | bytes 196616 | tf_op jit(solution)/shard_map/grad_weight_out/ppermute | solution.py:339
  241.4 7.1 %collective-permute-start.63 = (bf16[48,768]{1,0:T(8,128)(2,1)S(1)}, bf16[48,768]{1,0:T(8,128)(2,1)S(1)}, u32[]{:S(2)}, u32[]{:S(2)}) collective-permute-start(bf16[48,768]{1,0:T(8,128)(2,1)S(1)} %get-tuple-element.351), channel_id=1, source_target_pairs={{0,2},{2,0},{1,3},{3,1},{4,6},{6,4},{5,7},{7,5},{8,10},{10,8},{9,1... | collective-permute-start | bytes 221192 | tf_op jit(solution)/shard_map/grad_weight_qkv/ppermute | solution.py:339
  244.0 19.6 %collective-permute-start.70 = (bf16[128,1024]{1,0:T(8,128)(2,1)S(1)}, bf16[128,1024]{1,0:T(8,128)(2,1)S(1)}, u32[]{:S(2)}, u32[]{:S(2)}) collective-permute-start(bf16[128,1024]{1,0:T(8,128)(2,1)S(1)} %get-tuple-element.320), channel_id=1, source_target_pairs={{0,2},{2,0},{1,3},{3,1},{4,6},{6,4},{5,7},{7,5},{8,10},{10,8},{9,1... | collective-permute-start | bytes 786440 | tf_op jit(solution)/shard_map/grad_tokens/ppermute | solution.py:339
  244.0 10.7 %collective-permute-start.65 = (bf16[48,768]{1,0:T(8,128)(2,1)S(1)}, bf16[48,768]{1,0:T(8,128)(2,1)S(1)}, u32[]{:S(2)}, u32[]{:S(2)}) collective-permute-start(bf16[48,768]{1,0:T(8,128)(2,1)S(1)} %get-tuple-element.348), channel_id=1, source_target_pairs={{0,6},{2,4},{4,2},{6,0},{1,7},{3,5},{5,3},{7,1},{8,14},{10,12},{12... | collective-permute-start | bytes 221192 | tf_op jit(solution)/shard_map/grad_weight_qkv/ppermute | solution.py:339
  245.6 9.2 %collective-permute-start.64 = (bf16[48,768]{1,0:T(8,128)(2,1)S(1)}, bf16[48,768]{1,0:T(8,128)(2,1)S(1)}, u32[]{:S(2)}, u32[]{:S(2)}) collective-permute-start(bf16[48,768]{1,0:T(8,128)(2,1)S(1)} %get-tuple-element.349), channel_id=1, source_target_pairs={{0,4},{4,0},{1,5},{5,1},{2,6},{6,2},{3,7},{7,3},{8,12},{12,8},{9,1... | collective-permute-start | bytes 221192 | tf_op jit(solution)/shard_map/grad_weight_qkv/ppermute | solution.py:339
  263.7 16.4 %collective-permute-start.71 = (bf16[128,1024]{1,0:T(8,128)(2,1)S(1)}, bf16[128,1024]{1,0:T(8,128)(2,1)S(1)}, u32[]{:S(2)}, u32[]{:S(2)}) collective-permute-start(bf16[128,1024]{1,0:T(8,128)(2,1)S(1)} %get-tuple-element.323), channel_id=1, source_target_pairs={{0,2},{2,0},{1,3},{3,1},{4,6},{6,4},{5,7},{7,5},{8,10},{10,8},{9,1... | collective-permute-start | bytes 786440 | tf_op jit(solution)/shard_map/grad_tokens/ppermute | solution.py:339
  265.0 15.2 %collective-permute-start.72 = (bf16[128,1024]{1,0:T(8,128)(2,1)S(1)}, bf16[128,1024]{1,0:T(8,128)(2,1)S(1)}, u32[]{:S(2)}, u32[]{:S(2)}) collective-permute-start(bf16[128,1024]{1,0:T(8,128)(2,1)S(1)} %add_convert_fusion.6), channel_id=1, source_target_pairs={{0,4},{4,0},{1,5},{5,1},{2,6},{6,2},{3,7},{7,3},{8,12},{12,8},{9,1... | collective-permute-start | bytes 786440 | tf_op jit(solution)/shard_map/grad_tokens/ppermute | solution.py:339
  (85 other events, 953.6 us)
